TPU v7x, 32 devices: a whole 2x2x4 slice. The times are simulated.
32 devices in a mesh: dp: 8 (over z, y), mp: 4 (over x, core).
Axes of the slice: x: 2, y: 2, z: 4, core: 2. Of those that a mesh axis runs over, the one named last changes fastest.
Arguments:
- tokens: bfloat16 [32768, 1024], P(('dp', 'mp')), may hold values from -6 to 6
- out_grad: bfloat16 [32768, 1024], P(('dp', 'mp')), may hold values from -6 to 6
- item_counts: int32 [8], P('dp'), may hold values from 1 to 2, as said below
- group_dataset: int32 [8], P('dp'), may hold values from 0 to 5
- variable_mask: int32 [6, 48], replicated, may hold values from 0 to 1, as said below
- first_gain: float32 [1024], replicated, may hold values from 0.5 to 1.5
- first_shift: float32 [1024], replicated, may hold values from -1.75 to 1.75
- input_weight: bfloat16 [3, 1024, 1024], P(None, None, 'mp'), may hold values from -0.1875 to 0.1875
- input_bias: float32 [2, 1024], P(None, 'mp'), may hold values from -3 to 3
- output_weight: bfloat16 [1024, 1024], P('mp'), may hold values from -2 to 2
- output_bias: float32 [1024], replicated, may hold values from -3 to 3
- second_gain: float32 [1024], replicated, may hold values from 0.5 to 1.5
- second_shift: float32 [1024], replicated, may hold values from -1.75 to 1.75
- up_weight: bfloat16 [1024, 4096], P(None, 'mp'), may hold values from -0.1875 to 0.1875
- up_bias: float32 [4096], P('mp'), may hold values from -3 to 3
- down_weight: bfloat16 [4096, 1024], P('mp'), may hold values from -0.09375 to 0.09375
- down_bias: float32 [1024], replicated, may hold values from -3 to 3
Outputs:
- result: bfloat16 [32768, 1024], P(('dp', 'mp'))
- token_grad: bfloat16 [32768, 1024], P(('dp', 'mp'))
- first_gain_grad: float32 [1024], replicated
- first_shift_grad: float32 [1024], replicated
- input_weight_grad: float32 [3, 1024, 1024], P(None, None, 'mp')
- input_bias_grad: float32 [2, 1024], P(None, 'mp')
- output_weight_grad: float32 [1024, 1024], P('mp')
- output_bias_grad: float32 [1024], replicated
- second_gain_grad: float32 [1024], replicated
- second_shift_grad: float32 [1024], replicated
- up_weight_grad: float32 [1024, 4096], P(None, 'mp')
- up_bias_grad: float32 [4096], P('mp')
- down_weight_grad: float32 [4096, 1024], P('mp')
- down_bias_grad: float32 [1024], replicated
Inputs may be any that keep to these rules, and one draw needn't show every extreme that they name: `item_counts`: every draw has some group with exactly 2 items in use. `variable_mask`: each row is a run of ones then zeros, with 30 to 48 ones; some row has 48 ones and some row 30.
All inputs are finite; a program needn't handle non-finite values.
Results may differ from a plain program's by a relative error of at most 0.012.
The roundings to bfloat16 on the way count: a program that leaves them out, or rounds other values in their place, can miss the bound.
Values may be sent and summed in bfloat16 or wider, within the bound.
No kernel may reach another device: no remote copies, remote signals or barrier semaphores. Data moves between devices by JAX's collectives and lax.ppermute only.
A program may use at most 256 MiB of HBM per device.

v0:
```python
import jax
import jax.numpy as jnp
from jax import lax
from jax.sharding import PartitionSpec as P

HEAD_DIM = 64
SEQ = 2048


norm_eps = 1e-06


def layer_norm(values, gain_vec, offset_vec):
    row_mean = jnp.mean(values, axis=-1, keepdims=True)
    centered = values - row_mean
    variance = jnp.mean(centered * centered, axis=-1, keepdims=True)
    return centered * lax.rsqrt(variance + norm_eps) * gain_vec + offset_vec


def exact_gelu(values):
    return jax.nn.gelu(values, approximate=False)


def block_length(seq_rows):
    return min(512, seq_rows)


def forward_block(query_block, key_rows, value_rows):
    score_scale = query_block.shape[2] ** (-0.5)
    scores = (
        jnp.einsum("qhd,khd->hqk", query_block, key_rows, preferred_element_type=jnp.float32)
        * score_scale
    )
    row_peak = jnp.max(scores, axis=2, keepdims=True)
    weights = jnp.exp(scores - row_peak)
    row_total = jnp.sum(weights, axis=2, keepdims=True)
    probabilities = (weights / row_total).astype(jnp.bfloat16)
    attended = jnp.einsum(
        "hqk,khd->qhd", probabilities, value_rows, preferred_element_type=jnp.float32
    )
    return (attended.astype(jnp.bfloat16), row_peak + jnp.log(row_total))


def attend_forward(inputs):
    queries, key_rows, value_rows = inputs
    seq_rows = queries.shape[0]
    block_rows = block_length(seq_rows)
    query_blocks = queries.reshape((seq_rows // block_rows, block_rows) + queries.shape[1:])

    def one_block(query_block):
        return forward_block(query_block, key_rows, value_rows)

    attended, log_total = lax.map(one_block, query_blocks)
    return (attended.reshape(queries.shape), log_total)


def attend_backward(inputs):
    queries, key_rows, value_rows, log_totals, grad_rows = inputs
    seq_rows = queries.shape[0]
    block_rows = block_length(seq_rows)
    block_shape = (seq_rows // block_rows, block_rows) + queries.shape[1:]
    score_scale = queries.shape[2] ** (-0.5)

    def one_block(carry, pieces):
        keys_acc, values_acc = carry
        query_block, log_total, grad_block = pieces
        scores = (
            jnp.einsum("qhd,khd->hqk", query_block, key_rows, preferred_element_type=jnp.float32)
            * score_scale
        )
        probabilities = jnp.exp(scores - log_total)
        grad_probs = jnp.einsum(
            "qhd,khd->hqk", grad_block, value_rows, preferred_element_type=jnp.float32
        )
        row_dot = jnp.sum(probabilities * grad_probs, axis=2, keepdims=True)
        grad_scores = (probabilities * (grad_probs - row_dot)).astype(jnp.bfloat16)
        grad_queries = (
            jnp.einsum("hqk,khd->qhd", grad_scores, key_rows, preferred_element_type=jnp.float32)
            * score_scale
        )
        keys_acc = (
            keys_acc
            + jnp.einsum(
                "hqk,qhd->khd", grad_scores, query_block, preferred_element_type=jnp.float32
            )
            * score_scale
        )
        values_acc = values_acc + jnp.einsum(
            "hqk,qhd->khd",
            probabilities.astype(jnp.bfloat16),
            grad_block,
            preferred_element_type=jnp.float32,
        )
        return ((keys_acc, values_acc), grad_queries)

    empty = jnp.zeros(key_rows.shape, jnp.float32)
    (grad_keys, grad_values), grad_queries = lax.scan(
        one_block,
        (empty, empty),
        (queries.reshape(block_shape), log_totals, grad_rows.reshape(block_shape)),
    )
    return (grad_queries.reshape(queries.shape), grad_keys, grad_values)


def body(
    tokens,
    out_grad,
    item_counts,
    group_dataset,
    variable_mask,
    first_gain,
    first_shift,
    input_weight,
    input_bias,
    output_weight,
    output_bias,
    second_gain,
    second_shift,
    up_weight,
    up_bias,
    down_weight,
    down_bias,
):
    local_rows = tokens.shape[0]
    shard_count = lax.axis_size("mp")
    group_rows = local_rows * shard_count
    item_total = group_rows // SEQ
    local_width = input_weight.shape[2]
    head_local = local_width // HEAD_DIM
    row_index = lax.axis_index("mp") * local_rows + jnp.arange(local_rows, dtype=jnp.int32)
    live_rows = (row_index // SEQ < item_counts[0]).astype(jnp.float32)[:, None]
    dataset_hit = jnp.arange(variable_mask.shape[0], dtype=jnp.int32) == group_dataset[0]
    own_units = (
        item_counts[0] * jnp.sum(jnp.where(dataset_hit[:, None], variable_mask, 0))
    ).astype(jnp.float32)
    rows_float = tokens.astype(jnp.float32)
    normed1, first_pull = jax.vjp(layer_norm, rows_float, first_gain, first_shift)
    normed1_all = lax.all_gather(normed1.astype(jnp.bfloat16), "mp", axis=0, tiled=True)
    projected = jnp.einsum(
        "rd,jdc->rjc", normed1_all, input_weight, preferred_element_type=jnp.float32
    )
    queries = (projected[:, 0] + input_bias[0]).astype(jnp.bfloat16)
    key_rows = projected[:, 1].astype(jnp.bfloat16)
    value_rows = (projected[:, 2] + input_bias[1]).astype(jnp.bfloat16)
    item_shape = (item_total, SEQ, head_local, HEAD_DIM)
    attended, log_totals = lax.map(
        attend_forward,
        (queries.reshape(item_shape), key_rows.reshape(item_shape), value_rows.reshape(item_shape)),
    )
    merged = attended.reshape(group_rows, local_width)
    attention_part = lax.psum_scatter(
        jnp.dot(merged, output_weight, preferred_element_type=jnp.float32),
        "mp",
        scatter_dimension=0,
        tiled=True,
    )
    middle = rows_float + attention_part + output_bias
    normed2, second_pull = jax.vjp(layer_norm, middle, second_gain, second_shift)
    normed2_all = lax.all_gather(normed2.astype(jnp.bfloat16), "mp", axis=0, tiled=True)
    hidden = jnp.dot(normed2_all, up_weight, preferred_element_type=jnp.float32) + up_bias
    activated, gelu_pull = jax.vjp(exact_gelu, hidden)
    activated_low = activated.astype(jnp.bfloat16)
    feedforward_part = lax.psum_scatter(
        jnp.dot(activated_low, down_weight, preferred_element_type=jnp.float32).astype(
            jnp.bfloat16
        ),
        "mp",
        scatter_dimension=0,
        tiled=True,
    ).astype(jnp.float32)
    result = ((middle + feedforward_part + down_bias) * live_rows).astype(jnp.bfloat16)
    out_cotangent = out_grad.astype(jnp.float32) * live_rows
    cotangent_all = lax.all_gather(out_cotangent.astype(jnp.bfloat16), "mp", axis=0, tiled=True)
    down_grad = jnp.einsum(
        "rf,rd->fd", activated_low, cotangent_all, preferred_element_type=jnp.float32
    )
    down_bias_grad = jnp.sum(out_cotangent, axis=0)
    activated_grad = jnp.einsum(
        "rd,fd->rf", cotangent_all, down_weight, preferred_element_type=jnp.float32
    )
    (hidden_grad,) = gelu_pull(activated_grad)
    up_bias_grad = jnp.sum(hidden_grad, axis=0)
    hidden_low = hidden_grad.astype(jnp.bfloat16)
    up_grad = jnp.einsum("rd,rf->df", normed2_all, hidden_low, preferred_element_type=jnp.float32)
    normed2_grad = lax.psum_scatter(
        jnp.einsum("rf,df->rd", hidden_low, up_weight, preferred_element_type=jnp.float32),
        "mp",
        scatter_dimension=0,
        tiled=True,
    )
    middle_part, second_gain_grad, second_shift_grad = second_pull(normed2_grad)
    middle_grad = out_cotangent + middle_part
    output_bias_grad = jnp.sum(middle_grad, axis=0)
    middle_all = lax.all_gather(middle_grad.astype(jnp.bfloat16), "mp", axis=0, tiled=True)
    output_grad = jnp.einsum("rc,rd->cd", merged, middle_all, preferred_element_type=jnp.float32)
    merged_grad = jnp.einsum(
        "rd,cd->rc", middle_all, output_weight, preferred_element_type=jnp.float32
    ).astype(jnp.bfloat16)
    grad_queries, grad_keys, grad_values = lax.map(
        attend_backward,
        (
            queries.reshape(item_shape),
            key_rows.reshape(item_shape),
            value_rows.reshape(item_shape),
            log_totals,
            merged_grad.reshape(item_shape),
        ),
    )
    grad_queries = grad_queries.reshape(group_rows, local_width)
    grad_keys = grad_keys.reshape(group_rows, local_width)
    grad_values = grad_values.reshape(group_rows, local_width)
    input_bias_grad = jnp.stack([jnp.sum(grad_queries, axis=0), jnp.sum(grad_values, axis=0)])
    inputs_low = jnp.stack([grad_queries, grad_keys, grad_values], axis=1).astype(jnp.bfloat16)
    input_grad = jnp.einsum(
        "rd,rjc->jdc", normed1_all, inputs_low, preferred_element_type=jnp.float32
    )
    normed1_grad = lax.psum_scatter(
        jnp.einsum("rjc,jdc->rd", inputs_low, input_weight, preferred_element_type=jnp.float32),
        "mp",
        scatter_dimension=0,
        tiled=True,
    )
    rows_part, first_gain_grad, first_shift_grad = first_pull(normed1_grad)
    token_grad = (middle_grad + rows_part).astype(jnp.bfloat16)
    large_sums = lax.psum(
        (
            input_grad * own_units,
            input_bias_grad * own_units,
            output_grad * own_units,
            up_grad * own_units,
            up_bias_grad * own_units,
            down_grad * own_units,
        ),
        "dp",
    )
    counted = lax.psum(
        (
            first_gain_grad * own_units,
            first_shift_grad * own_units,
            output_bias_grad * own_units,
            second_gain_grad * own_units,
            second_shift_grad * own_units,
            down_bias_grad * own_units,
            own_units / shard_count,
        ),
        ("dp", "mp"),
    )
    finals = tuple((member / counted[6] for member in large_sums + counted[:6]))
    return (
        result,
        token_grad,
        finals[6],
        finals[7],
        finals[0],
        finals[1],
        finals[2],
        finals[8],
        finals[9],
        finals[10],
        finals[3],
        finals[4],
        finals[5],
        finals[11],
    )


def solution(mesh):
    in_specs = (
        P(("dp", "mp"), None),
        P(("dp", "mp"), None),
        P("dp"),
        P("dp"),
        P(),
        P(),
        P(),
        P(None, None, "mp"),
        P(None, "mp"),
        P("mp", None),
        P(),
        P(),
        P(),
        P(None, "mp"),
        P("mp"),
        P("mp", None),
        P(),
    )
    out_specs = (
        P(("dp", "mp"), None),
        P(("dp", "mp"), None),
        P(),
        P(),
        P(None, None, "mp"),
        P(None, "mp"),
        P("mp", None),
        P(),
        P(),
        P(),
        P(None, "mp"),
        P("mp"),
        P("mp", None),
        P(),
    )
    return jax.shard_map(body, mesh=mesh, in_specs=in_specs, out_specs=out_specs, check_vma=False)
```

profile of v0, /device:TPU:0, one launch (start us, length us, event | category | flops | bytes accessed | tf_op | source)
XLA Modules:
  0.0 1890.1 jit_solution(8937751717753382836)
XLA Ops:
  15.3 60.9 %all-gather.5.cloned.1.call-done = bf16[4096,1024]{1,0:T(8,128)(2,1)} async-done(((bf16[1024,1024]{1,0:T(8,128)(2,1)}), bf16[4096,1024]{1,0:T(8,128)(2,1)}) %all-gather.5.cloned.1.call-update) | async-done | bytes 8388624 | tf_op jit(solution)/shard_map/all_gather | solution.py:138
  76.2 9.7 fusion.48
  141.9 126.2 %while.54 = (s32[]{:T(128)}, bf16[2,2048,4,64]{3,2,1,0:T(4,128)(2,1)}, f32[2,4,4,512,1]{3,2,1,4,0:T(4,128)}, bf16[2,2048,4,64]{1,3,2,0:T(8,128)(2,1)}, bf16[2,20...) while((s32[]{:T(128)}, ...), condition=%wide.region_7.8_spmd, body=%wide.region_2.7_spmd.sunk | while | flops 1111619584 | bytes 74055984 | solution.py:146
  150.0 47.5 %while.57 = (s32[]{:T(128)}, bf16[4,512,4,64]{1,3,2,0:T(8,128)(2,1)}, f32[4,4,512,1]{2,1,3,0:T(4,128)S(1)}, bf16[4,512,4,64]{1,3,2,0:T(8,128)(2,1)}, bf16[2048,4...) while((s32[]{:T(128)}, bf16[4,512,4,64]{1,3,2,0:T(8,128)(2,1)}, ...), condition=%wide.region_6.6_spmd, body=%wide.region_3.5_spmd.sunk | while | flops 1111619584 | bytes 57213052 | solution.py:53
  213.1 47.4 %while.57 = (s32[]{:T(128)}, bf16[4,512,4,64]{1,3,2,0:T(8,128)(2,1)}, f32[4,4,512,1]{2,1,3,0:T(4,128)S(1)}, bf16[4,512,4,64]{1,3,2,0:T(8,128)(2,1)}, bf16[2048,4...) while((s32[]{:T(128)}, bf16[4,512,4,64]{1,3,2,0:T(8,128)(2,1)}, ...), condition=%wide.region_6.6_spmd, body=%wide.region_3.5_spmd.sunk | while | flops 1111619584 | bytes 57213052 | solution.py:53
  275.1 9.7 fusion.92
  285.1 126.0 %reduce-scatter.5.cloned.1.call-done = f32[1024,1024]{1,0:T(8,128)} async-done(((f32[4096,1024]{1,0:T(8,128)}), f32[1024,1024]{1,0:T(8,128)}) %reduce-scatter.5.cloned.1.call-update) | async-done | bytes 4194320 | tf_op jit(solution)/shard_map/reduce_scatter | solution.py:151
  424.0 53.7 %all-gather.7.cloned.1.call-done = bf16[4096,1024]{1,0:T(8,128)(2,1)} async-done(((bf16[1024,1024]{1,0:T(8,128)(2,1)}), bf16[4096,1024]{1,0:T(8,128)(2,1)}) %all-gather.7.cloned.1.call-update) | async-done | bytes 8388624 | tf_op jit(solution)/shard_map/all_gather | solution.py:159
  477.7 16.2 fusion.93
  493.9 44.2 %all-gather.9.cloned.1.call-done = bf16[4096,1024]{1,0:T(8,128)(2,1)} async-done(((bf16[1024,1024]{1,0:T(8,128)(2,1)}), bf16[4096,1024]{1,0:T(8,128)(2,1)}) %all-gather.9.cloned.1.call-update) | async-done | bytes 8388624 | tf_op jit(solution)/shard_map/all_gather | solution.py:173
  538.1 51.5 %fusion.84 = (f32[1024]{0:T(1024)}, bf16[4096,1024]{1,0:T(8,128)(2,1)S(1)}, f32[4096,1024]{1,0:T(8,128)}) fusion(f32[4096,1024]{1,0:T(8,128)} %fusion.93, f32[1024]{0:T(1024)S(1)} %copy-done.59, bf16[4096,1024]{1,0:T(8,128)(2,1)} %all-gather.9.cloned.1.call-done, bf16[1024,1024]{1,0:T(8,128)(2,1)S(1)} %copy-done), kind=kOutput, calls=%fused_computation.172 | convolution fusion | flops 8900312064 | bytes 52436992 | tf_op jit(solution)/shard_map/rd,fd->rf/dot_general | solution.py:178
  593.0 12.1 fusion.64
  605.2 15.2 multiply_convert_fusion.1
  625.4 10.8 convolution_convert_fusion
  636.3 95.1 %reduce-scatter.9.cloned.1.call-done = f32[1024,1024]{1,0:T(8,128)} async-done(((f32[4096,1024]{1,0:T(8,128)}), f32[1024,1024]{1,0:T(8,128)}) %reduce-scatter.9.cloned.1.call-update) | async-done | bytes 4194320 | tf_op jit(solution)/shard_map/reduce_scatter | solution.py:185
  736.3 69.3 %reduce-scatter.7.cloned.1.call-done = bf16[1024,1024]{1,0:T(8,128)(2,1)} async-done(((bf16[4096,1024]{1,0:T(8,128)(2,1)}), bf16[1024,1024]{1,0:T(8,128)(2,1)}) %reduce-scatter.7.cloned.1.call-update) | async-done | bytes 2097168 | tf_op jit(solution)/shard_map/reduce_scatter | solution.py:163
  815.8 58.4 %all-gather.11.cloned.1.call-done = bf16[4096,1024]{1,0:T(8,128)(2,1)} async-done(((bf16[1024,1024]{1,0:T(8,128)(2,1)}), bf16[4096,1024]{1,0:T(8,128)(2,1)}) %all-gather.11.cloned.1.call-update) | async-done | bytes 8388624 | tf_op jit(solution)/shard_map/all_gather | solution.py:194
  890.1 373.1 %while.56 = (s32[]{:T(128)}, f32[2,2048,4,64]{3,2,1,0:T(4,128)}, bf16[2,2048,4,64]{1,3,2,0:T(8,128)(2,1)}, f32[2,2048,4,64]{1,3,2,0:T(8,128)}, bf16[2,2048,4,64]...) while((s32[]{:T(128)}, f32[2,2048,4,64]{3,2,1,0:T(4,128)}, ...), condition=%wide.region_19.20_spmd, body=%wide.region_15.19_spmd.sunk | while | flops 2737436672 | bytes 302637728 | solution.py:199
  903.9 158.2 %while.58 = (s32[]{:T(128)}, f32[2048,4,64]{0,2,1:T(8,128)}, f32[2048,4,64]{0,2,1:T(8,128)}, f32[4,512,4,64]{1,3,2,0:T(8,128)}, bf16[4,512,4,64]{1,3,2,0:T(8,128...) while((s32[]{:T(128)}, f32[2048,4,64]{0,2,1:T(8,128)}, ...), condition=%wide.region_18.18_spmd.clone, body=%wide.region_16.17_spmd.clone.sunk | while | flops 2737436672 | bytes 206102832 | solution.py:97
  912.6 9.2 multiply_reduce_fusion.7
  921.7 8.1 multiply_convert_fusion.4
  935.9 7.6 fusion.152
  952.1 9.2 multiply_reduce_fusion.7
  961.3 8.1 multiply_convert_fusion.4
  991.7 9.2 multiply_reduce_fusion.7
  1000.9 8.1 multiply_convert_fusion.4
  1031.2 9.2 multiply_reduce_fusion.7
  1040.4 8.1 multiply_convert_fusion.4
  1054.5 7.6 fusion.152
  1090.2 158.2 %while.58 = (s32[]{:T(128)}, f32[2048,4,64]{0,2,1:T(8,128)}, f32[2048,4,64]{0,2,1:T(8,128)}, f32[4,512,4,64]{1,3,2,0:T(8,128)}, bf16[4,512,4,64]{1,3,2,0:T(8,128...) while((s32[]{:T(128)}, f32[2048,4,64]{0,2,1:T(8,128)}, ...), condition=%wide.region_18.18_spmd.clone, body=%wide.region_16.17_spmd.clone.sunk | while | flops 2737436672 | bytes 206102832 | solution.py:97
  1098.8 9.2 multiply_reduce_fusion.7
  1108.0 8.1 multiply_convert_fusion.4
  1122.1 7.6 fusion.152
  1138.4 9.2 multiply_reduce_fusion.7
  1147.6 8.1 multiply_convert_fusion.4
  1177.9 9.2 multiply_reduce_fusion.7
  1187.1 8.1 multiply_convert_fusion.4
  1217.5 9.2 multiply_reduce_fusion.7
  1226.6 8.1 multiply_convert_fusion.4
  1291.7 10.6 fusion.90
  1314.4 9.6 convolution_bitcast_fusion
  1326.1 15.9 fusion.68
  1342.0 17.9 convolution_multiply_fusion.2
  1363.4 8.7 multiply_bitcast_fusion
  1373.0 21.7 %all-reduce.1 = (f32[2,256]{1,0:T(2,128)S(1)}, f32[1024]{0:T(1024)S(1)}) all-reduce(f32[2,256]{1,0:T(2,128)S(1)} %maximum_multiply_fusion, f32[1024]{0:T(1024)S(1)} %broadcast_multiply_fusion.1), channel_id=1, replica_groups=mesh['dp'=8,'mp'=4] {'dp'}, use_global_device_ids=true, to_apply=%region_32.33 | all-reduce | flops 1536 | bytes 12288 | tf_op jit(solution)/shard_map/psum | solution.py:225
  1394.7 55.6 %reduce-scatter.11.cloned.1.call-done = f32[1024,1024]{1,0:T(8,128)} async-done(((f32[4096,1024]{1,0:T(8,128)}), f32[1024,1024]{1,0:T(8,128)}) %reduce-scatter.11.cloned.1.call-update) | async-done | bytes 4194320 | tf_op jit(solution)/shard_map/reduce_scatter | solution.py:217
  1459.9 43.9 %all-reduce = (f32[1024]{0:T(1024)S(1)}, f32[]{:T(128)}, f32[1024]{0:T(1024)S(1)}, f32[1024]{0:T(1024)S(1)}, f32[1024]{0:T(1024)S(1)}, /*index=5*/f32[1024]{0:T(1024)S(1)}, f32[1024]{0:T(1024)S(1)}) all-reduce(f32[1024]{0:T(1024)S(1)} %get-tuple-element.398, f32[]{:T(128)S(6)} %div.131, ...), channel_id=1, replica_groups=mesh['dp'=8,'mp'=4] {'dp','mp'}, use_global_device_ids=true, to_apply=%region_25.26 | all-reduce | flops 6145 | bytes 49160 | tf_op jit(solution)/shard_map/psum | solution.py:236
  1505.0 352.7 %all-reduce.5.cloned.1.call-done = (f32[3,1024,256]{1,2,0:T(8,128)}, f32[256,1024]{1,0:T(8,128)}, f32[1024,1024]{1,0:T(8,128)}, f32[1024,1024]{1,0:T(8,128)}) async-done(((f32[3,1024,256]{1,2,0:T(8,128)}, f32[256,1024]{1,0:T(8,128)}, f32[1024,1024]{1,0:T(8,128)}, f32[1024,1024]{1,0:T(8,128)}), (f32[3,1024,256]{1,2,0:T(8,128)}, f32[256,1024]{1,0:T(8,128)}, f32[1024,1024]{1,0:T(8,128)}, ...) | async-done | bytes 12582928 | tf_op jit(solution)/shard_map/psum | solution.py:225
  (450 shorter events, 541.8 us)
Async XLA Ops:
  7.2 530.9 %copy-start = (bf16[1024,1024]{1,0:T(8,128)(2,1)S(1)}, bf16[1024,1024]{1,0:T(8,128)(2,1)}, u32[]{:S(2)}) copy-start(bf16[1024,1024]{1,0:T(8,128)(2,1)} %param.40) | copy-start | bytes 6291460
  7.2 69.0 %all-gather.5.cloned.1.call-start = ((), (), s32[]{:S(2)}) async-start(), calls=%async_computation.4 | async-start | bytes 10485760 | tf_op jit(solution)/shard_map/all_gather | solution.py:138
  15.1 396.0 %reduce-scatter.5.cloned.1.call-start = ((), (), s32[]{:S(2)}) async-start(), calls=%async_computation.5 | async-start | bytes 20971520 | tf_op jit(solution)/shard_map/reduce_scatter | solution.py:151
  284.8 126.3 %copy-start.53 = (f32[1024]{0:T(1024)S(1)}, f32[1024]{0:T(1024)}, u32[]{:S(2)}) copy-start(f32[1024]{0:T(1024)} %param.35) | copy-start | bytes 12292
  284.8 192.9 %all-gather.7.cloned.1.call-start = ((), (), s32[]{:S(2)}) async-start(), calls=%async_computation.6 | async-start | bytes 10485760 | tf_op jit(solution)/shard_map/all_gather | solution.py:159
  419.3 118.8 %all-gather.9.cloned.1.call-start = ((), (), s32[]{:S(2)}) async-start(), calls=%async_computation.8 | async-start | bytes 10485760 | tf_op jit(solution)/shard_map/all_gather | solution.py:173
  423.9 114.2 %copy-start.59 = (f32[1024]{0:T(1024)S(1)}, f32[1024]{0:T(1024)}, u32[]{:S(2)}) copy-start(f32[1024]{0:T(1024)} %param.39) | copy-start | bytes 12292
  423.9 307.5 %reduce-scatter.9.cloned.1.call-start = ((), (), s32[]{:S(2)}) async-start(), calls=%async_computation.9 | async-start | bytes 20971520 | tf_op jit(solution)/shard_map/reduce_scatter | solution.py:185
  538.1 54.9 %copy-start.61 = (bf16[1024,1024]{1,0:T(8,128)(2,1)S(1)}, bf16[1024,1024]{1,0:T(8,128)(2,1)}, u32[]{:S(2)}) copy-start(bf16[1024,1024]{1,0:T(8,128)(2,1)} %param.38) | copy-start | bytes 6291460
  605.1 200.5 %reduce-scatter.7.cloned.1.call-start = ((), (), s32[]{:S(2)}) async-start(), calls=%async_computation.7 | async-start | bytes 10485760 | tf_op jit(solution)/shard_map/reduce_scatter | solution.py:163
  636.2 95.2 %copy-start.33 = (f32[1024]{0:T(1024)S(1)}, f32[1024]{0:T(1024)}, u32[]{:S(2)}) copy-start(f32[1024]{0:T(1024)} %copy-done.32) | copy-start | bytes 12292
  636.2 95.2 %copy-start.38 = (f32[1024]{0:T(1024)S(1)}, f32[1024]{0:T(1024)}, u32[]{:S(2)}) copy-start(f32[1024]{0:T(1024)} %copy-done.37) | copy-start | bytes 12292
  636.2 95.2 %copy-start.44 = (f32[1024]{0:T(1024)S(1)}, f32[1024]{0:T(1024)}, u32[]{:S(2)}) copy-start(f32[1024]{0:T(1024)} %param.36) | copy-start | bytes 12292
  636.2 100.1 %copy-start.48 = (f32[1024]{0:T(1024)S(1)}, f32[1024]{0:T(1024)}, u32[]{:S(2)}) copy-start(f32[1024]{0:T(1024)} %copy-done.47) | copy-start | bytes 12292
  636.2 169.4 %copy-start.35 = (f32[1024]{0:T(1024)S(1)}, f32[1024]{0:T(1024)}, u32[]{:S(2)}) copy-start(f32[1024]{0:T(1024)} %copy-done.34) | copy-start | bytes 12292
  636.2 169.4 %copy-start.55 = (f32[1024]{0:T(1024)S(1)}, f32[1024]{0:T(1024)}, u32[]{:S(2)}) copy-start(f32[1024]{0:T(1024)} %param.41) | copy-start | bytes 12292
  636.3 237.9 %all-gather.11.cloned.1.call-start = ((), (), s32[]{:S(2)}) async-start(), calls=%async_computation.10 | async-start | bytes 10485760 | tf_op jit(solution)/shard_map/all_gather | solution.py:194
  736.3 77.3 %copy-start.18 = (bf16[1024,1024]{1,0:T(8,128)(2,1)S(1)}, bf16[1024,1024]{1,0:T(8,128)(2,1)}, u32[]{:S(2)}) copy-start(bf16[1024,1024]{1,0:T(8,128)(2,1)} %param.26) | copy-start | bytes 6291460
  813.6 60.6 %copy-start.29 = (bf16[256,1024]{1,0:T(8,128)(2,1)S(1)}, bf16[256,1024]{1,0:T(8,128)(2,1)}, u32[]{:S(2)}) copy-start(bf16[256,1024]{1,0:T(8,128)(2,1)} %param.34) | copy-start | bytes 1572868
  815.7 634.5 %reduce-scatter.11.cloned.1.call-start = ((), (), s32[]{:S(2)}) async-start(), calls=%async_computation.11 | async-start | bytes 20971520 | tf_op jit(solution)/shard_map/reduce_scatter | solution.py:217
  912.6 9.2 copy-start.4
  921.7 11.3 copy-start.6
  952.1 9.2 copy-start.4
  961.3 11.3 copy-start.6
  991.7 9.2 copy-start.4
  1000.9 11.3 copy-start.6
  1031.2 9.2 copy-start.4
  1040.4 11.3 copy-start.6
  1108.0 11.3 copy-start.6
  1138.4 9.2 copy-start.4
  1147.6 11.3 copy-start.6
  1187.1 11.3 copy-start.6
  1217.4 9.2 copy-start.4
  1226.6 11.3 copy-start.6
  1324.0 533.7 %all-reduce.5.cloned.1.call-start = ((), (), s32[]{:S(2)}) async-start(), calls=%async_computation.12 | async-start | bytes 25165824 | tf_op jit(solution)/shard_map/psum | solution.py:225
  1326.1 33.9 %slice-start = ((s8[8388608]{0:T(1024)(128)(4,1)}), s8[4194304]{0:T(1024)(128)(4,1)S(1)}, s32[]{:S(2)}) async-start(s8[8388608]{0:T(1024)(128)(4,1)} %bitcast.180), calls=%async_computation.13 | async-start | bytes 8388608
  1326.1 37.2 %slice-start.2 = ((s8[6291456]{0:T(1024)(128)(4,1)}), s8[4194304]{0:T(1024)(128)(4,1)S(1)}, s32[]{:S(2)}) async-start(s8[6291456]{0:T(1024)(128)(4,1)} %bitcast.182), calls=%async_computation.15 | async-start | bytes 8388608
  1326.1 37.2 %slice-start.4 = ((s8[8388608]{0:T(1024)(128)(4,1)}), s8[4194304]{0:T(1024)(128)(4,1)S(1)}, s32[]{:S(2)}) async-start(s8[8388608]{0:T(1024)(128)(4,1)} %bitcast.184), calls=%async_computation.17 | async-start | bytes 8388608
  1342.0 17.9 copy-start.15
  1342.0 17.9 slice-start.1
  1342.0 21.3 %slice-start.3 = ((s8[6291456]{0:T(1024)(128)(4,1)}), s8[2097152]{0:T(1024)(128)(4,1)S(1)}, s32[]{:S(2)}) async-start(s8[6291456]{0:T(1024)(128)(4,1)} %bitcast.182), calls=%async_computation.16 | async-start | bytes 4194304
  1342.0 21.3 %slice-start.5 = ((s8[8388608]{0:T(1024)(128)(4,1)}), s8[4194304]{0:T(1024)(128)(4,1)S(1)}, s32[]{:S(2)}) async-start(s8[8388608]{0:T(1024)(128)(4,1)} %bitcast.184), calls=%async_computation.18 | async-start | bytes 8388608
  1372.1 78.2 %copy-start.11 = (bf16[1024,1024]{1,0:T(8,128)(2,1)S(1)}, bf16[1024,1024]{1,0:T(8,128)(2,1)}, u32[]{:S(2)}) copy-start(bf16[1024,1024]{1,0:T(8,128)(2,1)} %param.25) | copy-start | bytes 6291460
  1372.1 78.2 %copy-start.31 = (f32[1024]{0:T(1024)S(1)}, f32[1024]{0:T(1024)}, u32[]{:S(2)}) copy-start(f32[1024]{0:T(1024)} %copy-done.30) | copy-start | bytes 12292
  1372.1 78.2 %copy-start.40 = (f32[1024]{0:T(1024)S(1)}, f32[1024]{0:T(1024)}, u32[]{:S(2)}) copy-start(f32[1024]{0:T(1024)} %param.30) | copy-start | bytes 12292
  1372.1 81.5 %copy-start.46 = (f32[1024]{0:T(1024)S(1)}, f32[1024]{0:T(1024)}, u32[]{:S(2)}) copy-start(f32[1024]{0:T(1024)} %copy-done.45) | copy-start | bytes 12292
  1372.1 81.6 %copy-start.42 = (f32[1024]{0:T(1024)S(1)}, f32[1024]{0:T(1024)}, u32[]{:S(2)}) copy-start(f32[1024]{0:T(1024)} %copy-done.41) | copy-start | bytes 12292
  1869.8 13.6 copy-start.1
  (78 other events, 299.5 us)
Sparse Core Ops, SparseCore 0:
  15.2 60.9 all-gather.4
  285.0 126.0 reduce-scatter.4
  419.4 58.2 all-gather.6
  479.8 58.2 all-gather.8
  605.3 126.0 reduce-scatter.8
  733.8 71.7 reduce-scatter.6
  815.8 58.2 all-gather.10
  1324.1 126.0 reduce-scatter.10
  1456.2 401.4 all-reduce.4
where the time goes:
time: 1900 us; the launch traced here: 1890 us
  waiting for transfers between devices  916 us (48%)
  matrix products  460 us (24%)
  local copies, waits for them, and re-layouts  240 us (13%)
  other arithmetic  190 us (10%)
  blocking collectives  65.6 us (3%)
    psum x1, waiting for transfers between devices, body(): lax.psum((input_grad * own_units, input_bias_grad * own_units, output_gra...  353 us
    reduce_scatter x1, waiting for transfers between devices, body(): lax.psum_scatter(jnp.dot(merged, output_weight, preferred_element_type=jn...  126 us
    reduce_scatter x1, waiting for transfers between devices, body(): lax.psum_scatter(jnp.einsum('rf,df->rd', hidden_low, up_weight, preferred...  95.1 us
    dot_general x8, matrix products, one_block(): jnp.einsum('qhd,khd->hqk', grad_block, value_rows, preferred_element_type...  73.4 us
    reduce_scatter x1, waiting for transfers between devices, body(): lax.psum_scatter(jnp.dot(activated_low, down_weight, preferred_element_ty...  69.3 us
    convert_element_type x8, other arithmetic, one_block(): grad_scores = (probabilities * (grad_probs - row_dot)).astype(jnp.bfloat16)  64.5 us
    dot_general x8, matrix products, one_block(): jnp.einsum('hqk,khd->qhd', grad_scores, key_rows, preferred_element_type=...  60.9 us
    all_gather x1, waiting for transfers between devices, body(): lax.all_gather(normed1.astype(jnp.bfloat16), 'mp', axis=0, tiled=True)  60.9 us
  transfers between devices with their start and end apart: 9, of which 9 were waited for; matrix products, arithmetic and copies ran while one was open for 6% of the time, Pallas kernels for 0%

commit v1 on v0

v1 whole, which is shorter than its diff:
```python
import jax
import jax.numpy as jnp
from jax import lax
from jax.experimental import pallas as pl
from jax.experimental.pallas import tpu as pltpu
from jax.sharding import PartitionSpec as P

HEAD_DIM = 64
LANES = 128
norm_eps = 1e-06
SCALE = HEAD_DIM**-0.5
LOG2E = 1.4426950408889634
RSQRT2 = 0.7071067811865476
RSQRT2PI = 0.3989422804014327

bf16 = jnp.bfloat16
f32 = jnp.float32
NN = (((1,), (0,)), ((), ()))
NT = (((1,), (1,)), ((), ()))
TN = (((0,), (0,)), ((), ()))
VMEM_BYTES = 60 << 20


def dot(left, right, dims=NN):
    return lax.dot_general(left, right, dims, preferred_element_type=f32)


def shape(dims, dtype):
    return jax.ShapeDtypeStruct(dims, dtype)


def whole(array):
    rank = len(array.shape)
    return pl.BlockSpec(array.shape, lambda *_: (0,) * rank, pipeline_mode=pl.Buffered(1))


def scalars():
    return pl.BlockSpec(memory_space=pltpu.SMEM)


def call(kernel, name, grid, in_specs, out_specs, out_shape, scratch=(), flops=0, nbytes=0, exps=0):
    return pl.pallas_call(
        kernel,
        name=name,
        grid=grid,
        in_specs=in_specs,
        out_specs=out_specs,
        out_shape=out_shape,
        scratch_shapes=list(scratch),
        compiler_params=pltpu.CompilerParams(vmem_limit_bytes=VMEM_BYTES),
        cost_estimate=pl.CostEstimate(
            flops=int(flops), bytes_accessed=int(nbytes), transcendentals=int(exps)
        ),
    )


def split_two(values):
    high = values.astype(bf16)
    return high, (values - high.astype(f32)).astype(bf16)


def split_three(values):
    high = values.astype(bf16)
    rest = values - high.astype(f32)
    mid = rest.astype(bf16)
    return high, mid, (rest - mid.astype(f32)).astype(bf16)


def stat_rows(vector, rows):
    high, mid, rest = (part.astype(f32) for part in split_three(vector))
    row = lax.broadcasted_iota(jnp.int32, (rows, vector.shape[1]), 0)
    return jnp.where(
        row == 0, high, jnp.where(row == 1, mid, jnp.where(row == 2, rest, 0.0))
    ).astype(bf16)


def normalize(values):
    centered = values - jnp.mean(values, axis=-1, keepdims=True)
    variance = jnp.mean(centered * centered, axis=-1, keepdims=True)
    inverse = lax.rsqrt(variance + norm_eps)
    return centered * inverse, inverse


def norm_back(grad, gain, unit, inverse):
    scaled = grad * gain
    return inverse * (
        scaled
        - jnp.mean(scaled, axis=-1, keepdims=True)
        - unit * jnp.mean(scaled * unit, axis=-1, keepdims=True)
    )


def add_rows(ref, rows, first):
    @pl.when(first)
    def _():
        ref[...] = jnp.zeros_like(ref)

    for place, row in enumerate(rows):
        ref[place : place + 1, :] += row


def first_norm(tokens, out_grad, params, scal):
    rows, width = tokens.shape
    block = 256

    def kernel(scal_ref, tok_ref, grad_ref, par_ref, norm_ref, cot_ref):
        unit, _ = normalize(tok_ref[...].astype(f32))
        norm_ref[...] = (unit * par_ref[0:1, :] + par_ref[1:2, :]).astype(bf16)
        cot_ref[...] = (grad_ref[...].astype(f32) * scal_ref[0]).astype(bf16)

    spec = pl.BlockSpec((block, width), lambda i: (i, 0))
    return call(
        kernel,
        "first_norm",
        (rows // block,),
        [scalars(), spec, spec, whole(params)],
        [spec, spec],
        [shape((rows, width), bf16)] * 2,
        flops=20 * rows * width,
        nbytes=8 * rows * width,
    )(scal, tokens, out_grad, params)


def halves(block, width, count):
    own = pl.BlockSpec((block, width), lambda i, *_: (jnp.minimum(i, count - 1), 0))
    other = pl.BlockSpec((block, width), lambda i, *_: (jnp.maximum(i - count, 0), 0))
    return own, other


def pick(count, own_ref, other_ref):
    return jnp.where(pl.program_id(0) < count, own_ref[...], other_ref[...])


def project(norm_own, norm_other, weight, bias):
    rows, width = norm_own.shape
    cols = weight.shape[2]
    block = 512
    count = rows // block

    def kernel(own_ref, other_ref, w_ref, b_ref, q_ref, k_ref, v_ref):
        x = pick(count, own_ref, other_ref)
        q_ref[...] = (dot(x, w_ref[0]) + b_ref[0:1, :]).astype(bf16)
        k_ref[...] = dot(x, w_ref[1]).astype(bf16)
        v_ref[...] = (dot(x, w_ref[2]) + b_ref[1:2, :]).astype(bf16)

    out = pl.BlockSpec((block, cols), lambda i: (i, 0))
    return call(
        kernel,
        "project",
        (2 * count,),
        [*halves(block, width, count), whole(weight), whole(bias)],
        [out] * 3,
        [shape((2 * rows, cols), bf16)] * 3,
        flops=12 * rows * width * cols,
        nbytes=4 * rows * width + 6 * width * cols + 12 * rows * cols,
    )(norm_own, norm_other, weight, bias)


def attend_forward(queries, keys, values):
    rows, width = queries.shape
    block = min(1024, rows)
    chunk = 256
    steps = rows // chunk

    def kernel(q_ref, k_ref, v_ref, o_ref, ot_ref, lse_ref, k_two, v_turned):
        @pl.when(pl.program_id(1) == 0)
        def _():
            k = k_ref[...]
            lane = lax.broadcasted_iota(jnp.int32, k.shape, 1)
            rolled = pltpu.roll(k.astype(f32), HEAD_DIM, 1).astype(bf16)
            k_two[0] = jnp.where(lane < HEAD_DIM, k, rolled)
            k_two[1] = jnp.where(lane < HEAD_DIM, rolled, k)
            turned = v_ref[...].astype(f32).T
            ones = jnp.ones((HEAD_DIM, rows), bf16)
            v_turned[0] = jnp.concatenate([turned[:HEAD_DIM].astype(bf16), ones], 0)
            v_turned[1] = jnp.concatenate([ones, turned[HEAD_DIM:].astype(bf16)], 0)

        q_turned = q_ref[...].astype(f32).T * (SCALE * LOG2E)
        outs = []
        for head in range(2):
            at = head * HEAD_DIM
            q_two = jnp.concatenate(split_two(q_turned[at : at + HEAD_DIM]), 0)
            scores = [dot(k_two[head, pl.ds(j * chunk, chunk), :], q_two) for j in range(steps)]
            peak = None
            for part in scores:
                top = part.reshape(chunk // 8, 8, block).max(axis=0)
                peak = top if peak is None else jnp.maximum(peak, top)
            peak = jnp.max(peak, axis=0, keepdims=True)
            total = None
            for j in range(steps):
                weights = jnp.exp2(scores[j] - peak).astype(bf16)
                part = dot(v_turned[head, :, pl.ds(j * chunk, chunk)], weights)
                total = part if total is None else total + part
            row_sum = total[HEAD_DIM - at : HEAD_DIM - at + 1]
            outs.append(total[at : at + HEAD_DIM] / row_sum)
            lse_ref[head : head + 1, :] = peak + jnp.log2(row_sum)
        turned = jnp.concatenate(outs, 0)
        ot_ref[...] = turned
        o_ref[...] = turned.T.astype(bf16)

    by_query = pl.BlockSpec((block, LANES), lambda j, i: (i, j))
    by_key = pl.BlockSpec((rows, LANES), lambda j, i: (0, j))
    turned_spec = pl.BlockSpec((LANES, block), lambda j, i: (j, i))
    stat_spec = pl.BlockSpec((None, 8, block), lambda j, i: (j, 0, i))
    pairs = width // LANES
    return call(
        kernel,
        "attend_forward",
        (pairs, rows // block),
        [by_query, by_key, by_key],
        [by_query, turned_spec, stat_spec],
        [shape((rows, width), bf16), shape((width, rows), f32), shape((pairs, 8, rows), f32)],
        [pltpu.VMEM((2, rows, LANES), bf16), pltpu.VMEM((2, LANES, rows), bf16)],
        flops=16 * rows * rows * width,
        nbytes=12 * rows * width,
        exps=rows * rows * width // HEAD_DIM,
    )(queries, keys, values)


def attend_backward(queries, keys, values, out_grad, out_turned, stats):
    rows, width = queries.shape
    block = min(1024, rows)
    chunk = 256
    count = rows // block

    def kernel(
        q_ref, k_ref, v_ref, g_ref, ot_ref, lse_ref, dq_ref, dk_ref, dv_ref, sum_ref,
        k_wide, k_turned, v_wide, dk_acc, dv_acc,
    ):
        i = pl.program_id(1)

        @pl.when(i == 0)
        def _():
            k = k_ref[...]
            v = v_ref[...]
            lane = lax.broadcasted_iota(jnp.int32, k.shape, 1)
            k_rolled = pltpu.roll(k.astype(f32), HEAD_DIM, 1).astype(bf16)
            v_rolled = pltpu.roll(v.astype(f32), HEAD_DIM, 1).astype(bf16)
            ones = jnp.where(lane < 3, 1.0, 0.0).astype(bf16)
            k_wide[0] = jnp.concatenate([jnp.where(lane < HEAD_DIM, k, k_rolled), ones], 1)
            k_wide[1] = jnp.concatenate([jnp.where(lane < HEAD_DIM, k_rolled, k), ones], 1)
            tail = jnp.where(lane < HEAD_DIM + 3, 1.0, 0.0).astype(bf16)
            v_wide[0] = jnp.where(lane < HEAD_DIM, v, tail)
            v_wide[1] = jnp.where(lane < HEAD_DIM, v_rolled, tail)
            k_turned[...] = k.astype(f32).T.astype(bf16)
            dk_acc[...] = jnp.zeros_like(dk_acc)
            dv_acc[...] = jnp.zeros_like(dv_acc)
            sum_ref[...] = jnp.zeros_like(sum_ref)

        q_turned = q_ref[...].astype(f32).T
        q_low = q_turned.astype(bf16)
        q_turned = q_turned * (SCALE * LOG2E)
        g_turned = g_ref[...].astype(f32).T
        g_low = g_turned.astype(bf16)
        dqs = []
        for head in range(2):
            part = slice(head * HEAD_DIM, (head + 1) * HEAD_DIM)
            q_wide = jnp.concatenate(
                [*split_two(q_turned[part]), stat_rows(-lse_ref[head : head + 1, :], LANES)], 0
            )
            row_dot = jnp.sum(g_turned[part] * ot_ref[part, :], axis=0, keepdims=True)
            g_wide = jnp.concatenate([g_low[part], stat_rows(-row_dot, HEAD_DIM)], 0)
            dq = None
            for j in range(rows // chunk):
                at = pl.ds(j * chunk, chunk)
                probabilities = jnp.exp2(dot(k_wide[head, at, :], q_wide))
                shifted = dot(v_wide[head, at, :], g_wide)
                probs_low = probabilities.astype(bf16)
                score_grad = (probabilities * shifted).astype(bf16)
                dv_acc[part, at] += dot(g_low[part], probs_low, NT)
                dk_acc[part, at] += dot(q_low[part], score_grad, NT)
                add = dot(k_turned[part, at], score_grad)
                dq = add if dq is None else dq + add
            dqs.append(dq)
        dq = (jnp.concatenate(dqs, 0) * SCALE).T
        dq_ref[...] = dq.astype(bf16)
        sum_ref[0:1, :] += jnp.sum(dq, axis=0, keepdims=True)

        @pl.when(i == count - 1)
        def _():
            dk_ref[...] = (dk_acc[...] * SCALE).T.astype(bf16)
            dv = dv_acc[...].T
            dv_ref[...] = dv.astype(bf16)
            sum_ref[1:2, :] = jnp.sum(dv, axis=0, keepdims=True)

    by_query = pl.BlockSpec((block, LANES), lambda j, i: (i, j))
    by_key = pl.BlockSpec((rows, LANES), lambda j, i: (0, j))
    turned_spec = pl.BlockSpec((LANES, block), lambda j, i: (j, i))
    stat_spec = pl.BlockSpec((None, 8, block), lambda j, i: (j, 0, i))
    sum_spec = pl.BlockSpec((8, LANES), lambda j, i: (0, j))
    return call(
        kernel,
        "attend_backward",
        (width // LANES, count),
        [by_query, by_key, by_key, by_query, turned_spec, stat_spec],
        [by_query, by_key, by_key, sum_spec],
        [shape((rows, width), bf16)] * 3 + [shape((8, width), f32)],
        [
            pltpu.VMEM((2, rows, 2 * LANES), bf16),
            pltpu.VMEM((LANES, rows), bf16),
            pltpu.VMEM((2, rows, LANES), bf16),
            pltpu.VMEM((LANES, rows), f32),
            pltpu.VMEM((LANES, rows), f32),
        ],
        flops=40 * rows * rows * width,
        nbytes=20 * rows * width,
        exps=rows * rows * width // HEAD_DIM,
    )(queries, keys, values, out_grad, out_turned, stats)


def output_other(first, second, weight_one, weight_two):
    total, cols = first.shape
    rows = total // 2
    width = weight_one.shape[1]
    block = 512
    count = rows // block

    def kernel(a_ref, b_ref, wa_ref, wb_ref, out_ref):
        out_ref[...] = (dot(a_ref[...], wa_ref[...]) + dot(b_ref[...], wb_ref[...])).astype(bf16)

    spec = pl.BlockSpec((block, cols), lambda i: (i + count, 0))
    return call(
        kernel,
        "output_other",
        (count,),
        [spec, spec, whole(weight_one), whole(weight_two)],
        pl.BlockSpec((block, width), lambda i: (i, 0)),
        shape((rows, width), bf16),
        flops=4 * rows * cols * width,
        nbytes=4 * rows * cols + 2 * rows * width,
    )(first, second, weight_one, weight_two)


def output_own(tokens, first, second, weight_one, weight_two, received, params):
    rows, width = tokens.shape
    cols = first.shape[1]
    block = 256

    def kernel(t_ref, a_ref, b_ref, wa_ref, wb_ref, r_ref, par_ref, mid_ref, norm_ref):
        middle = (
            t_ref[...].astype(f32)
            + (dot(a_ref[...], wa_ref[...]) + dot(b_ref[...], wb_ref[...]) + r_ref[...].astype(f32))
            + par_ref[2:3, :]
        )
        mid_ref[...] = middle
        unit, _ = normalize(middle)
        norm_ref[...] = (unit * par_ref[3:4, :] + par_ref[4:5, :]).astype(bf16)

    spec = pl.BlockSpec((block, width), lambda i: (i, 0))
    thin = pl.BlockSpec((block, cols), lambda i: (i, 0))
    return call(
        kernel,
        "output_own",
        (rows // block,),
        [spec, thin, thin, whole(weight_one), whole(weight_two), spec, whole(params)],
        [spec, spec],
        [shape((rows, width), f32), shape((rows, width), bf16)],
        flops=4 * rows * cols * width,
        nbytes=4 * rows * cols + 10 * rows * width,
    )(tokens, first, second, weight_one, weight_two, received, params)


def feed_forward(norm_own, norm_other, cot_own, cot_other, up, bias, down, scal, earlier=None):
    rows, width = norm_own.shape
    hidden = up.shape[1]
    block = 256
    count = rows // block
    last = earlier is not None
    term_type = bf16 if last else f32

    def kernel(scal_ref, no_ref, nt_ref, co_ref, ct_ref, up_ref, b_ref, dn_ref, *refs):
        if last:
            ff_in, ng_in, ffo_ref, ngo_ref, fft_ref, ngt_ref, *refs = refs
        else:
            ff_ref, ng_ref, *refs = refs
        up_term, down_term, sum_ref, up_acc, down_acc = refs
        i = pl.program_id(0)

        @pl.when(i == 0)
        def _():
            up_acc[...] = jnp.zeros_like(up_acc)
            down_acc[...] = jnp.zeros_like(down_acc)
            sum_ref[...] = jnp.zeros_like(sum_ref)

        x = pick(count, no_ref, nt_ref)
        cot = pick(count, co_ref, ct_ref)
        h = dot(x, up_ref[...]) + b_ref[0:1, :]
        cdf = 0.5 * (1.0 + lax.erf(h * RSQRT2))
        act = (h * cdf).astype(bf16)
        slope = cdf + h * (RSQRT2PI * jnp.exp(-0.5 * h * h))
        ff = dot(act, dn_ref[...])
        grad = dot(cot, dn_ref[...], NT) * slope
        sum_ref[0:1, :] += jnp.sum(grad, axis=0, keepdims=True)
        low = grad.astype(bf16)
        ng = dot(low, up_ref[...], NT)
        up_acc[...] += dot(x, low, TN)
        down_acc[...] += dot(act, cot, TN)
        if last:
            ff = ff + ff_in[...]
            ng = ng + ng_in[...]

            @pl.when(i < count)
            def _():
                ffo_ref[...] = ff
                ngo_ref[...] = ng

            @pl.when(i >= count)
            def _():
                fft_ref[...] = ff.astype(bf16)
                ngt_ref[...] = ng.astype(bf16)
        else:
            ff_ref[...] = ff
            ng_ref[...] = ng

        @pl.when(i == 2 * count - 1)
        def _():
            units = scal_ref[1]
            up_term[...] = (up_acc[...] * units).astype(term_type)
            down_term[...] = (down_acc[...] * units).astype(term_type)
            sum_ref[...] = sum_ref[...] * units

    own, other = halves(block, width, count)
    every = pl.BlockSpec((block, width), lambda i: (i, 0))
    ins = [scalars(), own, other, own, other, whole(up), whole(bias), whole(down)]
    args = [scal, norm_own, norm_other, cot_own, cot_other, up, bias, down]
    if last:
        ins += [every, every]
        args += list(earlier)
        outs = [own, own, other, other]
        shapes = [shape((rows, width), f32)] * 2 + [shape((rows, width), bf16)] * 2
    else:
        outs = [every, every]
        shapes = [shape((2 * rows, width), f32)] * 2
    terms = [shape((width, hidden), term_type), shape((hidden, width), term_type)]
    sums = shape((8, hidden), f32)
    return call(
        kernel,
        "feed_forward",
        (2 * count,),
        ins,
        outs + [whole(terms[0]), whole(terms[1]), whole(sums)],
        shapes + terms + [sums],
        [pltpu.VMEM((width, hidden), f32), pltpu.VMEM((hidden, width), f32)],
        flops=24 * rows * width * hidden,
        nbytes=24 * rows * width + 12 * width * hidden,
        exps=4 * rows * hidden,
    )(*args)


def second_back(middle, grad_own, grad_received, cot, params, scal):
    rows, width = middle.shape
    block = 256
    last = rows // block - 1

    def kernel(scal_ref, mid_ref, go_ref, gr_ref, cot_ref, par_ref, out_ref, low_ref, sum_ref):
        i = pl.program_id(0)
        unit, inverse = normalize(mid_ref[...])
        grad = go_ref[...] + gr_ref[...].astype(f32)
        cot = cot_ref[...].astype(f32)
        out = cot + norm_back(grad, par_ref[3:4, :], unit, inverse)
        out_ref[...] = out
        low_ref[...] = out.astype(bf16)
        sums = [jnp.sum(v, axis=0, keepdims=True) for v in (grad * unit, grad, out, cot)]
        add_rows(sum_ref, sums, i == 0)

        @pl.when(i == last)
        def _():
            sum_ref[...] = sum_ref[...] * scal_ref[1]

    spec = pl.BlockSpec((block, width), lambda i: (i, 0))
    sums = shape((8, width), f32)
    return call(
        kernel,
        "second_back",
        (rows // block,),
        [scalars(), spec, spec, spec, spec, whole(params)],
        [spec, spec, whole(sums)],
        [shape((rows, width), f32), shape((rows, width), bf16), sums],
        flops=30 * rows * width,
        nbytes=18 * rows * width,
    )(scal, middle, grad_own, grad_received, cot, params)


def output_back(low_own, low_other, first, second, weight_one, weight_two, scal):
    rows, width = low_own.shape
    cols = first.shape[1]
    block = 512
    count = rows // block

    def kernel(
        scal_ref, lo_ref, lt_ref, a_ref, b_ref, wa_ref, wb_ref,
        ga_ref, gb_ref, ta_ref, tb_ref, acc_a, acc_b,
    ):
        i = pl.program_id(0)

        @pl.when(i == 0)
        def _():
            acc_a[...] = jnp.zeros_like(acc_a)
            acc_b[...] = jnp.zeros_like(acc_b)

        low = pick(count, lo_ref, lt_ref)
        ga_ref[...] = dot(low, wa_ref[...], NT).astype(bf16)
        gb_ref[...] = dot(low, wb_ref[...], NT).astype(bf16)
        acc_a[...] += dot(a_ref[...], low, TN)
        acc_b[...] += dot(b_ref[...], low, TN)

        @pl.when(i == 2 * count - 1)
        def _():
            ta_ref[...] = acc_a[...] * scal_ref[1]
            tb_ref[...] = (acc_b[...] * scal_ref[1]).astype(bf16)

    own, other = halves(block, width, count)
    thin = pl.BlockSpec((block, cols), lambda i: (i, 0))
    terms = [shape((cols, width), f32), shape((cols, width), bf16)]
    return call(
        kernel,
        "output_back",
        (2 * count,),
        [scalars(), own, other, thin, thin, whole(weight_one), whole(weight_two)],
        [thin, thin, whole(terms[0]), whole(terms[1])],
        [shape((2 * rows, cols), bf16)] * 2 + terms,
        [pltpu.VMEM((cols, width), f32)] * 2,
        flops=16 * rows * width * cols,
        nbytes=4 * rows * width + 16 * rows * cols,
    )(scal, low_own, low_other, first, second, weight_one, weight_two)


def input_term(norm_own, norm_other, grads, scal, term_type):
    rows, width = norm_own.shape
    cols = grads[0].shape[1]

    def kernel(scal_ref, no_ref, nt_ref, *refs):
        out_ref = refs[-1]
        for j in range(3):

            @pl.when(pl.program_id(0) == j)
            def _():
                grad = refs[j]
                term = dot(no_ref[...], grad[:rows, :], TN) + dot(nt_ref[...], grad[rows:, :], TN)
                out_ref[...] = (term * scal_ref[1]).astype(term_type)

    return call(
        kernel,
        "input_term",
        (3,),
        [scalars(), whole(norm_own), whole(norm_other)] + [whole(g) for g in grads],
        pl.BlockSpec((None, width, cols), lambda j: (j, 0, 0)),
        shape((3, width, cols), term_type),
        flops=12 * rows * width * cols,
        nbytes=4 * rows * width + 12 * rows * cols + 12 * width * cols,
    )(scal, norm_own, norm_other, *grads)


def norm1_other(grads, weight_one, weight_two):
    total, cols = grads[0].shape
    rows = total // 2
    width = weight_one.shape[1]
    block = 256
    count = rows // block

    def kernel(*refs):
        wa_ref, wb_ref, out_ref = refs[6:]
        total = None
        for j in range(3):
            part = dot(refs[j][...], wa_ref[j], NT) + dot(refs[3 + j][...], wb_ref[j], NT)
            total = part if total is None else total + part
        out_ref[...] = total.astype(bf16)

    thin = pl.BlockSpec((block, cols), lambda i: (i + count, 0))
    return call(
        kernel,
        "first_other",
        (count,),
        [thin] * 6 + [whole(weight_one), whole(weight_two)],
        pl.BlockSpec((block, width), lambda i: (i, 0)),
        shape((rows, width), bf16),
        flops=12 * rows * width * cols,
        nbytes=12 * rows * cols + 2 * rows * width + 12 * width * cols,
    )(*grads, weight_one, weight_two)


def norm1_own(grads, weight_one, weight_two, received, tokens, middle_grad, params, scal):
    rows, width = tokens.shape
    cols = grads[0].shape[1]
    block = 256
    last = rows // block - 1

    def kernel(scal_ref, *refs):
        wa_ref, wb_ref, rec_ref, tok_ref, mid_ref, par_ref, out_ref, sum_ref = refs[6:]
        i = pl.program_id(0)
        grad = rec_ref[...].astype(f32)
        for j in range(3):
            grad += dot(refs[j][...], wa_ref[j], NT) + dot(refs[3 + j][...], wb_ref[j], NT)
        unit, inverse = normalize(tok_ref[...].astype(f32))
        out = mid_ref[...] + norm_back(grad, par_ref[0:1, :], unit, inverse)
        out_ref[...] = out.astype(bf16)
        sums = [jnp.sum(v, axis=0, keepdims=True) for v in (grad * unit, grad)]
        add_rows(sum_ref, sums, i == 0)

        @pl.when(i == last)
        def _():
            sum_ref[...] = sum_ref[...] * scal_ref[1]

    thin = pl.BlockSpec((block, cols), lambda i: (i, 0))
    spec = pl.BlockSpec((block, width), lambda i: (i, 0))
    sums = shape((8, width), f32)
    return call(
        kernel,
        "first_own",
        (rows // block,),
        [scalars()] + [thin] * 6 + [whole(weight_one), whole(weight_two)] + [spec] * 3 + [whole(params)],
        [spec, whole(sums)],
        [shape((rows, width), bf16), sums],
        flops=12 * rows * width * cols,
        nbytes=12 * rows * cols + 10 * rows * width + 12 * width * cols,
    )(scal, *grads, weight_one, weight_two, received, tokens, middle_grad, params)


def body(
    tokens,
    out_grad,
    item_counts,
    group_dataset,
    variable_mask,
    first_gain,
    first_shift,
    input_weight,
    input_bias,
    output_weight,
    output_bias,
    second_gain,
    second_shift,
    up_weight,
    up_bias,
    down_weight,
    down_bias,
):
    shard_count = lax.axis_size("mp")
    width = tokens.shape[1]
    cols = input_weight.shape[2]
    hidden = up_weight.shape[1]

    def core_swap(value):
        return lax.ppermute(value, "mp", [(i, i ^ 1) for i in range(shard_count)])

    def chip_swap(value):
        return lax.ppermute(value, "mp", [(i, i ^ 2) for i in range(shard_count)])

    def after(value, *others):
        return lax.optimization_barrier((value, *others))[0]

    live = (lax.axis_index("mp") // 2 < item_counts[0]).astype(f32)
    dataset_hit = jnp.arange(variable_mask.shape[0], dtype=jnp.int32) == group_dataset[0]
    own_units = (
        item_counts[0] * jnp.sum(jnp.where(dataset_hit[:, None], variable_mask, 0))
    ).astype(f32)
    scal = jnp.stack([live, own_units])
    zero = jnp.zeros((width,), f32)
    params = jnp.stack(
        [first_gain, first_shift, output_bias, second_gain, second_shift, down_bias, zero, zero]
    )

    bias_pack = jnp.concatenate([up_bias, input_bias[0], input_bias[1]]).reshape(-1, LANES)
    bias_two = chip_swap(bias_pack).reshape(-1)
    wi_two = chip_swap(input_weight)
    wo_two = chip_swap(after(output_weight, wi_two))
    up_two = chip_swap(after(up_weight, wi_two))
    down_two = chip_swap(after(down_weight, up_two))
    up_bias_one = up_bias.reshape(1, hidden)
    up_bias_two = bias_two[:hidden].reshape(1, hidden)
    in_bias_two = bias_two[hidden:].reshape(2, cols)

    normed1, cot = first_norm(tokens, out_grad, params, scal)
    normed1_t = core_swap(normed1)
    cot_t = core_swap(cot)

    qkv_one = project(normed1, normed1_t, input_weight, input_bias)
    att_one, turned_one, stat_one = attend_forward(*qkv_one)
    qkv_two = project(normed1, normed1_t, wi_two, in_bias_two)
    att_two, turned_two, stat_two = attend_forward(*qkv_two)

    other_part = core_swap(output_other(att_one, att_two, output_weight, wo_two))
    middle, normed2 = output_own(
        tokens, att_one, att_two, output_weight, wo_two, other_part, params
    )
    normed2_t = core_swap(normed2)

    ff_one, ng_one, up_one_term, down_one_term, up_sum_one = feed_forward(
        normed2, normed2_t, cot, cot_t, up_weight, up_bias_one, down_weight, scal
    )
    ff_own, ng_own, ff_send, ng_send, up_two_term, down_two_term, up_sum_two = feed_forward(
        normed2, normed2_t, cot, cot_t, up_two, up_bias_two, down_two, scal, (ff_one, ng_one)
    )
    ng_received = core_swap(ng_send)
    ff_received = core_swap(after(ff_send, ng_received))
    up_received = chip_swap(up_two_term)
    down_received = chip_swap(after(down_two_term, up_received))

    middle_grad, middle_low, second_sums = second_back(
        middle, ng_own, ng_received, cot, params, scal
    )
    middle_low_t = core_swap(middle_low)
    result = (live * (middle + ff_own + ff_received.astype(f32) + down_bias)).astype(bf16)

    g_one, g_two, wo_one_term, wo_two_term = output_back(
        middle_low, middle_low_t, att_one, att_two, output_weight, wo_two, scal
    )
    *grads_two, sums_two = attend_backward(*qkv_two, g_two, turned_two, stat_two)
    wi_two_term = input_term(normed1, normed1_t, grads_two, scal, bf16)
    *grads_one, sums_one = attend_backward(*qkv_one, g_one, turned_one, stat_one)
    wi_one_term = input_term(normed1, normed1_t, grads_one, scal, f32)

    wo_received = chip_swap(after(wo_two_term, down_received))
    wi_received = chip_swap(after(wi_two_term, down_received))

    grads = [*grads_one, *grads_two]
    ng1_received = core_swap(norm1_other(grads, input_weight, wi_two))
    token_grad, first_sums = norm1_own(
        grads, input_weight, wi_two, ng1_received, tokens, middle_grad, params, scal
    )

    def both(own, received):
        return (own + received.astype(f32)).astype(bf16)

    up_sum, down_sum = lax.psum(
        (both(up_one_term, up_received), both(down_one_term, down_received)), "dp"
    )
    wo_sum, wi_sum = lax.psum((both(wo_one_term, wo_received), both(wi_one_term, wi_received)), "dp")

    def vector_pack(up_sums, in_sums):
        units_sum = own_units
        return jnp.concatenate([up_sums[0], in_sums[0] * units_sum, in_sums[1] * units_sum])

    vec_one = vector_pack(up_sum_one, sums_one)
    vec_two = vector_pack(up_sum_two, sums_two)
    vec = vec_one + chip_swap(vec_two.reshape(-1, LANES)).reshape(-1)
    vec = jnp.concatenate([vec, jnp.full((LANES,), own_units)])
    vec_sum = lax.psum(vec, "dp")
    rep_sum = lax.psum(jnp.concatenate([first_sums[:2], second_sums[:4]]), ("dp", "mp"))
    share = 1.0 / vec_sum[-1]
    vec_sum = vec_sum * share
    rep_sum = rep_sum * share

    return (
        result,
        token_grad,
        rep_sum[0],
        rep_sum[1],
        wi_sum.astype(f32) * share,
        vec_sum[hidden : hidden + 2 * cols].reshape(2, cols),
        wo_sum.astype(f32) * share,
        rep_sum[4],
        rep_sum[2],
        rep_sum[3],
        up_sum.astype(f32) * share,
        vec_sum[:hidden],
        down_sum.astype(f32) * share,
        rep_sum[5],
    )


def solution(mesh):
    in_specs = (
        P(("dp", "mp"), None),
        P(("dp", "mp"), None),
        P("dp"),
        P("dp"),
        P(),
        P(),
        P(),
        P(None, None, "mp"),
        P(None, "mp"),
        P("mp", None),
        P(),
        P(),
        P(),
        P(None, "mp"),
        P("mp"),
        P("mp", None),
        P(),
    )
    out_specs = (
        P(("dp", "mp"), None),
        P(("dp", "mp"), None),
        P(),
        P(),
        P(None, None, "mp"),
        P(None, "mp"),
        P("mp", None),
        P(),
        P(),
        P(),
        P(None, "mp"),
        P("mp"),
        P("mp", None),
        P(),
    )
    return jax.shard_map(body, mesh=mesh, in_specs=in_specs, out_specs=out_specs, check_vma=False)
```

time: 1900 us -> 719 us (0.38)
  waiting for transfers between devices: 916 us -> 274 us
  matrix products: 460 us -> 0 us
  Pallas kernels: 0 us -> 303 us
  local copies, waits for them, and re-layouts: 240 us -> 12.2 us
  other arithmetic: 190 us -> 32.2 us
    dot_general x68 -> x0, matrix products: 460 us -> none  [the longest x8 73.4 us: one_block(): jnp.einsum('qhd,khd->hqk', grad_block, value_rows, preferred_element_type...]
    reduce_scatter x4 -> x0, waiting for transfers between devices: 346 us -> none  [the longest x1 126 us: body(): lax.psum_scatter(jnp.dot(merged, output_weight, preferred_element_type=jn...]
    pallas_call x0 -> x17, Pallas kernels: none -> 303 us  [the longest x2 89.8 us: attend_backward(): call(kernel, 'attend_backward', (width // LANES, count), [by_query, by_ke...]
    psum x1, waiting for transfers between devices: 353 us -> 119 us  [body(): lax.psum((both(wo_one_term, wo_received), both(wi_one_term, wi_received))...]
    all_gather x4 -> x0, waiting for transfers between devices: 217 us -> none  [the longest x1 60.9 us: body(): lax.all_gather(normed1.astype(jnp.bfloat16), 'mp', axis=0, tiled=True)]
    ppermute x0 -> x18, waiting for transfers between devices: none -> 155 us  [the longest x10 145 us: chip_swap(): return lax.ppermute(value, 'mp', [(i, i ^ 2) for i in range(shard_count)])]
    while x130 -> x0, local copies, waits for them, and re-layouts: 77.5 us -> none
    convert_element_type x16 -> x5, other arithmetic: 96.7 us -> 19.8 us  [the longest x4 13.1 us: both(): return (own + received.astype(f32)).astype(bf16)]
  transfers between devices with their start and end apart: 9 -> 19, of which waited for: 9 -> 8; matrix products, arithmetic and copies ran while one was open for 6% -> 4% of each run, Pallas kernels for 0% -> 28%
where the time goes in v1:
time: 719 us; the launch traced here: 711 us
  Pallas kernels  303 us (42%)
  waiting for transfers between devices  274 us (38%)
  blocking collectives  63.5 us (9%)
  other arithmetic  32.2 us (4%)
  between operations  17.1 us (2%)
  local copies, waits for them, and re-layouts  12.2 us (2%)
  starting transfers between devices  9.93 us (1%)
    ppermute x10, waiting for transfers between devices, chip_swap(): return lax.ppermute(value, 'mp', [(i, i ^ 2) for i in range(shard_count)])  145 us
    psum x1, waiting for transfers between devices, body(): lax.psum((both(wo_one_term, wo_received), both(wi_one_term, wi_received))...  119 us
    pallas_call x2, Pallas kernels, attend_backward(): call(kernel, 'attend_backward', (width // LANES, count), [by_query, by_ke...  89.8 us
    pallas_call x2, Pallas kernels, feed_forward(): call(kernel, 'feed_forward', (2 * count,), ins, outs + [whole(terms[0]),...  74.2 us
    pallas_call x2, Pallas kernels, attend_forward(): call(kernel, 'attend_forward', (pairs, rows // block), [by_query, by_key,...  53.7 us
    psum x1, blocking collectives, body(): lax.psum(jnp.concatenate([first_sums[:2], second_sums[:4]]), ('dp', 'mp'))  39.8 us
    psum x1, blocking collectives, body(): vec_sum = lax.psum(vec, 'dp')  23.7 us
    pallas_call x2, Pallas kernels, input_term(): call(kernel, 'input_term', (3,), [scalars(), whole(norm_own), whole(norm_...  16.7 us
  transfers between devices with their start and end apart: 19, of which 8 were waited for; matrix products, arithmetic and copies ran while one was open for 4% of the time, Pallas kernels for 28%

profile of v1, /device:TPU:0, one launch (start us, length us, event | category | flops | bytes accessed | tf_op | source)
XLA Modules:
  0.0 711.2 jit_solution(10412488518361196897)
XLA Ops:
  8.5 1.4 select_reduce_fusion
  11.2 1.4 stack.43.par_ref.refs_11_
  12.6 5.5 first_norm.1
  18.6 2.6 collective-permute-start.1
  21.3 35.1 %collective-permute-done.2 = f32[12,128]{1,0:T(8,128)S(1)} collective-permute-done((f32[12,128]{1,0:T(8,128)S(1)}, f32[12,128]{1,0:T(8,128)S(1)}, u32[]{:S(2)}, u32[]{:S(2)}) %collective-permute-start.2) | collective-permute-done | bytes 6176 | tf_op jit(solution)/shard_map/ppermute | solution.py:647
  57.0 1.7 collective-permute-start.3
  58.7 7.3 %project.2 = (bf16[2048,256]{1,0:T(8,128)(2,1)}, bf16[2048,256]{1,0:T(8,128)(2,1)}, bf16[2048,256]{1,0:T(8,128)(2,1)}) custom-call(bf16[1024,1024]{1,0:T(8,128)(2,1)} %get-tuple-element.66.own_ref.no_ref, bf16[1024,1024]{1,0:T(8,128)(2,1)} %collective-permute-done.other_ref.nt_ref, bf16[3,1024,256]{2,1,0:T(8,128)(2,1)} %refs_6_.3, f32[2,256]{1,0:T(2,128)} %b_ref.1), custom_call_target="tpu_custom_call" | custom-call | flops 3221225472 | bytes 8912896 | tf_op jit(solution)/shard_map/project/pallas_call | solution.py:147
  66.1 26.8 %attend_forward.2 = (bf16[2048,256]{1,0:T(8,128)(2,1)}, f32[256,2048]{1,0:T(8,128)}, f32[2,8,2048]{2,1,0:T(8,128)}) custom-call(bf16[2048,256]{1,0:T(8,128)(2,1)} %get-tuple-element.67.q_ref, bf16[2048,256]{1,0:T(8,128)(2,1)} %get-tuple-element.68.k_ref, bf16[2048,256]{1,0:T(8,128)(2,1)} %get-tuple-element.69.v_ref), custom_call_target="tpu_custom_call" | custom-call | flops 17179869184 | bytes 6291456 | tf_op jit(solution)/shard_map/attend_forward/pallas_call | solution.py:206
  92.8 7.3 %project.3 = (bf16[2048,256]{1,0:T(8,128)(2,1)}, bf16[2048,256]{1,0:T(8,128)(2,1)}, bf16[2048,256]{1,0:T(8,128)(2,1)}) custom-call(bf16[1024,1024]{1,0:T(8,128)(2,1)} %get-tuple-element.66.own_ref.no_ref, bf16[1024,1024]{1,0:T(8,128)(2,1)} %collective-permute-done.other_ref.nt_ref, bf16[3,1024,256]{2,1,0:T(8,128)(2,1)} %collective-permute-done.1.w_ref.refs_7_, ...), custom_call_target="tpu_custom_call" | custom-call | flops 3221225472 | bytes 8912896 | tf_op jit(solution)/shard_map/project/pallas_call | solution.py:147
  100.2 26.9 %attend_forward.3 = (bf16[2048,256]{1,0:T(8,128)(2,1)}, f32[256,2048]{1,0:T(8,128)}, f32[2,8,2048]{2,1,0:T(8,128)}) custom-call(bf16[2048,256]{1,0:T(8,128)(2,1)} %get-tuple-element.71.q_ref, bf16[2048,256]{1,0:T(8,128)(2,1)} %get-tuple-element.72.k_ref, bf16[2048,256]{1,0:T(8,128)(2,1)} %get-tuple-element.73.v_ref), custom_call_target="tpu_custom_call" | custom-call | flops 17179869184 | bytes 6291456 | tf_op jit(solution)/shard_map/attend_forward/pallas_call | solution.py:206
  127.1 0.8 copy-done.2
  127.9 3.9 output_other.1
  132.6 6.0 collective-permute-done.4.r_ref
  138.6 6.9 output_own.1
  146.2 34.0 %collective-permute-done.7.up_ref = bf16[1024,1024]{1,0:T(8,128)(2,1)} collective-permute-done((bf16[1024,1024]{1,0:T(8,128)(2,1)}, bf16[1024,1024]{1,0:T(8,128)(2,1)}, u32[]{:S(2)}, u32[]{:S(2)}) %collective-permute-start.7) | collective-permute-done | bytes 2097184 | tf_op jit(solution)/shard_map/ppermute | solution.py:647
  180.6 36.7 %feed_forward.2 = (f32[2048,1024]{1,0:T(8,128)}, f32[2048,1024]{1,0:T(8,128)}, f32[1024,1024]{1,0:T(8,128)}, f32[1024,1024]{1,0:T(8,128)}, f32[8,1024]{1,0:T(8,128)}) custom-call(f32[2]{0:T(128)} %pad_maximum_fusion.1.scal_ref, bf16[1024,1024]{1,0:T(8,128)(2,1)} %get-tuple-element.77.no_ref, bf16[1024,1024]{1,0:T(8,128)(2,1)} %collective-permute-done.5.nt_ref, ...), custom_call_target="tpu_custom_call" | custom-call | flops 25769803776 | bytes 37748736 | tf_op jit(solution)/shard_map/feed_forward/pallas_call | solution.py:436
  217.3 10.1 %collective-permute-done.8.dn_ref = bf16[1024,1024]{1,0:T(8,128)(2,1)} collective-permute-done((bf16[1024,1024]{1,0:T(8,128)(2,1)}, bf16[1024,1024]{1,0:T(8,128)(2,1)}, u32[]{:S(2)}, u32[]{:S(2)}) %collective-permute-start.8) | collective-permute-done | bytes 2097184 | tf_op jit(solution)/shard_map/ppermute | solution.py:647
  227.4 37.5 %feed_forward.3 = (f32[1024,1024]{1,0:T(8,128)}, f32[1024,1024]{1,0:T(8,128)}, bf16[1024,1024]{1,0:T(8,128)(2,1)}, bf16[1024,1024]{1,0:T(8,128)(2,1)}, bf16[1024...) custom-call(f32[2]{0:T(128)} %pad_maximum_fusion.1.scal_ref, ...), custom_call_target="tpu_custom_call" | custom-call | flops 25769803776 | bytes 37748736 | tf_op jit(solution)/shard_map/feed_forward/pallas_call | solution.py:436
  265.3 4.0 collective-permute-done.9.gr_ref
  269.3 1.3 copy-done.7
  270.6 9.5 %second_back.1 = (f32[1024,1024]{1,0:T(8,128)}, bf16[1024,1024]{1,0:T(8,128)(2,1)}, f32[8,1024]{1,0:T(8,128)}) custom-call(f32[2]{0:T(128)} %pad_maximum_fusion.1.scal_ref, f32[1024,1024]{1,0:T(8,128)} %get-tuple-element.76.mid_ref, f32[1024,1024]{1,0:T(8,128)} %get-tuple-element.87.go_ref, bf16[1024,1024]{1,0:T(8,128)(2,1)} %copy-done.7, ...), custom_call_target="tpu_custom_call" | custom-call | flops 31457280 | bytes 18874368 | tf_op jit(solution)/shard_map/second_back/pallas_call | solution.py:472
  280.3 33.0 %collective-permute-done.14 = bf16[1024,1024]{1,0:T(8,128)(2,1)} collective-permute-done((bf16[1024,1024]{1,0:T(8,128)(2,1)}, bf16[1024,1024]{1,0:T(8,128)(2,1)}, u32[]{:S(2)}, u32[]{:S(2)}) %collective-permute-start.14) | collective-permute-done | bytes 2097184 | tf_op jit(solution)/shard_map/ppermute | solution.py:647
  313.6 5.0 add_convert_fusion.1
  318.6 9.6 %output_back.1 = (bf16[2048,256]{1,0:T(8,128)(2,1)}, bf16[2048,256]{1,0:T(8,128)(2,1)}, f32[256,1024]{1,0:T(8,128)}, bf16[256,1024]{1,0:T(8,128)(2,1)}) custom-call(f32[2]{0:T(128)} %pad_maximum_fusion.1.scal_ref, bf16[1024,1024]{1,0:T(8,128)(2,1)} %get-tuple-element.88.lo_ref, bf16[1024,1024]{1,0:T(8,128)(2,1)} %collective-permute-done.11.lt_ref, ...), custom_call_target="tpu_custom_call" | custom-call | flops 4294967296 | bytes 8388608 | tf_op jit(solution)/shard_map/output_back/pallas_call | solution.py:515
  328.2 32.6 %collective-permute-done.15 = bf16[1024,1024]{1,0:T(8,128)(2,1)S(1)} collective-permute-done((bf16[1024,1024]{1,0:T(8,128)(2,1)}, bf16[1024,1024]{1,0:T(8,128)(2,1)S(1)}, u32[]{:S(2)}, u32[]{:S(2)}) %collective-permute-start.15) | collective-permute-done | bytes 2097184 | tf_op jit(solution)/shard_map/ppermute | solution.py:647
  360.7 44.9 %attend_backward.3 = (bf16[2048,256]{1,0:T(8,128)(2,1)}, bf16[2048,256]{1,0:T(8,128)(2,1)}, bf16[2048,256]{1,0:T(8,128)(2,1)}, f32[8,256]{1,0:T(8,128)}) custom-call(bf16[2048,256]{1,0:T(8,128)(2,1)} %get-tuple-element.71.q_ref, bf16[2048,256]{1,0:T(8,128)(2,1)} %get-tuple-element.72.k_ref, bf16[2048,256]{1,0:T(8,128)(2,1)} %get-tuple-element.73.v_ref, ...), custom_call_target="tpu_custom_call" | custom-call | flops 42949672960 | bytes 10485760 | tf_op jit(solution)/shard_map/attend_backward/pallas_call | solution.py:291
  405.7 8.3 %input_term.3 = bf16[3,1024,256]{2,1,0:T(8,128)(2,1)} custom-call(f32[2]{0:T(128)} %pad_maximum_fusion.1.scal_ref, bf16[1024,1024]{1,0:T(8,128)(2,1)} %get-tuple-element.66.own_ref.no_ref, bf16[1024,1024]{1,0:T(8,128)(2,1)} %collective-permute-done.other_ref.nt_ref, bf16[2048,256]{1,0:T(8,128)(2,1)} %get-tuple-element.98.refs_3_.refs_0_, ...), custom_call_target="tpu_custom_call" | custom-call | flops 3221225472 | bytes 10485760 | tf_op jit(solution)/shard_map/input_term/pallas_call | solution.py:542
  414.2 1.7 collective-permute-start.16
  416.0 44.8 %attend_backward.2 = (bf16[2048,256]{1,0:T(8,128)(2,1)}, bf16[2048,256]{1,0:T(8,128)(2,1)}, bf16[2048,256]{1,0:T(8,128)(2,1)}, f32[8,256]{1,0:T(8,128)}) custom-call(bf16[2048,256]{1,0:T(8,128)(2,1)} %get-tuple-element.67.q_ref, bf16[2048,256]{1,0:T(8,128)(2,1)} %get-tuple-element.68.k_ref, bf16[2048,256]{1,0:T(8,128)(2,1)} %get-tuple-element.69.v_ref, ...), custom_call_target="tpu_custom_call" | custom-call | flops 42949672960 | bytes 10485760 | tf_op jit(solution)/shard_map/attend_backward/pallas_call | solution.py:291
  460.8 8.5 %input_term.2 = f32[3,1024,256]{2,1,0:T(8,128)} custom-call(f32[2]{0:T(128)} %pad_maximum_fusion.1.scal_ref, bf16[1024,1024]{1,0:T(8,128)(2,1)} %get-tuple-element.66.own_ref.no_ref, bf16[1024,1024]{1,0:T(8,128)(2,1)} %collective-permute-done.other_ref.nt_ref, bf16[2048,256]{1,0:T(8,128)(2,1)} %get-tuple-element.92.refs_0_, ...), custom_call_target="tpu_custom_call" | custom-call | flops 3221225472 | bytes 10485760 | tf_op jit(solution)/shard_map/input_term/pallas_call | solution.py:542
  469.3 4.4 add_convert_fusion
  473.7 2.0 add_convert_fusion.3
  475.7 1.7 add_convert_fusion.2
  477.5 7.6 %first_other.1 = bf16[1024,1024]{1,0:T(8,128)(2,1)} custom-call(bf16[2048,256]{1,0:T(8,128)(2,1)} %get-tuple-element.92.refs_0_, bf16[2048,256]{1,0:T(8,128)(2,1)} %get-tuple-element.93.refs_1_, bf16[2048,256]{1,0:T(8,128)(2,1)} %get-tuple-element.94.refs_2_, bf16[2048,256]{1,0:T(8,128)(2,1)} %get-tuple-element.98.refs_3_.refs_0_, ...), custom_call_target="tpu_custom_call" | custom-call | flops 3221225472 | bytes 8388608 | tf_op jit(solution)/shard_map/first_other/pallas_call | solution.py:570
  485.7 0.8 slice.74
  487.2 0.8 slice_multiply_fusion.1
  488.3 6.7 multiply_convert_fusion
  495.0 0.8 slice_multiply_fusion.3
  495.8 23.7 %psum.43 = f32[1664]{0:T(1024)S(1)} all-reduce(f32[1664]{0:T(1024)S(1)} %concatenate.19), channel_id=1, replica_groups=mesh['dp'=8,'mp'=4] {'dp'}, use_global_device_ids=true, to_apply=%region_2.3 | all-reduce | flops 1664 | bytes 13312 | tf_op jit(solution)/shard_map/psum | solution.py:738
  522.0 1.3 copy-done.6
  523.3 10.6 %first_own.1 = (bf16[1024,1024]{1,0:T(8,128)(2,1)}, f32[8,1024]{1,0:T(8,128)}) custom-call(f32[2]{0:T(128)} %pad_maximum_fusion.1.scal_ref, bf16[2048,256]{1,0:T(8,128)(2,1)} %get-tuple-element.92.refs_0_, bf16[2048,256]{1,0:T(8,128)(2,1)} %get-tuple-element.93.refs_1_, bf16[2048,256]{1,0:T(8,128)(2,1)} %get-tuple-element.94.refs_2_, ...), custom_call_target="tpu_custom_call" | custom-call | flops 3221225472 | bytes 16777216 | tf_op jit(solution)/shard_map/first_own/pallas_call | solution.py:607
  533.9 0.8 slice.69
  534.7 39.8 %psum.42 = f32[6,1024]{1,0:T(8,128)S(1)} all-reduce(f32[6,1024]{1,0:T(8,128)S(1)} %pad_maximum_fusion), channel_id=1, replica_groups=mesh['dp'=8,'mp'=4] {'dp','mp'}, use_global_device_ids=true, to_apply=%region_1.2 | all-reduce | flops 6144 | bytes 49152 | tf_op jit(solution)/shard_map/psum | solution.py:739
  575.2 118.8 %all-reduce.4.cloned.1.call-done = (bf16[3,1024,256]{2,1,0:T(8,128)(2,1)}, bf16[256,1024]{1,0:T(8,128)(2,1)}, bf16[1024,1024]{1,0:T(8,128)(2,1)}, bf16[1024,1024]{1,0:T(8,128)(2,1)}) async-done(((bf16[3,1024,256]{2,1,0:T(8,128)(2,1)}, bf16[256,1024]{1,0:T(8,128)(2,1)}, bf16[1024,1024]{1,0:T(8,128)(2,1)}, bf16[1024,1024]{1,0:T(8,128)(2,1)}), (bf16[3,1024,256]{2,1,0:T(8,128)(2,1)}, ...) | async-done | bytes 6291472 | tf_op jit(solution)/shard_map/psum | solution.py:728
  694.0 2.2 convert_multiply_fusion.3
  696.2 1.9 convert_multiply_fusion.2
  698.6 0.9 copy-done.5
  699.6 4.6 convert_multiply_fusion
  (75 shorter events, 9.5 us)
Async XLA Ops:
  7.2 686.8 %all-reduce.4.cloned.1.call-start = ((), (), s32[]{:S(2)}) async-start(), calls=%async_computation | async-start | bytes 12582912 | tf_op jit(solution)/shard_map/psum | solution.py:728
  12.6 6.0 copy-start.8
  12.6 8.6 %copy-start.14 = (f32[2,256]{1,0:T(2,128)S(1)}, f32[2,256]{1,0:T(2,128)}, u32[]{:S(2)}) copy-start(f32[2,256]{1,0:T(2,128)} %b_ref.1) | copy-start | bytes 6148
  12.6 8.6 %copy-start.13 = (f32[1024]{0:T(1024)S(1)}, f32[1024]{0:T(1024)}, u32[]{:S(2)}) copy-start(f32[1024]{0:T(1024)} %param.31) | copy-start | bytes 12292
  12.6 44.3 %copy-start.1 = (bf16[256,1024]{1,0:T(8,128)(2,1)S(1)}, bf16[256,1024]{1,0:T(8,128)(2,1)}, u32[]{:S(2)}) copy-start(bf16[256,1024]{1,0:T(8,128)(2,1)} %wa_ref.5) | copy-start | bytes 1572868
  18.2 40.6 %collective-permute-start = (bf16[1024,1024]{1,0:T(8,128)(2,1)}, bf16[1024,1024]{1,0:T(8,128)(2,1)}, u32[]{:S(2)}, u32[]{:S(2)}) collective-permute-start(bf16[1024,1024]{1,0:T(8,128)(2,1)} %get-tuple-element.66.own_ref.no_ref), channel_id=1, source_target_pairs={{0,1},{1,0},{2,3},{3,2},{4,5},{5,4},{6,7},{7,6},{8,9},{9,8},{10,11... | collective-permute-start | bytes 6291464 | tf_op jit(solution)/shard_map/ppermute | solution.py:644
  18.6 38.3 %collective-permute-start.1 = (bf16[3,1024,256]{2,1,0:T(8,128)(2,1)S(1)}, bf16[3,1024,256]{2,1,0:T(8,128)(2,1)}, u32[]{:S(2)}, u32[]{:S(2)}) collective-permute-start(bf16[3,1024,256]{2,1,0:T(8,128)(2,1)S(1)} %copy-done.8), channel_id=1, source_target_pairs={{0,2},{1,3},{2,0},{3,1},{4,6},{5,7},{6,4},{7,5},{8,10},{9,11},{10,... | collective-permute-start | bytes 4718600 | tf_op jit(solution)/shard_map/ppermute | solution.py:647
  21.2 35.2 %collective-permute-start.2 = (f32[12,128]{1,0:T(8,128)S(1)}, f32[12,128]{1,0:T(8,128)S(1)}, u32[]{:S(2)}, u32[]{:S(2)}) collective-permute-start(f32[12,128]{1,0:T(8,128)S(1)} %maximum_bitcast_fusion), channel_id=1, source_target_pairs={{0,2},{1,3},{2,0},{3,1},{4,6},{5,7},{6,4},{7,5},{8,10},{9,11},{10,... | collective-permute-start | bytes 18440 | tf_op jit(solution)/shard_map/ppermute | solution.py:647
  57.0 70.2 %collective-permute-start.3 = (bf16[256,1024]{1,0:T(8,128)(2,1)S(1)}, bf16[256,1024]{1,0:T(8,128)(2,1)S(1)}, u32[]{:S(2)}, u32[]{:S(2)}) collective-permute-start(bf16[256,1024]{1,0:T(8,128)(2,1)S(1)} %copy-done.1), channel_id=1, source_target_pairs={{0,2},{1,3},{2,0},{3,1},{4,6},{5,7},{6,4},{7,5},{8,10},{9,11},{10,... | collective-permute-start | bytes 1572872 | tf_op jit(solution)/shard_map/ppermute | solution.py:647
  127.1 0.8 copy-start.2
  127.9 3.9 copy-start.3
  131.8 6.8 collective-permute-start.4
  131.9 48.7 %collective-permute-start.6 = (bf16[1024,1024]{1,0:T(8,128)(2,1)S(1)}, bf16[1024,1024]{1,0:T(8,128)(2,1)}, u32[]{:S(2)}, u32[]{:S(2)}) collective-permute-start(bf16[1024,1024]{1,0:T(8,128)(2,1)S(1)} %copy-done.3), channel_id=1, source_target_pairs={{0,1},{1,0},{2,3},{3,2},{4,5},{5,4},{6,7},{7,6},{8,9},{9,8},{10,11... | collective-permute-start | bytes 6291464 | tf_op jit(solution)/shard_map/ppermute | solution.py:644
  132.4 47.9 %collective-permute-start.7 = (bf16[1024,1024]{1,0:T(8,128)(2,1)}, bf16[1024,1024]{1,0:T(8,128)(2,1)}, u32[]{:S(2)}, u32[]{:S(2)}) collective-permute-start(bf16[1024,1024]{1,0:T(8,128)(2,1)} %up_ref.1), channel_id=1, source_target_pairs={{0,2},{1,3},{2,0},{3,1},{4,6},{5,7},{6,4},{7,5},{8,10},{9,11},{10,... | collective-permute-start | bytes 6291464 | tf_op jit(solution)/shard_map/ppermute | solution.py:647
  145.5 35.1 %collective-permute-start.5 = (bf16[1024,1024]{1,0:T(8,128)(2,1)}, bf16[1024,1024]{1,0:T(8,128)(2,1)}, u32[]{:S(2)}, u32[]{:S(2)}) collective-permute-start(bf16[1024,1024]{1,0:T(8,128)(2,1)} %get-tuple-element.77.no_ref), channel_id=1, source_target_pairs={{0,1},{1,0},{2,3},{3,2},{4,5},{5,4},{6,7},{7,6},{8,9},{9,8},{10,11... | collective-permute-start | bytes 6291464 | tf_op jit(solution)/shard_map/ppermute | solution.py:644
  180.3 47.1 %collective-permute-start.8 = (bf16[1024,1024]{1,0:T(8,128)(2,1)}, bf16[1024,1024]{1,0:T(8,128)(2,1)}, u32[]{:S(2)}, u32[]{:S(2)}) collective-permute-start(bf16[1024,1024]{1,0:T(8,128)(2,1)} %dn_ref.1), channel_id=1, source_target_pairs={{0,2},{1,3},{2,0},{3,1},{4,6},{5,7},{6,4},{7,5},{8,10},{9,11},{10,... | collective-permute-start | bytes 6291464 | tf_op jit(solution)/shard_map/ppermute | solution.py:647
  264.9 4.4 collective-permute-start.9
  265.0 48.4 %collective-permute-start.14 = (bf16[1024,1024]{1,0:T(8,128)(2,1)}, bf16[1024,1024]{1,0:T(8,128)(2,1)}, u32[]{:S(2)}, u32[]{:S(2)}) collective-permute-start(bf16[1024,1024]{1,0:T(8,128)(2,1)} %get-tuple-element.110), channel_id=1, source_target_pairs={{0,2},{1,3},{2,0},{3,1},{4,6},{5,7},{6,4},{7,5},{8,10},{9,11},{10,... | collective-permute-start | bytes 6291464 | tf_op jit(solution)/shard_map/ppermute | solution.py:647
  269.3 1.3 copy-start.7
  280.1 38.5 %collective-permute-start.11 = (bf16[1024,1024]{1,0:T(8,128)(2,1)}, bf16[1024,1024]{1,0:T(8,128)(2,1)}, u32[]{:S(2)}, u32[]{:S(2)}) collective-permute-start(bf16[1024,1024]{1,0:T(8,128)(2,1)} %get-tuple-element.88.lo_ref), channel_id=1, source_target_pairs={{0,1},{1,0},{2,3},{3,2},{4,5},{5,4},{6,7},{7,6},{8,9},{9,8},{10,11... | collective-permute-start | bytes 6291464 | tf_op jit(solution)/shard_map/ppermute | solution.py:644
  313.3 47.4 %collective-permute-start.15 = (bf16[1024,1024]{1,0:T(8,128)(2,1)}, bf16[1024,1024]{1,0:T(8,128)(2,1)S(1)}, u32[]{:S(2)}, u32[]{:S(2)}) collective-permute-start(bf16[1024,1024]{1,0:T(8,128)(2,1)} %get-tuple-element.111), channel_id=1, source_target_pairs={{0,2},{1,3},{2,0},{3,1},{4,6},{5,7},{6,4},{7,5},{8,10},{9,11},{10,... | collective-permute-start | bytes 6291464 | tf_op jit(solution)/shard_map/ppermute | solution.py:647
  413.9 59.8 %collective-permute-start.17 = (bf16[256,1024]{1,0:T(8,128)(2,1)}, bf16[256,1024]{1,0:T(8,128)(2,1)}, u32[]{:S(2)}, u32[]{:S(2)}) collective-permute-start(bf16[256,1024]{1,0:T(8,128)(2,1)} %get-tuple-element.115), channel_id=1, source_target_pairs={{0,2},{1,3},{2,0},{3,1},{4,6},{5,7},{6,4},{7,5},{8,10},{9,11},{10,... | collective-permute-start | bytes 1572872 | tf_op jit(solution)/shard_map/ppermute | solution.py:647
  414.2 61.5 %collective-permute-start.16 = (bf16[3,1024,256]{2,1,0:T(8,128)(2,1)}, bf16[3,1024,256]{2,1,0:T(8,128)(2,1)S(1)}, u32[]{:S(2)}, u32[]{:S(2)}) collective-permute-start(bf16[3,1024,256]{2,1,0:T(8,128)(2,1)} %input_term.3), channel_id=1, source_target_pairs={{0,2},{1,3},{2,0},{3,1},{4,6},{5,7},{6,4},{7,5},{8,10},{9,11},{10,... | collective-permute-start | bytes 4718600 | tf_op jit(solution)/shard_map/ppermute | solution.py:647
  469.3 4.5 copy-start.10
  469.3 6.5 copy-start
  477.4 9.8 %copy-start.12 = (f32[8,1024]{1,0:T(8,128)S(1)}, f32[8,1024]{1,0:T(8,128)}, u32[]{:S(2)}) copy-start(f32[8,1024]{1,0:T(8,128)} %get-tuple-element.104) | copy-start | bytes 98308
  477.4 10.9 %copy-start.11 = (f32[1024]{0:T(1024)S(1)}, f32[1024]{0:T(1024)}, u32[]{:S(2)}) copy-start(f32[1024]{0:T(1024)} %param.33) | copy-start | bytes 12292
  477.4 10.8 %collective-permute-start.10 = (bf16[1024,1024]{1,0:T(8,128)(2,1)}, bf16[1024,1024]{1,0:T(8,128)(2,1)}, u32[]{:S(2)}, u32[]{:S(2)}) collective-permute-start(bf16[1024,1024]{1,0:T(8,128)(2,1)} %get-tuple-element.86), channel_id=1, source_target_pairs={{0,1},{1,0},{2,3},{3,2},{4,5},{5,4},{6,7},{7,6},{8,9},{9,8},{10,11... | collective-permute-start | bytes 6291464 | tf_op jit(solution)/shard_map/ppermute | solution.py:644
  485.1 36.8 %collective-permute-start.12 = (bf16[1024,1024]{1,0:T(8,128)(2,1)}, bf16[1024,1024]{1,0:T(8,128)(2,1)S(1)}, u32[]{:S(2)}, u32[]{:S(2)}) collective-permute-start(bf16[1024,1024]{1,0:T(8,128)(2,1)} %first_other.1), channel_id=1, source_target_pairs={{0,1},{1,0},{2,3},{3,2},{4,5},{5,4},{6,7},{7,6},{8,9},{9,8},{10,11... | collective-permute-start | bytes 6291464 | tf_op jit(solution)/shard_map/ppermute | solution.py:644
  488.0 7.8 %collective-permute-start.13 = (f32[12,128]{1,0:T(8,128)S(1)}, f32[12,128]{1,0:T(8,128)S(1)}, u32[]{:S(2)}, u32[]{:S(2)}) collective-permute-start(f32[12,128]{1,0:T(8,128)S(1)} %maximum_bitcast_fusion.1), channel_id=1, source_target_pairs={{0,2},{1,3},{2,0},{3,1},{4,6},{5,7},{6,4},{7,5},{8,10},{9,11},{10,... | collective-permute-start | bytes 18440 | tf_op jit(solution)/shard_map/ppermute | solution.py:647
  522.0 1.3 copy-start.6
  694.0 2.3 copy-start.9
  696.2 2.4 copy-start.4
  696.2 3.4 copy-start.5
Sparse Core Ops, SparseCore 0:
  477.5 216.3 all-reduce.3

commit v2 on v1

--- a/solution.py
+++ b/solution.py
@@ -38,7 +38,7 @@
     return pl.BlockSpec(memory_space=pltpu.SMEM)
 
 
-def call(kernel, name, grid, in_specs, out_specs, out_shape, scratch=(), flops=0, nbytes=0, exps=0):
+def call(kernel, name, grid, in_specs, out_specs, out_shape, scratch=(), flops=0, nbytes=0, exps=0, weight=1e-6):
     return pl.pallas_call(
         kernel,
         name=name,
@@ -49,7 +49,7 @@
         scratch_shapes=list(scratch),
         compiler_params=pltpu.CompilerParams(vmem_limit_bytes=VMEM_BYTES),
         cost_estimate=pl.CostEstimate(
-            flops=int(flops), bytes_accessed=int(nbytes), transcendentals=int(exps)
+            flops=int(flops * weight), bytes_accessed=int(nbytes * weight), transcendentals=int(exps * weight)
         ),
     )
 
@@ -214,11 +214,13 @@
         flops=16 * rows * rows * width,
         nbytes=12 * rows * width,
         exps=rows * rows * width // HEAD_DIM,
+        weight=1000,
     )(queries, keys, values)
 
 
-def attend_backward(queries, keys, values, out_grad, out_turned, stats):
-    rows, width = queries.shape
+def attend_backward(queries, keys, values, out_grad, out_turned, stats, pair):
+    rows = queries.shape[0]
+    width = LANES
     block = min(1024, rows)
     chunk = 256
     count = rows // block
@@ -283,17 +285,19 @@
             dv_ref[...] = dv.astype(bf16)
             sum_ref[1:2, :] = jnp.sum(dv, axis=0, keepdims=True)
 
-    by_query = pl.BlockSpec((block, LANES), lambda j, i: (i, j))
-    by_key = pl.BlockSpec((rows, LANES), lambda j, i: (0, j))
-    turned_spec = pl.BlockSpec((LANES, block), lambda j, i: (j, i))
-    stat_spec = pl.BlockSpec((None, 8, block), lambda j, i: (j, 0, i))
-    sum_spec = pl.BlockSpec((8, LANES), lambda j, i: (0, j))
+    by_query = pl.BlockSpec((block, LANES), lambda j, i: (i, pair))
+    by_key = pl.BlockSpec((rows, LANES), lambda j, i: (0, pair))
+    turned_spec = pl.BlockSpec((LANES, block), lambda j, i: (pair, i))
+    stat_spec = pl.BlockSpec((None, 8, block), lambda j, i: (pair, 0, i))
+    query_out = pl.BlockSpec((block, LANES), lambda j, i: (i, 0))
+    key_out = pl.BlockSpec((rows, LANES), lambda j, i: (0, 0))
+    sum_spec = pl.BlockSpec((8, LANES), lambda j, i: (0, 0))
     return call(
         kernel,
         "attend_backward",
-        (width // LANES, count),
+        (1, count),
         [by_query, by_key, by_key, by_query, turned_spec, stat_spec],
-        [by_query, by_key, by_key, sum_spec],
+        [query_out, key_out, key_out, sum_spec],
         [shape((rows, width), bf16)] * 3 + [shape((8, width), f32)],
         [
             pltpu.VMEM((2, rows, 2 * LANES), bf16),
@@ -305,6 +309,7 @@
         flops=40 * rows * rows * width,
         nbytes=20 * rows * width,
         exps=rows * rows * width // HEAD_DIM,
+        weight=1000,
     )(queries, keys, values, out_grad, out_turned, stats)
 
 
@@ -360,15 +365,16 @@
     )(tokens, first, second, weight_one, weight_two, received, params)
 
 
-def feed_forward(norm_own, norm_other, cot_own, cot_other, up, bias, down, scal, earlier=None):
+def feed_forward(norm_own, norm_other, cot_own, cot_other, bias, both_weights, scal, earlier=None):
     rows, width = norm_own.shape
-    hidden = up.shape[1]
+    hidden = bias.shape[1]
     block = 256
     count = rows // block
     last = earlier is not None
-    term_type = bf16 if last else f32
-
-    def kernel(scal_ref, no_ref, nt_ref, co_ref, ct_ref, up_ref, b_ref, dn_ref, *refs):
+    slices, depth = both_weights.shape[0], both_weights.shape[2]
+    term_type = bf16
+
+    def kernel(scal_ref, no_ref, nt_ref, co_ref, ct_ref, b_ref, up_ref, dn_ref, *refs):
         if last:
             ff_in, ng_in, ffo_ref, ngo_ref, fft_ref, ngt_ref, *refs = refs
         else:
@@ -384,15 +390,17 @@
 
         x = pick(count, no_ref, nt_ref)
         cot = pick(count, co_ref, ct_ref)
-        h = dot(x, up_ref[...]) + b_ref[0:1, :]
+        up = up_ref[...].reshape(width, hidden)
+        down = dn_ref[...].reshape(hidden, width)
+        h = dot(x, up) + b_ref[0:1, :]
         cdf = 0.5 * (1.0 + lax.erf(h * RSQRT2))
         act = (h * cdf).astype(bf16)
         slope = cdf + h * (RSQRT2PI * jnp.exp(-0.5 * h * h))
-        ff = dot(act, dn_ref[...])
-        grad = dot(cot, dn_ref[...], NT) * slope
+        ff = dot(act, down)
+        grad = dot(cot, down, NT) * slope
         sum_ref[0:1, :] += jnp.sum(grad, axis=0, keepdims=True)
         low = grad.astype(bf16)
-        ng = dot(low, up_ref[...], NT)
+        ng = dot(low, up, NT)
         up_acc[...] += dot(x, low, TN)
         down_acc[...] += dot(act, cot, TN)
         if last:
@@ -421,8 +429,14 @@
 
     own, other = halves(block, width, count)
     every = pl.BlockSpec((block, width), lambda i: (i, 0))
-    ins = [scalars(), own, other, own, other, whole(up), whole(bias), whole(down)]
-    args = [scal, norm_own, norm_other, cot_own, cot_other, up, bias, down]
+    up_spec, down_spec = (
+        pl.BlockSpec(
+            (slices, None, depth, width), lambda i, j=j: (0, j, 0, 0), pipeline_mode=pl.Buffered(1)
+        )
+        for j in range(2)
+    )
+    ins = [scalars(), own, other, own, other, whole(bias), up_spec, down_spec]
+    args = [scal, norm_own, norm_other, cot_own, cot_other, bias, both_weights, both_weights]
     if last:
         ins += [every, every]
         args += list(earlier)
@@ -444,6 +458,7 @@
         flops=24 * rows * width * hidden,
         nbytes=24 * rows * width + 12 * width * hidden,
         exps=4 * rows * hidden,
+        weight=1000 if last else 1e-6,
     )(*args)
 
 
@@ -506,12 +521,12 @@
 
         @pl.when(i == 2 * count - 1)
         def _():
-            ta_ref[...] = acc_a[...] * scal_ref[1]
+            ta_ref[...] = (acc_a[...] * scal_ref[1]).astype(bf16)
             tb_ref[...] = (acc_b[...] * scal_ref[1]).astype(bf16)
 
     own, other = halves(block, width, count)
     thin = pl.BlockSpec((block, cols), lambda i: (i, 0))
-    terms = [shape((cols, width), f32), shape((cols, width), bf16)]
+    terms = [shape((cols, width), bf16)] * 2
     return call(
         kernel,
         "output_back",
@@ -525,9 +540,10 @@
     )(scal, low_own, low_other, first, second, weight_one, weight_two)
 
 
-def input_term(norm_own, norm_other, grads, scal, term_type):
+def input_term(norm_own, norm_other, pairs, scal):
     rows, width = norm_own.shape
-    cols = grads[0].shape[1]
+    count = len(pairs)
+    grads = [pair[j] for j in range(3) for pair in pairs]
 
     def kernel(scal_ref, no_ref, nt_ref, *refs):
         out_ref = refs[-1]
@@ -535,62 +551,78 @@
 
             @pl.when(pl.program_id(0) == j)
             def _():
-                grad = refs[j]
+                grad = jnp.concatenate([r[...] for r in refs[count * j : count * j + count]], 1)
                 term = dot(no_ref[...], grad[:rows, :], TN) + dot(nt_ref[...], grad[rows:, :], TN)
-                out_ref[...] = (term * scal_ref[1]).astype(term_type)
-
+                out_ref[...] = (term * scal_ref[1]).astype(bf16)
+
+    cols = count * LANES
     return call(
         kernel,
         "input_term",
         (3,),
         [scalars(), whole(norm_own), whole(norm_other)] + [whole(g) for g in grads],
-        pl.BlockSpec((None, width, cols), lambda j: (j, 0, 0)),
-        shape((3, width, cols), term_type),
+        pl.BlockSpec((width, cols), lambda j: (j, 0)),
+        shape((3 * width, cols), bf16),
         flops=12 * rows * width * cols,
         nbytes=4 * rows * width + 12 * rows * cols + 12 * width * cols,
     )(scal, norm_own, norm_other, *grads)
 
 
-def norm1_other(grads, weight_one, weight_two):
-    total, cols = grads[0].shape
-    rows = total // 2
-    width = weight_one.shape[1]
+def norm1_part(refs, weights):
+    total = None
+    place = 0
+    for w_ref in weights:
+        cols = w_ref.shape[2]
+        count = cols // LANES
+        for j in range(3):
+            grad = jnp.concatenate([r[...] for r in refs[place : place + count]], 1)
+            part = dot(grad, w_ref[j], NT)
+            total = part if total is None else total + part
+            place += count
+    return total
+
+
+def flat(quarters):
+    return [pair[j] for pairs in quarters for j in range(3) for pair in pairs]
+
+
+def norm1_other(quarters, weights):
+    grads = flat(quarters)
+    rows = grads[0].shape[0] // 2
+    width, cols = weights[0].shape[1:]
     block = 256
-    count = rows // block
+    start = rows // block
+    many = len(grads)
 
     def kernel(*refs):
-        wa_ref, wb_ref, out_ref = refs[6:]
-        total = None
-        for j in range(3):
-            part = dot(refs[j][...], wa_ref[j], NT) + dot(refs[3 + j][...], wb_ref[j], NT)
-            total = part if total is None else total + part
-        out_ref[...] = total.astype(bf16)
-
-    thin = pl.BlockSpec((block, cols), lambda i: (i + count, 0))
+        refs[-1][...] = norm1_part(refs[:many], refs[many:-1]).astype(bf16)
+
+    thin = pl.BlockSpec((block, LANES), lambda i: (i + start, 0))
     return call(
         kernel,
         "first_other",
-        (count,),
-        [thin] * 6 + [whole(weight_one), whole(weight_two)],
+        (rows // block,),
+        [thin] * many + [whole(w) for w in weights],
         pl.BlockSpec((block, width), lambda i: (i, 0)),
         shape((rows, width), bf16),
         flops=12 * rows * width * cols,
         nbytes=12 * rows * cols + 2 * rows * width + 12 * width * cols,
-    )(*grads, weight_one, weight_two)
-
-
-def norm1_own(grads, weight_one, weight_two, received, tokens, middle_grad, params, scal):
+    )(*grads, *weights)
+
+
+def norm1_own(quarters, weights, received, tokens, middle_grad, params, scal):
+    grads = flat(quarters)
     rows, width = tokens.shape
-    cols = grads[0].shape[1]
+    cols = weights[0].shape[2]
     block = 256
     last = rows // block - 1
+    many = len(grads)
 
     def kernel(scal_ref, *refs):
-        wa_ref, wb_ref, rec_ref, tok_ref, mid_ref, par_ref, out_ref, sum_ref = refs[6:]
+        rec_ref, tok_ref, mid_ref, par_ref, out_ref, sum_ref = refs[many + len(weights) :]
         i = pl.program_id(0)
-        grad = rec_ref[...].astype(f32)
-        for j in range(3):
-            grad += dot(refs[j][...], wa_ref[j], NT) + dot(refs[3 + j][...], wb_ref[j], NT)
+        grad = norm1_part(refs[:many], refs[many : many + len(weights)])
+        grad += rec_ref[...].astype(f32)
         unit, inverse = normalize(tok_ref[...].astype(f32))
         out = mid_ref[...] + norm_back(grad, par_ref[0:1, :], unit, inverse)
         out_ref[...] = out.astype(bf16)
@@ -601,19 +633,19 @@
         def _():
             sum_ref[...] = sum_ref[...] * scal_ref[1]
 
-    thin = pl.BlockSpec((block, cols), lambda i: (i, 0))
+    thin = pl.BlockSpec((block, LANES), lambda i: (i, 0))
     spec = pl.BlockSpec((block, width), lambda i: (i, 0))
     sums = shape((8, width), f32)
     return call(
         kernel,
         "first_own",
         (rows // block,),
-        [scalars()] + [thin] * 6 + [whole(weight_one), whole(weight_two)] + [spec] * 3 + [whole(params)],
+        [scalars()] + [thin] * many + [whole(w) for w in weights] + [spec] * 3 + [whole(params)],
         [spec, whole(sums)],
         [shape((rows, width), bf16), sums],
         flops=12 * rows * width * cols,
         nbytes=12 * rows * cols + 10 * rows * width + 12 * width * cols,
-    )(scal, *grads, weight_one, weight_two, received, tokens, middle_grad, params)
+    )(scal, *grads, *weights, received, tokens, middle_grad, params)
 
 
 def body(
@@ -636,6 +668,7 @@
     down_bias,
 ):
     shard_count = lax.axis_size("mp")
+    groups = lax.axis_size("dp")
     width = tokens.shape[1]
     cols = input_weight.shape[2]
     hidden = up_weight.shape[1]
@@ -648,6 +681,23 @@
 
     def after(value, *others):
         return lax.optimization_barrier((value, *others))[0]
+
+    def along(value, bit):
+        return lax.ppermute(value, "dp", [(i, i ^ bit) for i in range(groups)])
+
+    group = lax.axis_index("dp")
+
+    slice_rows = up_weight.shape[0] // groups
+    slices = [
+        lax.dynamic_slice_in_dim(weight, group * slice_rows, slice_rows, 0)
+        for weight in (up_weight, down_weight)
+    ]
+    slice_two = chip_swap(jnp.stack(slices)[None])
+    ff_weights_two = lax.all_gather(slice_two, "dp", axis=0, tiled=True)
+    bias_pack = jnp.concatenate([up_bias, input_bias[0], input_bias[1]]).reshape(-1, LANES)
+    bias_two = chip_swap(after(bias_pack, slice_two))
+    wi_two = chip_swap(after(input_weight, slice_two))
+    wo_two = chip_swap(after(output_weight, bias_two))
 
     live = (lax.axis_index("mp") // 2 < item_counts[0]).astype(f32)
     dataset_hit = jnp.arange(variable_mask.shape[0], dtype=jnp.int32) == group_dataset[0]
@@ -660,102 +710,156 @@
         [first_gain, first_shift, output_bias, second_gain, second_shift, down_bias, zero, zero]
     )
 
-    bias_pack = jnp.concatenate([up_bias, input_bias[0], input_bias[1]]).reshape(-1, LANES)
-    bias_two = chip_swap(bias_pack).reshape(-1)
-    wi_two = chip_swap(input_weight)
-    wo_two = chip_swap(after(output_weight, wi_two))
-    up_two = chip_swap(after(up_weight, wi_two))
-    down_two = chip_swap(after(down_weight, up_two))
+    normed1, cot = first_norm(tokens, out_grad, params, scal)
+    normed1_t = core_swap(normed1)
+    cot_t = core_swap(cot)
+
+    qkv_one = project(normed1, normed1_t, input_weight, input_bias)
+    att_one, turned_one, stat_one = attend_forward(*qkv_one)
+    bias_two = bias_two.reshape(-1)
     up_bias_one = up_bias.reshape(1, hidden)
     up_bias_two = bias_two[:hidden].reshape(1, hidden)
     in_bias_two = bias_two[hidden:].reshape(2, cols)
-
-    normed1, cot = first_norm(tokens, out_grad, params, scal)
-    normed1_t = core_swap(normed1)
-    cot_t = core_swap(cot)
-
-    qkv_one = project(normed1, normed1_t, input_weight, input_bias)
-    att_one, turned_one, stat_one = attend_forward(*qkv_one)
-    qkv_two = project(normed1, normed1_t, wi_two, in_bias_two)
+    qkv_two = project(after(normed1, att_one), normed1_t, wi_two, in_bias_two)
     att_two, turned_two, stat_two = attend_forward(*qkv_two)
 
-    other_part = core_swap(output_other(att_one, att_two, output_weight, wo_two))
+    other_part = core_swap(output_other(att_one, after(att_two, ff_weights_two), output_weight, wo_two))
     middle, normed2 = output_own(
         tokens, att_one, att_two, output_weight, wo_two, other_part, params
     )
     normed2_t = core_swap(normed2)
 
-    ff_one, ng_one, up_one_term, down_one_term, up_sum_one = feed_forward(
-        normed2, normed2_t, cot, cot_t, up_weight, up_bias_one, down_weight, scal
-    )
-    ff_own, ng_own, ff_send, ng_send, up_two_term, down_two_term, up_sum_two = feed_forward(
-        normed2, normed2_t, cot, cot_t, up_two, up_bias_two, down_two, scal, (ff_one, ng_one)
+    ff_two, ng_two, up_two_term, down_two_term, up_sum_two = feed_forward(
+        normed2, normed2_t, cot, cot_t, up_bias_two, ff_weights_two, scal
+    )
+    up_received = chip_swap(up_two_term)
+    ff_weights = jnp.stack([w.reshape(1, -1, width) for w in (up_weight, down_weight)], 1)
+    ff_own, ng_own, ff_send, ng_send, up_one_term, down_one_term, up_sum_one = feed_forward(
+        normed2, normed2_t, cot, cot_t, up_bias_one, ff_weights, scal, (ff_two, ng_two)
     )
     ng_received = core_swap(ng_send)
-    ff_received = core_swap(after(ff_send, ng_received))
-    up_received = chip_swap(up_two_term)
     down_received = chip_swap(after(down_two_term, up_received))
-
     middle_grad, middle_low, second_sums = second_back(
-        middle, ng_own, ng_received, cot, params, scal
+        middle, ng_own, after(ng_received, up_received), cot, params, scal
     )
     middle_low_t = core_swap(middle_low)
-    result = (live * (middle + ff_own + ff_received.astype(f32) + down_bias)).astype(bf16)
-
     g_one, g_two, wo_one_term, wo_two_term = output_back(
         middle_low, middle_low_t, att_one, att_two, output_weight, wo_two, scal
     )
-    *grads_two, sums_two = attend_backward(*qkv_two, g_two, turned_two, stat_two)
-    wi_two_term = input_term(normed1, normed1_t, grads_two, scal, bf16)
-    *grads_one, sums_one = attend_backward(*qkv_one, g_one, turned_one, stat_one)
-    wi_one_term = input_term(normed1, normed1_t, grads_one, scal, f32)
-
-    wo_received = chip_swap(after(wo_two_term, down_received))
-    wi_received = chip_swap(after(wi_two_term, down_received))
-
-    grads = [*grads_one, *grads_two]
-    ng1_received = core_swap(norm1_other(grads, input_weight, wi_two))
+
+    def pairs_back(qkv, grad, turned, stat, begin, between):
+        pairs = []
+        waits = begin
+        for pair in range(cols // LANES):
+            pairs.append(attend_backward(*qkv, after(grad, *waits), turned, stat, pair))
+            waits = [pairs[-1][0], *between(pair, pairs[-1])]
+        return pairs
+
+    def both(own, received, *last):
+        return own.astype(f32) + after(received, *last).astype(f32)
+
+    sums = []
+
+    def between_two(pair, outs):
+        if pair > 0:
+            return []
+        up_both = both(up_one_term, up_received, outs[0]).astype(bf16)
+        down_both = both(down_one_term, down_received, outs[0]).astype(bf16)
+        sums.extend(lax.psum((up_both, down_both), "dp"))
+        return [up_both, down_both]
+
+    pairs_two = pairs_back(qkv_two, g_two, turned_two, stat_two, [], between_two)
+    up_sum, down_sum = sums
+    wi_two_term = input_term(normed1, normed1_t, pairs_two, scal)
+    ff_received = core_swap(after(ff_send, pairs_two[0][0]))
+    wo_received = chip_swap(after(wo_two_term, pairs_two[0][0]))
+    wi_received = chip_swap(wi_two_term)
+    pairs_one = pairs_back(
+        qkv_one, g_one, turned_one, stat_one, [wi_two_term], lambda *_: [wo_received]
+    )
+
+    quarters = [pairs_one, pairs_two]
+    weights = [input_weight, wi_two]
+    ng1_send = norm1_other(quarters, [input_weight, after(wi_two, wi_received, wo_received)])
+    ng1_received = core_swap(ng1_send)
+    wi_one_term = input_term(after(normed1, ng1_send), normed1_t, pairs_one, scal)
     token_grad, first_sums = norm1_own(
-        grads, input_weight, wi_two, ng1_received, tokens, middle_grad, params, scal
-    )
-
-    def both(own, received):
-        return (own + received.astype(f32)).astype(bf16)
-
-    up_sum, down_sum = lax.psum(
-        (both(up_one_term, up_received), both(down_one_term, down_received)), "dp"
-    )
-    wo_sum, wi_sum = lax.psum((both(wo_one_term, wo_received), both(wi_one_term, wi_received)), "dp")
-
-    def vector_pack(up_sums, in_sums):
-        units_sum = own_units
-        return jnp.concatenate([up_sums[0], in_sums[0] * units_sum, in_sums[1] * units_sum])
-
-    vec_one = vector_pack(up_sum_one, sums_one)
-    vec_two = vector_pack(up_sum_two, sums_two)
-    vec = vec_one + chip_swap(vec_two.reshape(-1, LANES)).reshape(-1)
-    vec = jnp.concatenate([vec, jnp.full((LANES,), own_units)])
-    vec_sum = lax.psum(vec, "dp")
-    rep_sum = lax.psum(jnp.concatenate([first_sums[:2], second_sums[:4]]), ("dp", "mp"))
-    share = 1.0 / vec_sum[-1]
-    vec_sum = vec_sum * share
-    rep_sum = rep_sum * share
+        quarters, weights, after(ng1_received, wi_one_term), tokens, middle_grad, params, scal
+    )
+    result = live * (middle + ff_own + ff_received.astype(f32) + down_bias)
+    result = result.astype(bf16)
+
+    def columns(term):
+        return jnp.concatenate([term[:, k * cols : (k + 1) * cols] for k in range(width // cols)])
+
+    tail = jnp.concatenate(
+        [both(wi_one_term, wi_received), both(columns(wo_one_term), columns(wo_received))]
+    )
+    bits = [1 << k for k in range(groups.bit_length() - 1)]
+    orders = [bits, bits[1:] + bits[:1]]
+    middle_row = tail.shape[0] // 2
+    parts = [tail[:middle_row], tail[middle_row:]]
+
+    def upper(bit):
+        return (group // bit) % 2
+
+    for turn in range(len(bits)):
+        if turn == 1:
+            parts = [after(part, token_grad) for part in parts]
+        for k in range(2):
+            bit = orders[k][turn]
+            half = parts[k].shape[0] // 2
+            keep = lax.dynamic_slice_in_dim(parts[k], upper(bit) * half, half, 0)
+            send = lax.dynamic_slice_in_dim(parts[k], (1 - upper(bit)) * half, half, 0)
+            parts[k] = keep + along(send.astype(bf16), bit).astype(f32)
+    parts = [part.astype(bf16) for part in parts]
+    for turn in reversed(range(len(bits))):
+        for k in range(2):
+            bit = orders[k][turn]
+            received = along(parts[k], bit)
+            is_upper = upper(bit) == 1
+            parts[k] = jnp.concatenate(
+                [jnp.where(is_upper, received, parts[k]), jnp.where(is_upper, parts[k], received)]
+            )
+    wi_rows = 3 * width
+    tail_sum = jnp.concatenate(parts)
+    wi_sum = tail_sum[:wi_rows].reshape(3, width, cols)
+    wo_sum = tail_sum[wi_rows:].reshape(width // cols, cols, cols)
+    wo_sum = jnp.concatenate([wo_sum[k] for k in range(width // cols)], 1)
+
+    def quarter_rows(pairs, up_sums):
+        sums_all = jnp.concatenate([pair[3] for pair in pairs], 1)
+        rest = jnp.full((1, width - 2 * cols), own_units)
+        bias_row = jnp.concatenate([sums_all[0:1] * own_units, sums_all[1:2] * own_units, rest], 1)
+        return jnp.concatenate([bias_row, up_sums[:1]])
+
+    late = jnp.concatenate([first_sums[:2], second_sums[:4]])
+    late = late + core_swap(late)
+    late_one, late_two = (
+        jnp.concatenate([late, quarter_rows(pairs, up_sums)])
+        for pairs, up_sums in ((pairs_one, up_sum_one), (pairs_two, up_sum_two))
+    )
+    late = late_one + chip_swap(late_two)
+    for bit in bits:
+        late = late + along(late, bit)
+    share = 2.0 / late[6, -1]
+    late = late * share
 
     return (
         result,
         token_grad,
-        rep_sum[0],
-        rep_sum[1],
+        late[0],
+        late[1],
         wi_sum.astype(f32) * share,
-        vec_sum[hidden : hidden + 2 * cols].reshape(2, cols),
+        late[6, : 2 * cols].reshape(2, cols),
         wo_sum.astype(f32) * share,
-        rep_sum[4],
-        rep_sum[2],
-        rep_sum[3],
+        late[4],
+        late[2],
+        late[3],
         up_sum.astype(f32) * share,
-        vec_sum[:hidden],
+        late[7],
         down_sum.astype(f32) * share,
-        rep_sum[5],
+        late[5],
     )
 
 

time: 719 us -> 537 us (0.75)
  waiting for transfers between devices: 274 us -> 109 us
  blocking collectives: 63.5 us -> 0 us
  starting transfers between devices: 9.93 us -> 35 us
  other arithmetic: 32.2 us -> 40.4 us
  local copies, waits for them, and re-layouts: 12.2 us -> 19.4 us
    psum x1, waiting for transfers between devices: 119 us -> 0.02 us  [between_two(): sums.extend(lax.psum((up_both, down_both), 'dp'))]
    ppermute x10 -> x9, waiting for transfers between devices: 145 us -> 33.8 us  [chip_swap(): return lax.ppermute(value, 'mp', [(i, i ^ 2) for i in range(shard_count)])]
    ppermute x0 -> x15, waiting for transfers between devices: none -> 67.8 us  [along(): return lax.ppermute(value, 'dp', [(i, i ^ bit) for i in range(groups)])]
    psum x2 -> x0, blocking collectives: 63.5 us -> none  [the longest x1 39.8 us: body(): lax.psum(jnp.concatenate([first_sums[:2], second_sums[:4]]), ('dp', 'mp'))]
    ppermute x0 -> x15, starting transfers between devices: none -> 20.3 us  [along(): return lax.ppermute(value, 'dp', [(i, i ^ bit) for i in range(groups)])]
    pallas_call x4 -> x6, Pallas kernels: 108 us -> 114 us  [the longest x4 96.1 us: attend_backward(): call(kernel, 'attend_backward', (1, count), [by_query, by_key, by_key, by...]
    convert_element_type x5 -> x6, other arithmetic: 19.8 us -> 16.2 us  [the longest x1 6.76 us: body(): result = result.astype(bf16)]
  transfers between devices with their start and end apart: 19 -> 35, of which waited for: 8 -> 17; matrix products, arithmetic and copies ran while one was open for 4% -> 8% of each run, Pallas kernels for 28% -> 48%
where the time goes in v2:
time: 537 us; the launch traced here: 528 us
  Pallas kernels  307 us (57%)
  waiting for transfers between devices  109 us (20%)
  other arithmetic  40.4 us (8%)
  starting transfers between devices  35 us (7%)
  local copies, waits for them, and re-layouts  19.4 us (4%)
  between operations  17.7 us (3%)
    pallas_call x4, Pallas kernels, attend_backward(): call(kernel, 'attend_backward', (1, count), [by_query, by_key, by_key, by...  96.1 us
    pallas_call x2, Pallas kernels, feed_forward(): call(kernel, 'feed_forward', (2 * count,), ins, outs + [whole(terms[0]),...  73 us
    ppermute x15, waiting for transfers between devices, along(): return lax.ppermute(value, 'dp', [(i, i ^ bit) for i in range(groups)])  67.8 us
    pallas_call x2, Pallas kernels, attend_forward(): call(kernel, 'attend_forward', (pairs, rows // block), [by_query, by_key,...  53.9 us
    ppermute x9, waiting for transfers between devices, chip_swap(): return lax.ppermute(value, 'mp', [(i, i ^ 2) for i in range(shard_count)])  33.8 us
    ppermute x15, starting transfers between devices, along(): return lax.ppermute(value, 'dp', [(i, i ^ bit) for i in range(groups)])  20.3 us
    pallas_call x2, Pallas kernels, input_term(): call(kernel, 'input_term', (3,), [scalars(), whole(norm_own), whole(norm_...  16.5 us
    pallas_call x2, Pallas kernels, project(): call(kernel, 'project', (2 * count,), [*halves(block, width, count), whol...  14.8 us
  transfers between devices with their start and end apart: 35, of which 17 were waited for; matrix products, arithmetic and copies ran while one was open for 8% of the time, Pallas kernels for 48%

profile of v2, /device:TPU:0, one launch (start us, length us, event | category | flops | bytes accessed | tf_op | source)
XLA Modules:
  0.0 528.4 jit_solution(17826027830170476666)
XLA Ops:
  12.7 5.4 %first_norm.1 = (bf16[1024,1024]{1,0:T(8,128)(2,1)}, bf16[1024,1024]{1,0:T(8,128)(2,1)}) custom-call(f32[2]{0:T(128)} %pad_maximum_fusion.9.scal_ref, bf16[1024,1024]{1,0:T(8,128)(2,1)} %refs_15_.1, bf16[1024,1024]{1,0:T(8,128)(2,1)} %grad_ref.1, f32[8,1024]{1,0:T(8,128)} %stack.55.par_ref.refs_17_), custom_call_target="tpu_custom_call" | custom-call | flops 20 | bytes 8 | tf_op jit(solution)/shard_map/first_norm/pallas_call | solution.py:112
  19.7 2.6 collective-permute-start.1
  22.3 12.5 %collective-permute-done.1 = bf16[1,2,128,1024]{3,2,1,0:T(8,128)(2,1)S(1)} collective-permute-done((bf16[1,2,128,1024]{3,2,1,0:T(8,128)(2,1)S(1)}, bf16[1,2,128,1024]{3,2,1,0:T(8,128)(2,1)S(1)}, u32[]{:S(2)}, u32[]{:S(2)}) %collective-permute-start.1) | collective-permute-done | bytes 524320 | tf_op jit(solution)/shard_map/ppermute | solution.py:680
  39.1 1.8 collective-permute-start.4
  42.2 7.4 %project.2 = (bf16[2048,256]{1,0:T(8,128)(2,1)}, bf16[2048,256]{1,0:T(8,128)(2,1)}, bf16[2048,256]{1,0:T(8,128)(2,1)}) custom-call(bf16[1024,1024]{1,0:T(8,128)(2,1)} %get-tuple-element.143.own_ref.no_ref, bf16[1024,1024]{1,0:T(8,128)(2,1)} %copy-done, bf16[3,1024,256]{2,1,0:T(8,128)(2,1)} %refs_12_.3, f32[2,256]{1,0:T(2,128)} %b_ref.1), custom_call_target="tpu_custom_call" | custom-call | flops 3221 | bytes 8 | tf_op jit(solution)/shard_map/project/pallas_call | solution.py:147
  49.6 26.8 %attend_forward.2 = (bf16[2048,256]{1,0:T(8,128)(2,1)}, f32[256,2048]{1,0:T(8,128)}, f32[2,8,2048]{2,1,0:T(8,128)}) custom-call(bf16[2048,256]{1,0:T(8,128)(2,1)} %get-tuple-element.87.q_ref, bf16[2048,256]{1,0:T(8,128)(2,1)} %get-tuple-element.88.k_ref, bf16[2048,256]{1,0:T(8,128)(2,1)} %get-tuple-element.89.v_ref), custom_call_target="tpu_custom_call" | custom-call | flops 17179869184000 | bytes 6291456000 | tf_op jit(solution)/shard_map/attend_forward/pallas_call | solution.py:206
  76.5 7.4 %project.3 = (bf16[2048,256]{1,0:T(8,128)(2,1)}, bf16[2048,256]{1,0:T(8,128)(2,1)}, bf16[2048,256]{1,0:T(8,128)(2,1)}) custom-call(bf16[1024,1024]{1,0:T(8,128)(2,1)} %get-tuple-element.143.own_ref.no_ref, bf16[1024,1024]{1,0:T(8,128)(2,1)} %copy-done, bf16[3,1024,256]{2,1,0:T(8,128)(2,1)} %collective-permute-done.2.w_ref.refs_13_, f32[2,256]{1,0:T(2,128)} %reshape.66.b_ref), custom_call_target="tpu_custom_call" | custom-call | flops 3221 | bytes 8 | tf_op jit(solution)/shard_map/project/pallas_call | solution.py:147
  83.9 27.1 %attend_forward.3 = (bf16[2048,256]{1,0:T(8,128)(2,1)}, f32[256,2048]{1,0:T(8,128)}, f32[2,8,2048]{2,1,0:T(8,128)}) custom-call(bf16[2048,256]{1,0:T(8,128)(2,1)} %get-tuple-element.94.q_ref, bf16[2048,256]{1,0:T(8,128)(2,1)} %get-tuple-element.95.k_ref, bf16[2048,256]{1,0:T(8,128)(2,1)} %get-tuple-element.96.v_ref), custom_call_target="tpu_custom_call" | custom-call | flops 17179869184000 | bytes 6291456000 | tf_op jit(solution)/shard_map/attend_forward/pallas_call | solution.py:206
  112.0 3.8 output_other.1
  116.3 6.3 %collective-permute-done.5.r_ref = bf16[1024,1024]{1,0:T(8,128)(2,1)} collective-permute-done((bf16[1024,1024]{1,0:T(8,128)(2,1)}, bf16[1024,1024]{1,0:T(8,128)(2,1)}, u32[]{:S(2)}, u32[]{:S(2)}) %collective-permute-start.5) | collective-permute-done | bytes 2097184 | tf_op jit(solution)/shard_map/ppermute | solution.py:677
  122.5 6.9 %output_own.1 = (f32[1024,1024]{1,0:T(8,128)}, bf16[1024,1024]{1,0:T(8,128)(2,1)}) custom-call(bf16[1024,1024]{1,0:T(8,128)(2,1)} %refs_15_.1, bf16[2048,256]{1,0:T(8,128)(2,1)} %get-tuple-element.90.a_ref, bf16[2048,256]{1,0:T(8,128)(2,1)} %get-tuple-element.99.b_ref, bf16[256,1024]{1,0:T(8,128)(2,1)} %wa_ref.5, ...), custom_call_target="tpu_custom_call" | custom-call | flops 1073 | bytes 11 | tf_op jit(solution)/shard_map/output_own/pallas_call | solution.py:356
  129.6 4.6 pad_maximum_fusion.up_ref.dn_ref
  134.8 35.5 %feed_forward.2 = (f32[2048,1024]{1,0:T(8,128)}, f32[2048,1024]{1,0:T(8,128)}, bf16[1024,1024]{1,0:T(8,128)(2,1)}, bf16[1024,1024]{1,0:T(8,128)(2,1)}, f32[8,1024]{1,0:T(8,128)}) custom-call(f32[2]{0:T(128)} %pad_maximum_fusion.9.scal_ref, bf16[1024,1024]{1,0:T(8,128)(2,1)} %get-tuple-element.101.no_ref, bf16[1024,1024]{1,0:T(8,128)(2,1)} %collective-permute-done.6.nt_ref, ...), custom_call_target="tpu_custom_call" | custom-call | flops 25769 | bytes 37 | tf_op jit(solution)/shard_map/feed_forward/pallas_call | solution.py:450
  171.8 37.6 %feed_forward.3 = (f32[1024,1024]{1,0:T(8,128)}, f32[1024,1024]{1,0:T(8,128)}, bf16[1024,1024]{1,0:T(8,128)(2,1)}, bf16[1024,1024]{1,0:T(8,128)(2,1)}, bf16[1024...) custom-call(f32[2]{0:T(128)} %pad_maximum_fusion.9.scal_ref, ...), custom_call_target="tpu_custom_call" | custom-call | flops 25769803776000 | bytes 37748736000 | tf_op jit(solution)/shard_map/feed_forward/pallas_call | solution.py:450
  209.5 9.0 %collective-permute-done.9 = bf16[1024,1024]{1,0:T(8,128)(2,1)} collective-permute-done((bf16[1024,1024]{1,0:T(8,128)(2,1)}, bf16[1024,1024]{1,0:T(8,128)(2,1)}, u32[]{:S(2)}, u32[]{:S(2)}) %collective-permute-start.9) | collective-permute-done | bytes 2097184 | tf_op jit(solution)/shard_map/ppermute | solution.py:680
  219.9 9.3 %second_back.1 = (f32[1024,1024]{1,0:T(8,128)}, bf16[1024,1024]{1,0:T(8,128)(2,1)}, f32[8,1024]{1,0:T(8,128)}) custom-call(f32[2]{0:T(128)} %pad_maximum_fusion.9.scal_ref, f32[1024,1024]{1,0:T(8,128)} %get-tuple-element.100.mid_ref, f32[1024,1024]{1,0:T(8,128)} %get-tuple-element.107.go_ref, bf16[1024,1024]{1,0:T(8,128)(2,1)} %copy-done.10, ...), custom_call_target="tpu_custom_call" | custom-call | flops 31 | bytes 18 | tf_op jit(solution)/shard_map/second_back/pallas_call | solution.py:487
  236.3 9.1 %output_back.1 = (bf16[2048,256]{1,0:T(8,128)(2,1)}, bf16[2048,256]{1,0:T(8,128)(2,1)}, bf16[256,1024]{1,0:T(8,128)(2,1)}, bf16[256,1024]{1,0:T(8,128)(2,1)}) custom-call(f32[2]{0:T(128)} %pad_maximum_fusion.9.scal_ref, bf16[1024,1024]{1,0:T(8,128)(2,1)} %get-tuple-element.111.lo_ref, bf16[1024,1024]{1,0:T(8,128)(2,1)} %copy-done.11, ...), custom_call_target="tpu_custom_call" | custom-call | flops 4294 | bytes 8 | tf_op jit(solution)/shard_map/output_back/pallas_call | solution.py:530
  245.4 24.3 %attend_backward.4 = (bf16[2048,128]{1,0:T(8,128)(2,1)}, bf16[2048,128]{1,0:T(8,128)(2,1)}, bf16[2048,128]{1,0:T(8,128)(2,1)}, f32[8,128]{1,0:T(8,128)}) custom-call(bf16[2048,256]{1,0:T(8,128)(2,1)} %get-tuple-element.94.q_ref, bf16[2048,256]{1,0:T(8,128)(2,1)} %get-tuple-element.95.k_ref, bf16[2048,256]{1,0:T(8,128)(2,1)} %get-tuple-element.96.v_ref, ...), custom_call_target="tpu_custom_call" | custom-call | flops 21474836480000 | bytes 5242880000 | tf_op jit(solution)/shard_map/attend_backward/pallas_call | solution.py:295
  269.8 10.6 %collective-permute-done.12 = bf16[1024,1024]{1,0:T(8,128)(2,1)} collective-permute-done((bf16[1024,1024]{1,0:T(8,128)(2,1)}, bf16[1024,1024]{1,0:T(8,128)(2,1)}, u32[]{:S(2)}, u32[]{:S(2)}) %collective-permute-start.12) | collective-permute-done | bytes 2097184 | tf_op jit(solution)/shard_map/ppermute | solution.py:680
  280.4 3.9 add_convert_fusion
  284.3 3.9 add_convert_fusion.1
  289.8 23.9 %attend_backward.5 = (bf16[2048,128]{1,0:T(8,128)(2,1)}, bf16[2048,128]{1,0:T(8,128)(2,1)}, bf16[2048,128]{1,0:T(8,128)(2,1)}, f32[8,128]{1,0:T(8,128)}) custom-call(bf16[2048,256]{1,0:T(8,128)(2,1)} %get-tuple-element.94.q_ref, bf16[2048,256]{1,0:T(8,128)(2,1)} %get-tuple-element.95.k_ref, bf16[2048,256]{1,0:T(8,128)(2,1)} %get-tuple-element.96.v_ref, ...), custom_call_target="tpu_custom_call" | custom-call | flops 21474836480000 | bytes 5242880000 | tf_op jit(solution)/shard_map/attend_backward/pallas_call | solution.py:295
  313.7 8.1 %input_term.2 = bf16[3072,256]{1,0:T(8,128)(2,1)} custom-call(f32[2]{0:T(128)} %pad_maximum_fusion.9.scal_ref, bf16[1024,1024]{1,0:T(8,128)(2,1)} %get-tuple-element.143.own_ref.no_ref, bf16[1024,1024]{1,0:T(8,128)(2,1)} %copy-done, bf16[2048,128]{1,0:T(8,128)(2,1)} %get-tuple-element.115.refs_0_.refs_6_, ...), custom_call_target="tpu_custom_call" | custom-call | flops 3221 | bytes 10 | tf_op jit(solution)/shard_map/input_term/pallas_call | solution.py:559
  323.0 23.9 %attend_backward.6 = (bf16[2048,128]{1,0:T(8,128)(2,1)}, bf16[2048,128]{1,0:T(8,128)(2,1)}, bf16[2048,128]{1,0:T(8,128)(2,1)}, f32[8,128]{1,0:T(8,128)}) custom-call(bf16[2048,256]{1,0:T(8,128)(2,1)} %get-tuple-element.87.q_ref, bf16[2048,256]{1,0:T(8,128)(2,1)} %get-tuple-element.88.k_ref, bf16[2048,256]{1,0:T(8,128)(2,1)} %get-tuple-element.89.v_ref, ...), custom_call_target="tpu_custom_call" | custom-call | flops 21474836480000 | bytes 5242880000 | tf_op jit(solution)/shard_map/attend_backward/pallas_call | solution.py:295
  348.3 24.0 %attend_backward.7 = (bf16[2048,128]{1,0:T(8,128)(2,1)}, bf16[2048,128]{1,0:T(8,128)(2,1)}, bf16[2048,128]{1,0:T(8,128)(2,1)}, f32[8,128]{1,0:T(8,128)}) custom-call(bf16[2048,256]{1,0:T(8,128)(2,1)} %get-tuple-element.87.q_ref, bf16[2048,256]{1,0:T(8,128)(2,1)} %get-tuple-element.88.k_ref, bf16[2048,256]{1,0:T(8,128)(2,1)} %get-tuple-element.89.v_ref, ...), custom_call_target="tpu_custom_call" | custom-call | flops 21474836480000 | bytes 5242880000 | tf_op jit(solution)/shard_map/attend_backward/pallas_call | solution.py:295
  372.3 7.8 %first_other.1 = bf16[1024,1024]{1,0:T(8,128)(2,1)} custom-call(bf16[2048,128]{1,0:T(8,128)(2,1)} %get-tuple-element.133.refs_0_, bf16[2048,128]{1,0:T(8,128)(2,1)} %get-tuple-element.137.refs_1_, bf16[2048,128]{1,0:T(8,128)(2,1)} %get-tuple-element.138.refs_2_, bf16[2048,128]{1,0:T(8,128)(2,1)} %get-tuple-element.139.refs_3_, ...), custom_call_target="tpu_custom_call" | custom-call | flops 3221 | bytes 8 | tf_op jit(solution)/shard_map/first_other/pallas_call | solution.py:601
  383.1 8.5 %input_term.3 = bf16[3072,256]{1,0:T(8,128)(2,1)} custom-call(f32[2]{0:T(128)} %pad_maximum_fusion.9.scal_ref, bf16[1024,1024]{1,0:T(8,128)(2,1)} %get-tuple-element.143.own_ref.no_ref, bf16[1024,1024]{1,0:T(8,128)(2,1)} %copy-done, bf16[2048,128]{1,0:T(8,128)(2,1)} %get-tuple-element.133.refs_0_, bf16[2048,128]{1,0:T(8,128)(2,1)} %get-tuple-element.137.refs_1_, ...), custom_call_target="tpu_custom_call" | custom-call | flops 3221 | bytes 10 | tf_op jit(solution)/shard_map/input_term/pallas_call | solution.py:559
  391.5 2.2 convert_add_fusion
  399.9 10.5 %first_own.1 = (bf16[1024,1024]{1,0:T(8,128)(2,1)}, f32[8,1024]{1,0:T(8,128)}) custom-call(f32[2]{0:T(128)} %pad_maximum_fusion.9.scal_ref, bf16[2048,128]{1,0:T(8,128)(2,1)} %get-tuple-element.133.refs_0_, bf16[2048,128]{1,0:T(8,128)(2,1)} %get-tuple-element.137.refs_1_, bf16[2048,128]{1,0:T(8,128)(2,1)} %get-tuple-element.138.refs_2_, ...), custom_call_target="tpu_custom_call" | custom-call | flops 3221 | bytes 16 | tf_op jit(solution)/shard_map/first_own/pallas_call | solution.py:639
  411.3 6.8 %multiply_convert_fusion = bf16[1024,1024]{1,0:T(8,128)(2,1)} fusion(bf16[1024,1024]{1,0:T(8,128)(2,1)} %collective-permute-done.11, f32[1024,1024]{1,0:T(8,128)} %get-tuple-element.100.mid_ref, f32[1024,1024]{1,0:T(8,128)} %get-tuple-element.105, f32[1024]{0:T(1024)S(1)} %copy-done.19, f32[]{:T(128)} %convert_element_type.97), kind=kLoop, calls=%fused_computation.5 | loop fusion | flops 6291456 | bytes 12587012 | tf_op jit(solution)/shard_map/convert_element_type | solution.py:790
  419.2 23.1 %collective-permute-done.27 = bf16[1024,256]{1,0:T(8,128)(2,1)S(1)} collective-permute-done((bf16[1024,256]{1,0:T(8,128)(2,1)}, bf16[1024,256]{1,0:T(8,128)(2,1)S(1)}, u32[]{:S(2)}, u32[]{:S(2)}) %collective-permute-start.27) | collective-permute-done | bytes 524320 | tf_op jit(solution)/shard_map/ppermute | solution.py:686
  445.1 1.8 collective-permute-done.18
  447.0 4.6 collective-permute-start.28
  451.6 2.8 collective-permute-start.20
  454.4 2.8 collective-permute-start.22
  457.2 9.1 %collective-permute-done.20 = f32[8,1024]{1,0:T(8,128)S(1)} collective-permute-done((f32[8,1024]{1,0:T(8,128)S(1)}, f32[8,1024]{1,0:T(8,128)S(1)}, u32[]{:S(2)}, u32[]{:S(2)}) %collective-permute-start.20) | collective-permute-done | bytes 32800 | tf_op jit(solution)/shard_map/ppermute | solution.py:686
  470.0 1.7 collective-permute-start.29
  471.9 3.1 collective-permute-done.29
  475.0 1.7 collective-permute-start.30
  476.8 2.2 collective-permute-done.23
  480.1 2.0 collective-permute-start.31
  482.2 10.9 %collective-permute-done.24 = bf16[256,256]{1,0:T(8,128)(2,1)S(1)} collective-permute-done((bf16[256,256]{1,0:T(8,128)(2,1)S(1)}, bf16[256,256]{1,0:T(8,128)(2,1)S(1)}, u32[]{:S(2)}, u32[]{:S(2)}) %collective-permute-start.24) | collective-permute-done | bytes 131104 | tf_op jit(solution)/shard_map/ppermute | solution.py:686
  493.2 4.2 convert_multiply_fusion
  499.6 4.7 collective-permute-done.25
  504.7 2.6 convert_multiply_fusion.1
  507.3 8.1 %collective-permute-done.32 = bf16[1024,256]{1,0:T(8,128)(2,1)S(1)} collective-permute-done((bf16[1024,256]{1,0:T(8,128)(2,1)S(1)}, bf16[1024,256]{1,0:T(8,128)(2,1)S(1)}, u32[]{:S(2)}, u32[]{:S(2)}) %collective-permute-start.32) | collective-permute-done | bytes 524320 | tf_op jit(solution)/shard_map/ppermute | solution.py:686
  515.7 2.5 collective-permute-done.26
  518.5 1.9 convert_multiply_fusion.2
  (181 shorter events, 49.4 us)
Async XLA Ops:
  7.2 104.8 %all-gather.2.cloned.1.call-start = ((), (), s32[]{:S(2)}) async-start(), calls=%async_computation | async-start | bytes 4718592 | tf_op jit(solution)/shard_map/all_gather | solution.py:696
  18.1 22.9 %collective-permute-start = (bf16[1024,1024]{1,0:T(8,128)(2,1)}, bf16[1024,1024]{1,0:T(8,128)(2,1)S(1)}, u32[]{:S(2)}, u32[]{:S(2)}) collective-permute-start(bf16[1024,1024]{1,0:T(8,128)(2,1)} %get-tuple-element.143.own_ref.no_ref), channel_id=1, source_target_pairs={{0,1},{1,0},{2,3},{3,2},{4,5},{5,4},{6,7},{7,6},{8,9},{9,8},{10,11... | collective-permute-start | bytes 6291464 | tf_op jit(solution)/shard_map/ppermute | solution.py:677
  19.7 15.2 %collective-permute-start.1 = (bf16[1,2,128,1024]{3,2,1,0:T(8,128)(2,1)S(1)}, bf16[1,2,128,1024]{3,2,1,0:T(8,128)(2,1)S(1)}, u32[]{:S(2)}, u32[]{:S(2)}) collective-permute-start(bf16[1,2,128,1024]{3,2,1,0:T(8,128)(2,1)S(1)} %maximum_bitcast_fusion), channel_id=1, source_target_pairs={{0,2},{1,3},{2,0},{3,1},{4,6},{5,7},{6,4},{7,5},{8,10},{9,11},{10,... | collective-permute-start | bytes 1572872 | tf_op jit(solution)/shard_map/ppermute | solution.py:680
  34.8 3.7 collective-permute-start.3
  36.6 39.9 %collective-permute-start.2 = (bf16[3,1024,256]{2,1,0:T(8,128)(2,1)}, bf16[3,1024,256]{2,1,0:T(8,128)(2,1)}, u32[]{:S(2)}, u32[]{:S(2)}) collective-permute-start(bf16[3,1024,256]{2,1,0:T(8,128)(2,1)} %refs_12_.3), channel_id=1, source_target_pairs={{0,2},{1,3},{2,0},{3,1},{4,6},{5,7},{6,4},{7,5},{8,10},{9,11},{10,... | collective-permute-start | bytes 4718600 | tf_op jit(solution)/shard_map/ppermute | solution.py:680
  36.9 456.3 %all-reduce.3.cloned.1.call-start = ((), (), s32[]{:S(2)}) async-start(), calls=%async_computation.1 | async-start | bytes 8388608 | tf_op jit(solution)/shard_map/psum | solution.py:768
  38.5 38.0 %copy-start.23 = (f32[12,128]{1,0:T(8,128)}, f32[12,128]{1,0:T(8,128)S(1)}, u32[]{:S(2)}) copy-start(f32[12,128]{1,0:T(8,128)S(1)} %collective-permute-done.3) | copy-start | bytes 18436
  39.1 72.9 %collective-permute-start.4 = (bf16[256,1024]{1,0:T(8,128)(2,1)}, bf16[256,1024]{1,0:T(8,128)(2,1)}, u32[]{:S(2)}, u32[]{:S(2)}) collective-permute-start(bf16[256,1024]{1,0:T(8,128)(2,1)} %wa_ref.5), channel_id=1, source_target_pairs={{0,2},{1,3},{2,0},{3,1},{4,6},{5,7},{6,4},{7,5},{8,10},{9,11},{10,... | collective-permute-start | bytes 1572872 | tf_op jit(solution)/shard_map/ppermute | solution.py:680
  115.7 6.8 %collective-permute-start.5 = (bf16[1024,1024]{1,0:T(8,128)(2,1)}, bf16[1024,1024]{1,0:T(8,128)(2,1)}, u32[]{:S(2)}, u32[]{:S(2)}) collective-permute-start(bf16[1024,1024]{1,0:T(8,128)(2,1)} %output_other.1), channel_id=1, source_target_pairs={{0,1},{1,0},{2,3},{3,2},{4,5},{5,4},{6,7},{7,6},{8,9},{9,8},{10,11... | collective-permute-start | bytes 6291464 | tf_op jit(solution)/shard_map/ppermute | solution.py:677
  115.8 19.0 %collective-permute-start.7 = (bf16[1024,1024]{1,0:T(8,128)(2,1)S(1)}, bf16[1024,1024]{1,0:T(8,128)(2,1)}, u32[]{:S(2)}, u32[]{:S(2)}) collective-permute-start(bf16[1024,1024]{1,0:T(8,128)(2,1)S(1)} %copy-done.3), channel_id=1, source_target_pairs={{0,1},{1,0},{2,3},{3,2},{4,5},{5,4},{6,7},{7,6},{8,9},{9,8},{10,11... | collective-permute-start | bytes 6291464 | tf_op jit(solution)/shard_map/ppermute | solution.py:677
  129.4 5.4 %collective-permute-start.6 = (bf16[1024,1024]{1,0:T(8,128)(2,1)}, bf16[1024,1024]{1,0:T(8,128)(2,1)}, u32[]{:S(2)}, u32[]{:S(2)}) collective-permute-start(bf16[1024,1024]{1,0:T(8,128)(2,1)} %get-tuple-element.101.no_ref), channel_id=1, source_target_pairs={{0,1},{1,0},{2,3},{3,2},{4,5},{5,4},{6,7},{7,6},{8,9},{9,8},{10,11... | collective-permute-start | bytes 6291464 | tf_op jit(solution)/shard_map/ppermute | solution.py:677
  170.3 48.3 %collective-permute-start.9 = (bf16[1024,1024]{1,0:T(8,128)(2,1)}, bf16[1024,1024]{1,0:T(8,128)(2,1)}, u32[]{:S(2)}, u32[]{:S(2)}) collective-permute-start(bf16[1024,1024]{1,0:T(8,128)(2,1)} %get-tuple-element.109), channel_id=1, source_target_pairs={{0,2},{1,3},{2,0},{3,1},{4,6},{5,7},{6,4},{7,5},{8,10},{9,11},{10,... | collective-permute-start | bytes 6291464 | tf_op jit(solution)/shard_map/ppermute | solution.py:680
  209.4 9.2 %collective-permute-start.8 = (bf16[1024,1024]{1,0:T(8,128)(2,1)}, bf16[1024,1024]{1,0:T(8,128)(2,1)S(1)}, u32[]{:S(2)}, u32[]{:S(2)}) collective-permute-start(bf16[1024,1024]{1,0:T(8,128)(2,1)} %get-tuple-element.108), channel_id=1, source_target_pairs={{0,1},{1,0},{2,3},{3,2},{4,5},{5,4},{6,7},{7,6},{8,9},{9,8},{10,11... | collective-permute-start | bytes 6291464 | tf_op jit(solution)/shard_map/ppermute | solution.py:677
  229.3 5.7 %collective-permute-start.10 = (bf16[1024,1024]{1,0:T(8,128)(2,1)}, bf16[1024,1024]{1,0:T(8,128)(2,1)S(1)}, u32[]{:S(2)}, u32[]{:S(2)}) collective-permute-start(bf16[1024,1024]{1,0:T(8,128)(2,1)} %get-tuple-element.111.lo_ref), channel_id=1, source_target_pairs={{0,1},{1,0},{2,3},{3,2},{4,5},{5,4},{6,7},{7,6},{8,9},{9,8},{10,11... | collective-permute-start | bytes 6291464 | tf_op jit(solution)/shard_map/ppermute | solution.py:677
  232.2 48.2 %collective-permute-start.12 = (bf16[1024,1024]{1,0:T(8,128)(2,1)}, bf16[1024,1024]{1,0:T(8,128)(2,1)}, u32[]{:S(2)}, u32[]{:S(2)}) collective-permute-start(bf16[1024,1024]{1,0:T(8,128)(2,1)} %get-tuple-element.122), channel_id=1, source_target_pairs={{0,2},{1,3},{2,0},{3,1},{4,6},{5,7},{6,4},{7,5},{8,10},{9,11},{10,... | collective-permute-start | bytes 6291464 | tf_op jit(solution)/shard_map/ppermute | solution.py:680
  245.4 35.0 %copy-start.9 = (bf16[1024,1024]{1,0:T(8,128)(2,1)S(1)}, bf16[1024,1024]{1,0:T(8,128)(2,1)}, u32[]{:S(2)}) copy-start(bf16[1024,1024]{1,0:T(8,128)(2,1)} %get-tuple-element.120) | copy-start | bytes 6291460
  269.7 14.5 %copy-start.8 = (bf16[1024,1024]{1,0:T(8,128)(2,1)S(1)}, bf16[1024,1024]{1,0:T(8,128)(2,1)}, u32[]{:S(2)}) copy-start(bf16[1024,1024]{1,0:T(8,128)(2,1)} %get-tuple-element.118) | copy-start | bytes 6291460
  288.2 60.1 %collective-permute-start.13 = (bf16[256,1024]{1,0:T(8,128)(2,1)}, bf16[256,1024]{1,0:T(8,128)(2,1)}, u32[]{:S(2)}, u32[]{:S(2)}) collective-permute-start(bf16[256,1024]{1,0:T(8,128)(2,1)} %get-tuple-element.135), channel_id=1, source_target_pairs={{0,2},{1,3},{2,0},{3,1},{4,6},{5,7},{6,4},{7,5},{8,10},{9,11},{10,... | collective-permute-start | bytes 1572872 | tf_op jit(solution)/shard_map/ppermute | solution.py:680
  321.7 50.6 %collective-permute-start.14 = (bf16[3072,256]{1,0:T(8,128)(2,1)}, bf16[3072,256]{1,0:T(8,128)(2,1)}, u32[]{:S(2)}, u32[]{:S(2)}) collective-permute-start(bf16[3072,256]{1,0:T(8,128)(2,1)} %input_term.2), channel_id=1, source_target_pairs={{0,2},{1,3},{2,0},{3,1},{4,6},{5,7},{6,4},{7,5},{8,10},{9,11},{10,... | collective-permute-start | bytes 4718600 | tf_op jit(solution)/shard_map/ppermute | solution.py:680
  323.0 23.9 %copy-start.25 = (f32[8,256]{1,0:T(8,128)S(1)}, f32[8,256]{1,0:T(8,128)}, u32[]{:S(2)}) copy-start(f32[8,256]{1,0:T(8,128)} %constant_dynamic-update-slice_fusion.3) | copy-start | bytes 24580
  323.0 23.9 %copy-start.32 = (f32[8,128]{1,0:T(8,128)S(1)}, f32[8,128]{1,0:T(8,128)}, u32[]{:S(2)}) copy-start(f32[8,128]{1,0:T(8,128)} %get-tuple-element.153) | copy-start | bytes 12292
  323.0 24.5 %copy-start.12 = (bf16[256,1024]{1,0:T(8,128)(2,1)S(1)}, bf16[256,1024]{1,0:T(8,128)(2,1)}, u32[]{:S(2)}) copy-start(bf16[256,1024]{1,0:T(8,128)(2,1)} %get-tuple-element.156) | copy-start | bytes 1572868
  372.3 9.6 %copy-start.31 = (f32[8,128]{1,0:T(8,128)S(1)}, f32[8,128]{1,0:T(8,128)}, u32[]{:S(2)}) copy-start(f32[8,128]{1,0:T(8,128)} %get-tuple-element.150) | copy-start | bytes 12292
  380.1 19.7 %collective-permute-start.15 = (bf16[1024,1024]{1,0:T(8,128)(2,1)}, bf16[1024,1024]{1,0:T(8,128)(2,1)}, u32[]{:S(2)}, u32[]{:S(2)}) collective-permute-start(bf16[1024,1024]{1,0:T(8,128)(2,1)} %first_other.1), channel_id=1, source_target_pairs={{0,1},{1,0},{2,3},{3,2},{4,5},{5,4},{6,7},{7,6},{8,9},{9,8},{10,11... | collective-permute-start | bytes 6291464 | tf_op jit(solution)/shard_map/ppermute | solution.py:677
  380.2 31.1 %collective-permute-start.11 = (bf16[1024,1024]{1,0:T(8,128)(2,1)}, bf16[1024,1024]{1,0:T(8,128)(2,1)}, u32[]{:S(2)}, u32[]{:S(2)}) collective-permute-start(bf16[1024,1024]{1,0:T(8,128)(2,1)} %get-tuple-element.116), channel_id=1, source_target_pairs={{0,1},{1,0},{2,3},{3,2},{4,5},{5,4},{6,7},{7,6},{8,9},{9,8},{10,11... | collective-permute-start | bytes 6291464 | tf_op jit(solution)/shard_map/ppermute | solution.py:677
  396.7 45.6 %collective-permute-start.27 = (bf16[1024,256]{1,0:T(8,128)(2,1)}, bf16[1024,256]{1,0:T(8,128)(2,1)S(1)}, u32[]{:S(2)}, u32[]{:S(2)}) collective-permute-start(bf16[1024,256]{1,0:T(8,128)(2,1)} %fusion.1), channel_id=1, source_target_pairs={{0,8},{4,12},{8,0},{12,4},{16,24},{20,28},{24,16},{28,20},{1,9},{5... | collective-permute-start | bytes 1572872 | tf_op jit(solution)/shard_map/ppermute | solution.py:686
  398.5 12.7 %copy-start.18 = (f32[4,1024]{1,0:T(4,128)S(1)}, f32[4,1024]{1,0:T(4,128)}, u32[]{:S(2)}) copy-start(f32[4,1024]{1,0:T(4,128)} %slice.116) | copy-start | bytes 49156
  398.5 12.8 %copy-start.19 = (f32[1024]{0:T(1024)S(1)}, f32[1024]{0:T(1024)}, u32[]{:S(2)}) copy-start(f32[1024]{0:T(1024)} %param.33) | copy-start | bytes 12292
  398.5 45.4 %collective-permute-start.21 = (bf16[1024,256]{1,0:T(8,128)(2,1)}, bf16[1024,256]{1,0:T(8,128)(2,1)}, u32[]{:S(2)}, u32[]{:S(2)}) collective-permute-start(bf16[1024,256]{1,0:T(8,128)(2,1)} %dynamic-slice_convert_fusion), channel_id=1, source_target_pairs={{0,4},{4,0},{8,12},{12,8},{16,20},{20,16},{24,28},{28,24},{1,5},{5... | collective-permute-start | bytes 1572872 | tf_op jit(solution)/shard_map/ppermute | solution.py:686
  411.2 31.1 %copy-start.2 = (f32[1024,256]{1,0:T(8,128)S(1)}, f32[1024,256]{1,0:T(8,128)}, u32[]{:S(2)}) copy-start(f32[1024,256]{1,0:T(8,128)} %convert_add_fusion.1) | copy-start | bytes 3145732
  411.2 6.9 %collective-permute-start.16 = (f32[6,1024]{1,0:T(8,128)S(1)}, f32[6,1024]{1,0:T(8,128)S(1)}, u32[]{:S(2)}, u32[]{:S(2)}) collective-permute-start(f32[6,1024]{1,0:T(8,128)S(1)} %pad_maximum_fusion.8), channel_id=1, source_target_pairs={{0,1},{1,0},{2,3},{3,2},{4,5},{5,4},{6,7},{7,6},{8,9},{9,8},{10,11... | collective-permute-start | bytes 73736 | tf_op jit(solution)/shard_map/ppermute | solution.py:677
  418.1 24.7 %copy-start.21 = (f32[1,1024]{1,0:T(1,128)S(1)}, f32[1,1024]{1,0:T(1,128)}, u32[]{:S(2)}) copy-start(f32[1,1024]{1,0:T(1,128)} %slice.119) | copy-start | bytes 12292
  418.2 25.7 %copy-start.5 = (f32[2048,256]{1,0:T(8,128)S(1)}, f32[2048,256]{1,0:T(8,128)}, u32[]{:S(2)}) copy-start(f32[2048,256]{1,0:T(8,128)} %copy-done.4) | copy-start | bytes 6291460
  418.2 24.7 %collective-permute-start.17 = (f32[8,1024]{1,0:T(8,128)S(1)}, f32[8,1024]{1,0:T(8,128)S(1)}, u32[]{:S(2)}, u32[]{:S(2)}) collective-permute-start(f32[8,1024]{1,0:T(8,128)S(1)} %fusion.8), channel_id=1, source_target_pairs={{0,2},{1,3},{2,0},{3,1},{4,6},{5,7},{6,4},{7,5},{8,10},{9,11},{10,... | collective-permute-start | bytes 98312 | tf_op jit(solution)/shard_map/ppermute | solution.py:680
  442.9 24.7 %copy-start.6 = (f32[1024,256]{1,0:T(8,128)}, f32[1024,256]{1,0:T(8,128)S(1)}, u32[]{:S(2)}) copy-start(f32[1024,256]{1,0:T(8,128)S(1)} %fusion.3) | copy-start | bytes 3145732
  442.9 4.0 collective-permute-start.18
  446.9 4.7 collective-permute-start.19
  447.0 21.9 %collective-permute-start.28 = (bf16[512,256]{1,0:T(8,128)(2,1)S(1)}, bf16[512,256]{1,0:T(8,128)(2,1)S(1)}, u32[]{:S(2)}, u32[]{:S(2)}) collective-permute-start(bf16[512,256]{1,0:T(8,128)(2,1)S(1)} %dynamic-slice_convert_fusion.1), channel_id=1, source_target_pairs={{0,16},{4,20},{8,24},{12,28},{16,0},{20,4},{24,8},{28,12},{1,17},{... | collective-permute-start | bytes 786440 | tf_op jit(solution)/shard_map/ppermute | solution.py:686
  451.6 14.7 %collective-permute-start.20 = (f32[8,1024]{1,0:T(8,128)S(1)}, f32[8,1024]{1,0:T(8,128)S(1)}, u32[]{:S(2)}, u32[]{:S(2)}) collective-permute-start(f32[8,1024]{1,0:T(8,128)S(1)} %add.142), channel_id=1, source_target_pairs={{0,16},{4,20},{8,24},{12,28},{16,0},{20,4},{24,8},{28,12},{1,17},{... | collective-permute-start | bytes 98312 | tf_op jit(solution)/shard_map/ppermute | solution.py:686
  454.4 17.3 %collective-permute-start.22 = (bf16[512,256]{1,0:T(8,128)(2,1)S(1)}, bf16[512,256]{1,0:T(8,128)(2,1)S(1)}, u32[]{:S(2)}, u32[]{:S(2)}) collective-permute-start(bf16[512,256]{1,0:T(8,128)(2,1)S(1)} %dynamic-slice_convert_fusion.2), channel_id=1, source_target_pairs={{0,8},{4,12},{8,0},{12,4},{16,24},{20,28},{24,16},{28,20},{1,9},{5... | collective-permute-start | bytes 786440 | tf_op jit(solution)/shard_map/ppermute | solution.py:686
  470.0 5.0 collective-permute-start.29
  471.8 7.2 %collective-permute-start.23 = (bf16[256,256]{1,0:T(8,128)(2,1)S(1)}, bf16[256,256]{1,0:T(8,128)(2,1)S(1)}, u32[]{:S(2)}, u32[]{:S(2)}) collective-permute-start(bf16[256,256]{1,0:T(8,128)(2,1)S(1)} %dynamic-slice_convert_fusion.4), channel_id=1, source_target_pairs={{0,16},{4,20},{8,24},{12,28},{16,0},{20,4},{24,8},{28,12},{1,17},{... | collective-permute-start | bytes 393224 | tf_op jit(solution)/shard_map/ppermute | solution.py:686
  475.0 5.0 collective-permute-start.30
  479.1 14.0 %collective-permute-start.24 = (bf16[256,256]{1,0:T(8,128)(2,1)S(1)}, bf16[256,256]{1,0:T(8,128)(2,1)S(1)}, u32[]{:S(2)}, u32[]{:S(2)}) collective-permute-start(bf16[256,256]{1,0:T(8,128)(2,1)S(1)} %add_convert_fusion.3), channel_id=1, source_target_pairs={{0,16},{4,20},{8,24},{12,28},{16,0},{20,4},{24,8},{28,12},{1,17},{... | collective-permute-start | bytes 393224 | tf_op jit(solution)/shard_map/ppermute | solution.py:686
  480.1 18.5 %collective-permute-start.31 = (bf16[512,256]{1,0:T(8,128)(2,1)S(1)}, bf16[512,256]{1,0:T(8,128)(2,1)S(1)}, u32[]{:S(2)}, u32[]{:S(2)}) collective-permute-start(bf16[512,256]{1,0:T(8,128)(2,1)S(1)} %pad_maximum_fusion.5), channel_id=1, source_target_pairs={{0,16},{4,20},{8,24},{12,28},{16,0},{20,4},{24,8},{28,12},{1,17},{... | collective-permute-start | bytes 786440 | tf_op jit(solution)/shard_map/ppermute | solution.py:686
  493.1 11.2 %collective-permute-start.25 = (bf16[512,256]{1,0:T(8,128)(2,1)S(1)}, bf16[512,256]{1,0:T(8,128)(2,1)S(1)}, u32[]{:S(2)}, u32[]{:S(2)}) collective-permute-start(bf16[512,256]{1,0:T(8,128)(2,1)S(1)} %pad_maximum_fusion.4), channel_id=1, source_target_pairs={{0,8},{4,12},{8,0},{12,4},{16,24},{20,28},{24,16},{28,20},{1,9},{5... | collective-permute-start | bytes 786440 | tf_op jit(solution)/shard_map/ppermute | solution.py:686
  498.8 16.6 %collective-permute-start.32 = (bf16[1024,256]{1,0:T(8,128)(2,1)S(1)}, bf16[1024,256]{1,0:T(8,128)(2,1)S(1)}, u32[]{:S(2)}, u32[]{:S(2)}) collective-permute-start(bf16[1024,256]{1,0:T(8,128)(2,1)S(1)} %pad_maximum_fusion.3), channel_id=1, source_target_pairs={{0,8},{4,12},{8,0},{12,4},{16,24},{20,28},{24,16},{28,20},{1,9},{5... | collective-permute-start | bytes 1572872 | tf_op jit(solution)/shard_map/ppermute | solution.py:686
  504.4 13.8 %collective-permute-start.26 = (bf16[1024,256]{1,0:T(8,128)(2,1)S(1)}, bf16[1024,256]{1,0:T(8,128)(2,1)S(1)}, u32[]{:S(2)}, u32[]{:S(2)}) collective-permute-start(bf16[1024,256]{1,0:T(8,128)(2,1)S(1)} %pad_maximum_fusion.1), channel_id=1, source_target_pairs={{0,4},{4,0},{8,12},{12,8},{16,20},{20,16},{24,28},{28,24},{1,5},{5... | collective-permute-start | bytes 1572872 | tf_op jit(solution)/shard_map/ppermute | solution.py:686
  (20 other events, 80.0 us)
Sparse Core Ops, SparseCore 0:
  37.0 74.8 all-gather.1
  288.4 167.7 all-reduce.2

commit v3 on v2

--- a/solution.py
+++ b/solution.py
@@ -38,7 +38,7 @@
     return pl.BlockSpec(memory_space=pltpu.SMEM)
 
 
-def call(kernel, name, grid, in_specs, out_specs, out_shape, scratch=(), flops=0, nbytes=0, exps=0, weight=1e-6):
+def call(kernel, name, grid, in_specs, out_specs, out_shape, scratch=(), flops=0, nbytes=0, exps=0, weight=1e-6, aliases=None):
     return pl.pallas_call(
         kernel,
         name=name,
@@ -47,6 +47,7 @@
         out_specs=out_specs,
         out_shape=out_shape,
         scratch_shapes=list(scratch),
+        input_output_aliases=aliases or {},
         compiler_params=pltpu.CompilerParams(vmem_limit_bytes=VMEM_BYTES),
         cost_estimate=pl.CostEstimate(
             flops=int(flops * weight), bytes_accessed=int(nbytes * weight), transcendentals=int(exps * weight)
@@ -90,13 +91,13 @@
     )
 
 
-def add_rows(ref, rows, first):
+def add_rows(ref, rows, first, start):
     @pl.when(first)
     def _():
         ref[...] = jnp.zeros_like(ref)
 
     for place, row in enumerate(rows):
-        ref[place : place + 1, :] += row
+        ref[start + place : start + place + 1, :] += row
 
 
 def first_norm(tokens, out_grad, params, scal):
@@ -131,86 +132,84 @@
     return jnp.where(pl.program_id(0) < count, own_ref[...], other_ref[...])
 
 
-def project(norm_own, norm_other, weight, bias):
-    rows, width = norm_own.shape
+def project(norm, weight, bias, earlier=None):
+    rows, width = norm.shape
     cols = weight.shape[2]
     block = 512
-    count = rows // block
-
-    def kernel(own_ref, other_ref, w_ref, b_ref, q_ref, k_ref, v_ref):
-        x = pick(count, own_ref, other_ref)
+    start = 0 if earlier is None else rows // block
+    skip = 0 if earlier is None else 3
+
+    def kernel(x_ref, w_ref, b_ref, *refs):
+        q_ref, k_ref, v_ref = refs[skip:]
+        x = x_ref[...]
         q_ref[...] = (dot(x, w_ref[0]) + b_ref[0:1, :]).astype(bf16)
         k_ref[...] = dot(x, w_ref[1]).astype(bf16)
         v_ref[...] = (dot(x, w_ref[2]) + b_ref[1:2, :]).astype(bf16)
 
-    out = pl.BlockSpec((block, cols), lambda i: (i, 0))
+    out = pl.BlockSpec((block, cols), lambda i: (i + start, 0))
     return call(
         kernel,
         "project",
-        (2 * count,),
-        [*halves(block, width, count), whole(weight), whole(bias)],
+        (rows // block,),
+        [pl.BlockSpec((block, width), lambda i: (i, 0)), whole(weight), whole(bias)]
+        + [pl.BlockSpec(memory_space=pl.ANY)] * skip,
         [out] * 3,
         [shape((2 * rows, cols), bf16)] * 3,
-        flops=12 * rows * width * cols,
-        nbytes=4 * rows * width + 6 * width * cols + 12 * rows * cols,
-    )(norm_own, norm_other, weight, bias)
+        flops=6 * rows * width * cols,
+        nbytes=2 * rows * width + 6 * width * cols + 6 * rows * cols,
+        weight=1000,
+        aliases={3 + k: k for k in range(skip)},
+    )(norm, weight, bias, *(earlier or ()))
 
 
 def attend_forward(queries, keys, values):
     rows, width = queries.shape
-    block = min(1024, rows)
-    chunk = 256
-    steps = rows // chunk
-
-    def kernel(q_ref, k_ref, v_ref, o_ref, ot_ref, lse_ref, k_two, v_turned):
-        @pl.when(pl.program_id(1) == 0)
-        def _():
-            k = k_ref[...]
-            lane = lax.broadcasted_iota(jnp.int32, k.shape, 1)
-            rolled = pltpu.roll(k.astype(f32), HEAD_DIM, 1).astype(bf16)
-            k_two[0] = jnp.where(lane < HEAD_DIM, k, rolled)
-            k_two[1] = jnp.where(lane < HEAD_DIM, rolled, k)
-            turned = v_ref[...].astype(f32).T
-            ones = jnp.ones((HEAD_DIM, rows), bf16)
-            v_turned[0] = jnp.concatenate([turned[:HEAD_DIM].astype(bf16), ones], 0)
-            v_turned[1] = jnp.concatenate([ones, turned[HEAD_DIM:].astype(bf16)], 0)
-
+    chunk = min(512, rows)
+
+    def kernel(q_ref, k_ref, v_ref, o_ref, ot_ref, lse_ref):
+        k = k_ref[...]
+        lane = lax.broadcasted_iota(jnp.int32, k.shape, 1)
+        rolled = pltpu.roll(k.astype(f32), HEAD_DIM, 1).astype(bf16)
+        turned = v_ref[...].astype(f32).T
+        ones = jnp.ones((HEAD_DIM, rows), bf16)
         q_turned = q_ref[...].astype(f32).T * (SCALE * LOG2E)
         outs = []
         for head in range(2):
             at = head * HEAD_DIM
+            k_two = jnp.where(lane < HEAD_DIM, k, rolled) if head == 0 else jnp.where(lane < HEAD_DIM, rolled, k)
+            own = turned[at : at + HEAD_DIM].astype(bf16)
+            v_turned = jnp.concatenate([own, ones] if head == 0 else [ones, own], 0)
             q_two = jnp.concatenate(split_two(q_turned[at : at + HEAD_DIM]), 0)
-            scores = [dot(k_two[head, pl.ds(j * chunk, chunk), :], q_two) for j in range(steps)]
-            peak = None
-            for part in scores:
-                top = part.reshape(chunk // 8, 8, block).max(axis=0)
-                peak = top if peak is None else jnp.maximum(peak, top)
-            peak = jnp.max(peak, axis=0, keepdims=True)
-            total = None
-            for j in range(steps):
-                weights = jnp.exp2(scores[j] - peak).astype(bf16)
-                part = dot(v_turned[head, :, pl.ds(j * chunk, chunk)], weights)
-                total = part if total is None else total + part
+            total = peak = None
+            for j in range(rows // chunk):
+                part = slice(j * chunk, (j + 1) * chunk)
+                scores = dot(k_two[part], q_two)
+                top = jnp.max(scores.reshape(chunk // 8, 8, rows).max(axis=0), axis=0, keepdims=True)
+                higher = top if peak is None else jnp.maximum(peak, top)
+                weights = jnp.exp2(scores - higher).astype(bf16)
+                add = dot(v_turned[:, part], weights)
+                total = add if total is None else total * jnp.exp2(peak - higher) + add
+                peak = higher
             row_sum = total[HEAD_DIM - at : HEAD_DIM - at + 1]
             outs.append(total[at : at + HEAD_DIM] / row_sum)
             lse_ref[head : head + 1, :] = peak + jnp.log2(row_sum)
-        turned = jnp.concatenate(outs, 0)
-        ot_ref[...] = turned
-        o_ref[...] = turned.T.astype(bf16)
-
-    by_query = pl.BlockSpec((block, LANES), lambda j, i: (i, j))
-    by_key = pl.BlockSpec((rows, LANES), lambda j, i: (0, j))
-    turned_spec = pl.BlockSpec((LANES, block), lambda j, i: (j, i))
-    stat_spec = pl.BlockSpec((None, 8, block), lambda j, i: (j, 0, i))
+        attended = jnp.concatenate(outs, 0)
+        ot_ref[...] = attended
+        o_ref[...] = attended.T.astype(bf16)
+
+    by_pair = pl.BlockSpec((rows, LANES), lambda j: (0, j))
     pairs = width // LANES
     return call(
         kernel,
         "attend_forward",
-        (pairs, rows // block),
-        [by_query, by_key, by_key],
-        [by_query, turned_spec, stat_spec],
+        (pairs,),
+        [by_pair] * 3,
+        [
+            by_pair,
+            pl.BlockSpec((LANES, rows), lambda j: (j, 0)),
+            pl.BlockSpec((None, 8, rows), lambda j: (j, 0, 0)),
+        ],
         [shape((rows, width), bf16), shape((width, rows), f32), shape((pairs, 8, rows), f32)],
-        [pltpu.VMEM((2, rows, LANES), bf16), pltpu.VMEM((2, LANES, rows), bf16)],
         flops=16 * rows * rows * width,
         nbytes=12 * rows * width,
         exps=rows * rows * width // HEAD_DIM,
@@ -218,15 +217,15 @@
     )(queries, keys, values)
 
 
-def attend_backward(queries, keys, values, out_grad, out_turned, stats, pair):
+def attend_backward(queries, keys, values, grad_own, grad_other, out_turned, stats, first, pairs):
     rows = queries.shape[0]
-    width = LANES
-    block = min(1024, rows)
+    width = LANES * pairs
+    block = grad_own.shape[0]
     chunk = 256
     count = rows // block
 
     def kernel(
-        q_ref, k_ref, v_ref, g_ref, ot_ref, lse_ref, dq_ref, dk_ref, dv_ref, sum_ref,
+        q_ref, k_ref, v_ref, go_ref, gt_ref, ot_ref, lse_ref, dq_ref, dk_ref, dv_ref, sum_ref,
         k_wide, k_turned, v_wide, dk_acc, dv_acc,
     ):
         i = pl.program_id(1)
@@ -252,7 +251,7 @@
         q_turned = q_ref[...].astype(f32).T
         q_low = q_turned.astype(bf16)
         q_turned = q_turned * (SCALE * LOG2E)
-        g_turned = g_ref[...].astype(f32).T
+        g_turned = jnp.where(i == 0, go_ref[...], gt_ref[...]).astype(f32).T
         g_low = g_turned.astype(bf16)
         dqs = []
         for head in range(2):
@@ -285,18 +284,19 @@
             dv_ref[...] = dv.astype(bf16)
             sum_ref[1:2, :] = jnp.sum(dv, axis=0, keepdims=True)
 
-    by_query = pl.BlockSpec((block, LANES), lambda j, i: (i, pair))
-    by_key = pl.BlockSpec((rows, LANES), lambda j, i: (0, pair))
-    turned_spec = pl.BlockSpec((LANES, block), lambda j, i: (pair, i))
-    stat_spec = pl.BlockSpec((None, 8, block), lambda j, i: (pair, 0, i))
-    query_out = pl.BlockSpec((block, LANES), lambda j, i: (i, 0))
-    key_out = pl.BlockSpec((rows, LANES), lambda j, i: (0, 0))
-    sum_spec = pl.BlockSpec((8, LANES), lambda j, i: (0, 0))
+    by_query = pl.BlockSpec((block, LANES), lambda j, i: (i, j + first))
+    by_key = pl.BlockSpec((rows, LANES), lambda j, i: (0, j + first))
+    half = pl.BlockSpec((block, LANES), lambda j, i: (0, j + first))
+    turned_spec = pl.BlockSpec((LANES, block), lambda j, i: (j + first, i))
+    stat_spec = pl.BlockSpec((None, 8, block), lambda j, i: (j + first, 0, i))
+    query_out = pl.BlockSpec((block, LANES), lambda j, i: (i, j))
+    key_out = pl.BlockSpec((rows, LANES), lambda j, i: (0, j))
+    sum_spec = pl.BlockSpec((8, LANES), lambda j, i: (0, j))
     return call(
         kernel,
         "attend_backward",
-        (1, count),
-        [by_query, by_key, by_key, by_query, turned_spec, stat_spec],
+        (pairs, count),
+        [by_query, by_key, by_key, half, half, turned_spec, stat_spec],
         [query_out, key_out, key_out, sum_spec],
         [shape((rows, width), bf16)] * 3 + [shape((8, width), f32)],
         [
@@ -310,43 +310,22 @@
         nbytes=20 * rows * width,
         exps=rows * rows * width // HEAD_DIM,
         weight=1000,
-    )(queries, keys, values, out_grad, out_turned, stats)
-
-
-def output_other(first, second, weight_one, weight_two):
-    total, cols = first.shape
-    rows = total // 2
-    width = weight_one.shape[1]
-    block = 512
-    count = rows // block
-
-    def kernel(a_ref, b_ref, wa_ref, wb_ref, out_ref):
-        out_ref[...] = (dot(a_ref[...], wa_ref[...]) + dot(b_ref[...], wb_ref[...])).astype(bf16)
-
-    spec = pl.BlockSpec((block, cols), lambda i: (i + count, 0))
-    return call(
-        kernel,
-        "output_other",
-        (count,),
-        [spec, spec, whole(weight_one), whole(weight_two)],
-        pl.BlockSpec((block, width), lambda i: (i, 0)),
-        shape((rows, width), bf16),
-        flops=4 * rows * cols * width,
-        nbytes=4 * rows * cols + 2 * rows * width,
-    )(first, second, weight_one, weight_two)
-
-
-def output_own(tokens, first, second, weight_one, weight_two, received, params):
+    )(queries, keys, values, grad_own, grad_other, out_turned, stats)
+
+
+def output_own(tokens, attended, weights, params):
     rows, width = tokens.shape
-    cols = first.shape[1]
+    cols = weights[0].shape[0]
     block = 256
-
-    def kernel(t_ref, a_ref, b_ref, wa_ref, wb_ref, r_ref, par_ref, mid_ref, norm_ref):
-        middle = (
-            t_ref[...].astype(f32)
-            + (dot(a_ref[...], wa_ref[...]) + dot(b_ref[...], wb_ref[...]) + r_ref[...].astype(f32))
-            + par_ref[2:3, :]
-        )
+    many = len(attended)
+
+    def kernel(t_ref, par_ref, *refs):
+        total = None
+        for a_ref, w_ref in zip(refs[:many], refs[many : 2 * many], strict=True):
+            part = dot(a_ref[...], w_ref[...])
+            total = part if total is None else total + part
+        mid_ref, norm_ref = refs[2 * many :]
+        middle = t_ref[...].astype(f32) + total + par_ref[2:3, :]
         mid_ref[...] = middle
         unit, _ = normalize(middle)
         norm_ref[...] = (unit * par_ref[3:4, :] + par_ref[4:5, :]).astype(bf16)
@@ -357,21 +336,22 @@
         kernel,
         "output_own",
         (rows // block,),
-        [spec, thin, thin, whole(weight_one), whole(weight_two), spec, whole(params)],
+        [spec, whole(params)] + [thin] * many + [whole(w) for w in weights],
         [spec, spec],
         [shape((rows, width), f32), shape((rows, width), bf16)],
-        flops=4 * rows * cols * width,
-        nbytes=4 * rows * cols + 10 * rows * width,
-    )(tokens, first, second, weight_one, weight_two, received, params)
-
-
-def feed_forward(norm_own, norm_other, cot_own, cot_other, bias, both_weights, scal, earlier=None):
+        flops=2 * rows * many * cols * width,
+        nbytes=2 * rows * many * cols + 8 * rows * width,
+    )(tokens, params, *attended, *weights)
+
+
+def feed_forward(norm_own, norm_other, cot_own, cot_other, bias, up, down, scal, earlier=None):
     rows, width = norm_own.shape
     hidden = bias.shape[1]
     block = 256
     count = rows // block
     last = earlier is not None
-    slices, depth = both_weights.shape[0], both_weights.shape[2]
+    (up, up_place), (down, down_place) = up, down
+    slices, depth = up.shape[0], up.shape[2]
     term_type = bf16
 
     def kernel(scal_ref, no_ref, nt_ref, co_ref, ct_ref, b_ref, up_ref, dn_ref, *refs):
@@ -390,17 +370,17 @@
 
         x = pick(count, no_ref, nt_ref)
         cot = pick(count, co_ref, ct_ref)
-        up = up_ref[...].reshape(width, hidden)
-        down = dn_ref[...].reshape(hidden, width)
-        h = dot(x, up) + b_ref[0:1, :]
+        up_now = up_ref[...].reshape(width, hidden)
+        down_now = dn_ref[...].reshape(hidden, width)
+        h = dot(x, up_now) + b_ref[0:1, :]
         cdf = 0.5 * (1.0 + lax.erf(h * RSQRT2))
         act = (h * cdf).astype(bf16)
         slope = cdf + h * (RSQRT2PI * jnp.exp(-0.5 * h * h))
-        ff = dot(act, down)
-        grad = dot(cot, down, NT) * slope
-        sum_ref[0:1, :] += jnp.sum(grad, axis=0, keepdims=True)
+        ff = dot(act, down_now)
+        grad = dot(cot, down_now, NT) * slope
+        sum_ref[7:8, :] += jnp.sum(grad, axis=0, keepdims=True)
         low = grad.astype(bf16)
-        ng = dot(low, up, NT)
+        ng = dot(low, up_now, NT)
         up_acc[...] += dot(x, low, TN)
         down_acc[...] += dot(act, cot, TN)
         if last:
@@ -433,10 +413,10 @@
         pl.BlockSpec(
             (slices, None, depth, width), lambda i, j=j: (0, j, 0, 0), pipeline_mode=pl.Buffered(1)
         )
-        for j in range(2)
+        for j in (up_place, down_place)
     )
     ins = [scalars(), own, other, own, other, whole(bias), up_spec, down_spec]
-    args = [scal, norm_own, norm_other, cot_own, cot_other, bias, both_weights, both_weights]
+    args = [scal, norm_own, norm_other, cot_own, cot_other, bias, up, down]
     if last:
         ins += [every, every]
         args += list(earlier)
@@ -476,7 +456,7 @@
         out_ref[...] = out
         low_ref[...] = out.astype(bf16)
         sums = [jnp.sum(v, axis=0, keepdims=True) for v in (grad * unit, grad, out, cot)]
-        add_rows(sum_ref, sums, i == 0)
+        add_rows(sum_ref, sums, i == 0, 2)
 
         @pl.when(i == last)
         def _():
@@ -496,54 +476,59 @@
     )(scal, middle, grad_own, grad_received, cot, params)
 
 
-def output_back(low_own, low_other, first, second, weight_one, weight_two, scal):
-    rows, width = low_own.shape
-    cols = first.shape[1]
+def output_back(low, attended, weights, scal, earlier=None):
+    rows, width = low.shape
+    cols = weights[0].shape[0]
     block = 512
-    count = rows // block
-
-    def kernel(
-        scal_ref, lo_ref, lt_ref, a_ref, b_ref, wa_ref, wb_ref,
-        ga_ref, gb_ref, ta_ref, tb_ref, acc_a, acc_b,
-    ):
+    last = earlier is not None
+    start = rows // block if last else 0
+
+    def kernel(scal_ref, low_ref, a_ref, b_ref, wa_ref, wb_ref, *refs):
+        before = refs[:2] if last else (None, None)
+        ga_ref, gb_ref, ta_ref, tb_ref, acc_a, acc_b = refs[2 if last else 0 :]
         i = pl.program_id(0)
-
-        @pl.when(i == 0)
+        now = low_ref[...]
+        ga_ref[...] = dot(now, wa_ref[...], NT).astype(bf16)
+        gb_ref[...] = dot(now, wb_ref[...], NT).astype(bf16)
+        for acc, rows_ref, old in ((acc_a, a_ref, before[0]), (acc_b, b_ref, before[1])):
+
+            @pl.when(i == 0)
+            def _():
+                acc[...] = jnp.zeros_like(acc) if old is None else old[...]
+
+            acc[...] += dot(rows_ref[...], now, TN)
+
+        @pl.when(i == rows // block - 1)
         def _():
-            acc_a[...] = jnp.zeros_like(acc_a)
-            acc_b[...] = jnp.zeros_like(acc_b)
-
-        low = pick(count, lo_ref, lt_ref)
-        ga_ref[...] = dot(low, wa_ref[...], NT).astype(bf16)
-        gb_ref[...] = dot(low, wb_ref[...], NT).astype(bf16)
-        acc_a[...] += dot(a_ref[...], low, TN)
-        acc_b[...] += dot(b_ref[...], low, TN)
-
-        @pl.when(i == 2 * count - 1)
-        def _():
-            ta_ref[...] = (acc_a[...] * scal_ref[1]).astype(bf16)
-            tb_ref[...] = (acc_b[...] * scal_ref[1]).astype(bf16)
-
-    own, other = halves(block, width, count)
+            factor = scal_ref[1] if last else 1.0
+            ta_ref[...] = (acc_a[...] * factor).astype(ta_ref.dtype)
+            tb_ref[...] = (acc_b[...] * factor).astype(tb_ref.dtype)
+
     thin = pl.BlockSpec((block, cols), lambda i: (i, 0))
-    terms = [shape((cols, width), bf16)] * 2
+    rows_in = pl.BlockSpec((block, cols), lambda i: (i + start, 0))
+    terms = [shape((cols, width), bf16 if last else f32)] * 2
+    before = list(earlier or ())
     return call(
         kernel,
         "output_back",
-        (2 * count,),
-        [scalars(), own, other, thin, thin, whole(weight_one), whole(weight_two)],
+        (rows // block,),
+        [scalars(), pl.BlockSpec((block, width), lambda i: (i, 0)), rows_in, rows_in]
+        + [whole(w) for w in weights]
+        + [whole(t) for t in before],
         [thin, thin, whole(terms[0]), whole(terms[1])],
-        [shape((2 * rows, cols), bf16)] * 2 + terms,
+        [shape((rows, cols), bf16)] * 2 + terms,
         [pltpu.VMEM((cols, width), f32)] * 2,
-        flops=16 * rows * width * cols,
-        nbytes=4 * rows * width + 16 * rows * cols,
-    )(scal, low_own, low_other, first, second, weight_one, weight_two)
-
-
-def input_term(norm_own, norm_other, pairs, scal):
+        flops=8 * rows * width * cols,
+        nbytes=2 * rows * width + 8 * rows * cols,
+        weight=1e-6 if last else 1000,
+    )(scal, low, *attended, *weights, *before)
+
+
+def input_term(norm_own, norm_other, parts, scal, other=None):
     rows, width = norm_own.shape
-    count = len(pairs)
-    grads = [pair[j] for j in range(3) for pair in pairs]
+    count = len(parts)
+    grads = [part[j] for j in range(3) for part in parts]
+    more = [] if other is None else [other]
 
     def kernel(scal_ref, no_ref, nt_ref, *refs):
         out_ref = refs[-1]
@@ -553,27 +538,31 @@
             def _():
                 grad = jnp.concatenate([r[...] for r in refs[count * j : count * j + count]], 1)
                 term = dot(no_ref[...], grad[:rows, :], TN) + dot(nt_ref[...], grad[rows:, :], TN)
-                out_ref[...] = (term * scal_ref[1]).astype(bf16)
-
-    cols = count * LANES
+                term = term * scal_ref[1]
+                if more:
+                    term = term + refs[-2][...].astype(f32)
+                out_ref[...] = term.astype(bf16)
+
+    cols = sum(part[0].shape[1] for part in parts)
+    out_spec = pl.BlockSpec((width, cols), lambda j: (j, 0))
     return call(
         kernel,
         "input_term",
         (3,),
-        [scalars(), whole(norm_own), whole(norm_other)] + [whole(g) for g in grads],
-        pl.BlockSpec((width, cols), lambda j: (j, 0)),
+        [scalars(), whole(norm_own), whole(norm_other)]
+        + [whole(g) for g in grads]
+        + [out_spec] * len(more),
+        out_spec,
         shape((3 * width, cols), bf16),
         flops=12 * rows * width * cols,
         nbytes=4 * rows * width + 12 * rows * cols + 12 * width * cols,
-    )(scal, norm_own, norm_other, *grads)
-
-
-def norm1_part(refs, weights):
+    )(scal, norm_own, norm_other, *grads, *more)
+
+
+def norm1_part(refs, weights, counts):
     total = None
     place = 0
-    for w_ref in weights:
-        cols = w_ref.shape[2]
-        count = cols // LANES
+    for w_ref, count in zip(weights, counts, strict=True):
         for j in range(3):
             grad = jnp.concatenate([r[...] for r in refs[place : place + count]], 1)
             part = dot(grad, w_ref[j], NT)
@@ -583,7 +572,11 @@
 
 
 def flat(quarters):
-    return [pair[j] for pairs in quarters for j in range(3) for pair in pairs]
+    return [part[j] for parts in quarters for j in range(3) for part in parts]
+
+
+def row_specs(grads, block, start):
+    return [pl.BlockSpec((block, g.shape[1]), lambda i: (i + start, 0)) for g in grads]
 
 
 def norm1_other(quarters, weights):
@@ -591,18 +584,17 @@
     rows = grads[0].shape[0] // 2
     width, cols = weights[0].shape[1:]
     block = 256
-    start = rows // block
     many = len(grads)
+    counts = [len(parts) for parts in quarters]
 
     def kernel(*refs):
-        refs[-1][...] = norm1_part(refs[:many], refs[many:-1]).astype(bf16)
-
-    thin = pl.BlockSpec((block, LANES), lambda i: (i + start, 0))
+        refs[-1][...] = norm1_part(refs[:many], refs[many:-1], counts).astype(bf16)
+
     return call(
         kernel,
         "first_other",
         (rows // block,),
-        [thin] * many + [whole(w) for w in weights],
+        row_specs(grads, block, rows // block) + [whole(w) for w in weights],
         pl.BlockSpec((block, width), lambda i: (i, 0)),
         shape((rows, width), bf16),
         flops=12 * rows * width * cols,
@@ -617,30 +609,34 @@
     block = 256
     last = rows // block - 1
     many = len(grads)
+    counts = [len(parts) for parts in quarters]
 
     def kernel(scal_ref, *refs):
         rec_ref, tok_ref, mid_ref, par_ref, out_ref, sum_ref = refs[many + len(weights) :]
         i = pl.program_id(0)
-        grad = norm1_part(refs[:many], refs[many : many + len(weights)])
+        grad = norm1_part(refs[:many], refs[many : many + len(weights)], counts)
         grad += rec_ref[...].astype(f32)
         unit, inverse = normalize(tok_ref[...].astype(f32))
         out = mid_ref[...] + norm_back(grad, par_ref[0:1, :], unit, inverse)
         out_ref[...] = out.astype(bf16)
         sums = [jnp.sum(v, axis=0, keepdims=True) for v in (grad * unit, grad)]
-        add_rows(sum_ref, sums, i == 0)
+        add_rows(sum_ref, sums, i == 0, 0)
 
         @pl.when(i == last)
         def _():
             sum_ref[...] = sum_ref[...] * scal_ref[1]
 
-    thin = pl.BlockSpec((block, LANES), lambda i: (i, 0))
     spec = pl.BlockSpec((block, width), lambda i: (i, 0))
     sums = shape((8, width), f32)
     return call(
         kernel,
         "first_own",
         (rows // block,),
-        [scalars()] + [thin] * many + [whole(w) for w in weights] + [spec] * 3 + [whole(params)],
+        [scalars()]
+        + row_specs(grads, block, 0)
+        + [whole(w) for w in weights]
+        + [spec] * 3
+        + [whole(params)],
         [spec, whole(sums)],
         [shape((rows, width), bf16), sums],
         flops=12 * rows * width * cols,
@@ -669,7 +665,7 @@
 ):
     shard_count = lax.axis_size("mp")
     groups = lax.axis_size("dp")
-    width = tokens.shape[1]
+    rows, width = tokens.shape
     cols = input_weight.shape[2]
     hidden = up_weight.shape[1]
 
@@ -714,28 +710,35 @@
     normed1_t = core_swap(normed1)
     cot_t = core_swap(cot)
 
-    qkv_one = project(normed1, normed1_t, input_weight, input_bias)
+    qkv_one = project(normed1, input_weight, input_bias)
+    qkv_one = project(normed1_t, input_weight, after(input_bias, qkv_one[0]), qkv_one)
     att_one, turned_one, stat_one = attend_forward(*qkv_one)
+    att_one_t = core_swap(att_one[rows:])
+    wo_one_t = core_swap(output_weight)
     bias_two = bias_two.reshape(-1)
     up_bias_one = up_bias.reshape(1, hidden)
     up_bias_two = bias_two[:hidden].reshape(1, hidden)
     in_bias_two = bias_two[hidden:].reshape(2, cols)
-    qkv_two = project(after(normed1, att_one), normed1_t, wi_two, in_bias_two)
+    qkv_two = project(after(normed1, att_one), wi_two, in_bias_two)
+    qkv_two = project(normed1_t, wi_two, after(in_bias_two, att_one_t), qkv_two)
     att_two, turned_two, stat_two = attend_forward(*qkv_two)
-
-    other_part = core_swap(output_other(att_one, after(att_two, ff_weights_two), output_weight, wo_two))
+    wo_two_t = core_swap(after(wo_two, qkv_two[0]))
+    att_two_t = core_swap(att_two[rows:])
     middle, normed2 = output_own(
-        tokens, att_one, att_two, output_weight, wo_two, other_part, params
+        tokens,
+        [att_one, att_two, att_one_t, after(att_two_t, ff_weights_two)],
+        [output_weight, wo_two, wo_one_t, wo_two_t],
+        params,
     )
     normed2_t = core_swap(normed2)
 
     ff_two, ng_two, up_two_term, down_two_term, up_sum_two = feed_forward(
-        normed2, normed2_t, cot, cot_t, up_bias_two, ff_weights_two, scal
+        normed2, normed2_t, cot, cot_t, up_bias_two, (ff_weights_two, 0), (ff_weights_two, 1), scal
     )
     up_received = chip_swap(up_two_term)
-    ff_weights = jnp.stack([w.reshape(1, -1, width) for w in (up_weight, down_weight)], 1)
+    up_one, down_one = ((w.reshape(1, 1, -1, width), 0) for w in (up_weight, down_weight))
     ff_own, ng_own, ff_send, ng_send, up_one_term, down_one_term, up_sum_one = feed_forward(
-        normed2, normed2_t, cot, cot_t, up_bias_one, ff_weights, scal, (ff_two, ng_two)
+        normed2, normed2_t, cot, cot_t, up_bias_one, up_one, down_one, scal, (ff_two, ng_two)
     )
     ng_received = core_swap(ng_send)
     down_received = chip_swap(after(down_two_term, up_received))
@@ -743,48 +746,34 @@
         middle, ng_own, after(ng_received, up_received), cot, params, scal
     )
     middle_low_t = core_swap(middle_low)
-    g_one, g_two, wo_one_term, wo_two_term = output_back(
-        middle_low, middle_low_t, att_one, att_two, output_weight, wo_two, scal
-    )
-
-    def pairs_back(qkv, grad, turned, stat, begin, between):
-        pairs = []
-        waits = begin
-        for pair in range(cols // LANES):
-            pairs.append(attend_backward(*qkv, after(grad, *waits), turned, stat, pair))
-            waits = [pairs[-1][0], *between(pair, pairs[-1])]
-        return pairs
+    out_weights = [output_weight, wo_two]
+    g_one, g_two, *wo_terms = output_back(middle_low, [att_one, att_two], out_weights, scal)
+    g_one_t, g_two_t, wo_one_term, wo_two_term = output_back(
+        middle_low_t, [att_one, att_two], out_weights, scal, wo_terms
+    )
 
     def both(own, received, *last):
-        return own.astype(f32) + after(received, *last).astype(f32)
-
-    sums = []
-
-    def between_two(pair, outs):
-        if pair > 0:
-            return []
-        up_both = both(up_one_term, up_received, outs[0]).astype(bf16)
-        down_both = both(down_one_term, down_received, outs[0]).astype(bf16)
-        sums.extend(lax.psum((up_both, down_both), "dp"))
-        return [up_both, down_both]
-
-    pairs_two = pairs_back(qkv_two, g_two, turned_two, stat_two, [], between_two)
-    up_sum, down_sum = sums
-    wi_two_term = input_term(normed1, normed1_t, pairs_two, scal)
-    ff_received = core_swap(after(ff_send, pairs_two[0][0]))
-    wo_received = chip_swap(after(wo_two_term, pairs_two[0][0]))
+        return (own.astype(f32) + after(received, *last).astype(f32)).astype(bf16)
+
+    parts_two = [attend_backward(*qkv_two, g_two, g_two_t, turned_two, stat_two, 0, 1)]
+    wait = parts_two[0][0]
+    up_both = both(up_one_term, up_received, wait)
+    down_both = both(down_one_term, down_received, wait)
+    up_sum, down_sum = lax.psum((up_both, down_both), "dp")
+    g_two = after(g_two, up_both, down_both, wait)
+    parts_two.append(attend_backward(*qkv_two, g_two, g_two_t, turned_two, stat_two, 1, cols // LANES - 1))
+    wi_two_term = input_term(normed1, normed1_t, parts_two, scal)
+    ff_received = core_swap(after(ff_send, wait))
+    wo_received = chip_swap(after(wo_two_term, parts_two[1][0]))
     wi_received = chip_swap(wi_two_term)
-    pairs_one = pairs_back(
-        qkv_one, g_one, turned_one, stat_one, [wi_two_term], lambda *_: [wo_received]
-    )
-
-    quarters = [pairs_one, pairs_two]
+    g_one = after(g_one, wi_two_term)
+    parts_one = [attend_backward(*qkv_one, g_one, g_one_t, turned_one, stat_one, 0, cols // LANES)]
+    wi_both = input_term(normed1, normed1_t, parts_one, scal, after(wi_received, wo_received))
+    quarters = [parts_one, parts_two]
     weights = [input_weight, wi_two]
-    ng1_send = norm1_other(quarters, [input_weight, after(wi_two, wi_received, wo_received)])
-    ng1_received = core_swap(ng1_send)
-    wi_one_term = input_term(after(normed1, ng1_send), normed1_t, pairs_one, scal)
+    ng1_received = core_swap(norm1_other(quarters, [input_weight, after(wi_two, wi_both)]))
     token_grad, first_sums = norm1_own(
-        quarters, weights, after(ng1_received, wi_one_term), tokens, middle_grad, params, scal
+        quarters, weights, ng1_received, tokens, middle_grad, params, scal
     )
     result = live * (middle + ff_own + ff_received.astype(f32) + down_bias)
     result = result.astype(bf16)
@@ -792,13 +781,11 @@
     def columns(term):
         return jnp.concatenate([term[:, k * cols : (k + 1) * cols] for k in range(width // cols)])
 
-    tail = jnp.concatenate(
-        [both(wi_one_term, wi_received), both(columns(wo_one_term), columns(wo_received))]
-    )
+    wo_both = columns(both(wo_one_term, wo_received))
+    middle_row = (wi_both.shape[0] + wo_both.shape[0]) // 2
+    parts = [wi_both[:middle_row], jnp.concatenate([wi_both[middle_row:], wo_both])]
     bits = [1 << k for k in range(groups.bit_length() - 1)]
     orders = [bits, bits[1:] + bits[:1]]
-    middle_row = tail.shape[0] // 2
-    parts = [tail[:middle_row], tail[middle_row:]]
 
     def upper(bit):
         return (group // bit) % 2
@@ -811,8 +798,7 @@
             half = parts[k].shape[0] // 2
             keep = lax.dynamic_slice_in_dim(parts[k], upper(bit) * half, half, 0)
             send = lax.dynamic_slice_in_dim(parts[k], (1 - upper(bit)) * half, half, 0)
-            parts[k] = keep + along(send.astype(bf16), bit).astype(f32)
-    parts = [part.astype(bf16) for part in parts]
+            parts[k] = both(keep, along(send, bit))
     for turn in reversed(range(len(bits))):
         for k in range(2):
             bit = orders[k][turn]
@@ -827,19 +813,16 @@
     wo_sum = tail_sum[wi_rows:].reshape(width // cols, cols, cols)
     wo_sum = jnp.concatenate([wo_sum[k] for k in range(width // cols)], 1)
 
-    def quarter_rows(pairs, up_sums):
-        sums_all = jnp.concatenate([pair[3] for pair in pairs], 1)
+    def quarter_rows(parts, up_sums):
+        sums_all = jnp.concatenate([part[3] for part in parts], 1)
         rest = jnp.full((1, width - 2 * cols), own_units)
         bias_row = jnp.concatenate([sums_all[0:1] * own_units, sums_all[1:2] * own_units, rest], 1)
-        return jnp.concatenate([bias_row, up_sums[:1]])
-
-    late = jnp.concatenate([first_sums[:2], second_sums[:4]])
+        return up_sums + jnp.pad(bias_row, ((6, 1), (0, 0)))
+
+    late = first_sums + second_sums
     late = late + core_swap(late)
-    late_one, late_two = (
-        jnp.concatenate([late, quarter_rows(pairs, up_sums)])
-        for pairs, up_sums in ((pairs_one, up_sum_one), (pairs_two, up_sum_two))
-    )
-    late = late_one + chip_swap(late_two)
+    late_one = late + quarter_rows(parts_one, up_sum_one)
+    late = late_one + chip_swap(late + quarter_rows(parts_two, up_sum_two))
     for bit in bits:
         late = late + along(late, bit)
     share = 2.0 / late[6, -1]

time: 537 us -> 485 us (0.903)
  waiting for transfers between devices: 109 us -> 90.6 us
  other arithmetic: 40.4 us -> 30.5 us
  starting transfers between devices: 35 us -> 27.3 us
  local copies, waits for them, and re-layouts: 19.4 us -> 13.1 us
    ppermute x9, waiting for transfers between devices: 33.8 us -> 18.3 us  [chip_swap(): return lax.ppermute(value, 'mp', [(i, i ^ 2) for i in range(shard_count)])]
    ppermute x15, starting transfers between devices: 20.3 us -> 13 us  [along(): return lax.ppermute(value, 'dp', [(i, i ^ bit) for i in range(groups)])]
    add x8 -> x3, other arithmetic: 6.23 us -> 0.79 us  [the longest x1 0.77 us: body(): late = first_sums + second_sums]
    pallas_call x13 -> x14, Pallas kernels: 203 us -> 198 us  [the longest x3 93.6 us: attend_backward(): call(kernel, 'attend_backward', (pairs, count), [by_query, by_key, by_key...]
  transfers between devices with their start and end apart: 35 -> 38, of which waited for: 17 -> 19; matrix products, arithmetic and copies ran while one was open for 8% -> 6% of each run, Pallas kernels for 48% -> 55%
where the time goes in v3:
time: 485 us; the launch traced here: 482 us
  Pallas kernels  302 us (62%)
  waiting for transfers between devices  90.6 us (19%)
  other arithmetic  30.5 us (6%)
  starting transfers between devices  27.3 us (6%)
  between operations  17.8 us (4%)
  local copies, waits for them, and re-layouts  13.1 us (3%)
    pallas_call x3, Pallas kernels, attend_backward(): call(kernel, 'attend_backward', (pairs, count), [by_query, by_key, by_key...  93.6 us
    pallas_call x2, Pallas kernels, feed_forward(): call(kernel, 'feed_forward', (2 * count,), ins, outs + [whole(terms[0]),...  72.7 us
    ppermute x15, waiting for transfers between devices, along(): return lax.ppermute(value, 'dp', [(i, i ^ bit) for i in range(groups)])  65.3 us
    pallas_call x2, Pallas kernels, attend_forward(): call(kernel, 'attend_forward', (pairs,), [by_pair] * 3, [by_pair, pl.Bloc...  45.8 us
    ppermute x9, waiting for transfers between devices, chip_swap(): return lax.ppermute(value, 'mp', [(i, i ^ 2) for i in range(shard_count)])  18.3 us
    pallas_call x4, Pallas kernels, project(): call(kernel, 'project', (rows // block,), [pl.BlockSpec((block, width), l...  18.2 us
    pallas_call x2, Pallas kernels, input_term(): call(kernel, 'input_term', (3,), [scalars(), whole(norm_own), whole(norm_...  16.7 us
    pallas_call x2, Pallas kernels, output_back(): call(kernel, 'output_back', (rows // block,), [scalars(), pl.BlockSpec((b...  14.2 us
  transfers between devices with their start and end apart: 38, of which 19 were waited for; matrix products, arithmetic and copies ran while one was open for 6% of the time, Pallas kernels for 55%

profile of v3, /device:TPU:0, one launch (start us, length us, event | category | flops | bytes accessed | tf_op | source)
XLA Modules:
  0.0 481.7 jit_solution(13417633397238645391)
XLA Ops:
  8.4 3.0 collective-permute-start.1
  15.4 5.4 %first_norm.1 = (bf16[1024,1024]{1,0:T(8,128)(2,1)}, bf16[1024,1024]{1,0:T(8,128)(2,1)}) custom-call(f32[2]{0:T(128)} %pad_maximum_fusion.4.scal_ref, bf16[1024,1024]{1,0:T(8,128)(2,1)} %refs_12_.1, bf16[1024,1024]{1,0:T(8,128)(2,1)} %grad_ref.1, f32[8,1024]{1,0:T(8,128)} %stack.49.par_ref.refs_14_), custom_call_target="tpu_custom_call" | custom-call | flops 20 | bytes 8 | tf_op jit(solution)/shard_map/first_norm/pallas_call | solution.py:113
  23.4 1.7 collective-permute-start.3
  25.1 4.5 project.4
  31.5 1.7 collective-permute-start.6
  33.2 4.5 project.5
  37.7 22.6 %attend_forward.2 = (bf16[2048,256]{1,0:T(8,128)(2,1)}, f32[256,2048]{1,0:T(8,128)}, f32[2,8,2048]{2,1,0:T(8,128)}) custom-call(bf16[2048,256]{1,0:T(8,128)(2,1)} %get-tuple-element.98.q_ref, bf16[2048,256]{1,0:T(8,128)(2,1)} %get-tuple-element.99.k_ref, bf16[2048,256]{1,0:T(8,128)(2,1)} %get-tuple-element.100.v_ref), custom_call_target="tpu_custom_call" | custom-call | flops 17179869184000 | bytes 6291456000 | tf_op jit(solution)/shard_map/attend_forward/pallas_call | solution.py:202
  60.3 1.9 slice.96
  62.2 5.1 %collective-permute-done.2.w_ref.refs_10_ = bf16[3,1024,256]{2,1,0:T(8,128)(2,1)} collective-permute-done((bf16[3,1024,256]{2,1,0:T(8,128)(2,1)}, bf16[3,1024,256]{2,1,0:T(8,128)(2,1)}, u32[]{:S(2)}, u32[]{:S(2)}) %collective-permute-start.2) | collective-permute-done | bytes 1572896 | tf_op jit(solution)/shard_map/ppermute | solution.py:676
  67.3 4.5 project.6
  71.8 4.6 project.7
  76.4 23.2 %attend_forward.3 = (bf16[2048,256]{1,0:T(8,128)(2,1)}, f32[256,2048]{1,0:T(8,128)}, f32[2,8,2048]{2,1,0:T(8,128)}) custom-call(bf16[2048,256]{1,0:T(8,128)(2,1)} %get-tuple-element.109.q_ref, bf16[2048,256]{1,0:T(8,128)(2,1)} %get-tuple-element.110.k_ref, bf16[2048,256]{1,0:T(8,128)(2,1)} %get-tuple-element.111.v_ref), custom_call_target="tpu_custom_call" | custom-call | flops 17179869184000 | bytes 6291456000 | tf_op jit(solution)/shard_map/attend_forward/pallas_call | solution.py:202
  102.6 2.4 all-gather.2.cloned.1.call-done.up_ref.dn_ref
  105.9 7.4 %output_own.1 = (f32[1024,1024]{1,0:T(8,128)}, bf16[1024,1024]{1,0:T(8,128)(2,1)}) custom-call(bf16[1024,1024]{1,0:T(8,128)(2,1)} %refs_12_.1, f32[8,1024]{1,0:T(8,128)} %stack.49.par_ref.refs_14_, bf16[2048,256]{1,0:T(8,128)(2,1)} %get-tuple-element.101.refs_0_.a_ref, bf16[2048,256]{1,0:T(8,128)(2,1)} %get-tuple-element.112.refs_1_.b_ref, ...), custom_call_target="tpu_custom_call" | custom-call | flops 2147 | bytes 10 | tf_op jit(solution)/shard_map/output_own/pallas_call | solution.py:335
  114.6 3.2 collective-permute-done.9.nt_ref
  117.8 35.1 %feed_forward.2 = (f32[2048,1024]{1,0:T(8,128)}, f32[2048,1024]{1,0:T(8,128)}, bf16[1024,1024]{1,0:T(8,128)(2,1)}, bf16[1024,1024]{1,0:T(8,128)(2,1)}, f32[8,1024]{1,0:T(8,128)}) custom-call(f32[2]{0:T(128)} %pad_maximum_fusion.4.scal_ref, bf16[1024,1024]{1,0:T(8,128)(2,1)} %get-tuple-element.117.no_ref, bf16[1024,1024]{1,0:T(8,128)(2,1)} %collective-permute-done.9.nt_ref, ...), custom_call_target="tpu_custom_call" | custom-call | flops 25769 | bytes 37 | tf_op jit(solution)/shard_map/feed_forward/pallas_call | solution.py:430
  154.5 37.6 %feed_forward.3 = (f32[1024,1024]{1,0:T(8,128)}, f32[1024,1024]{1,0:T(8,128)}, bf16[1024,1024]{1,0:T(8,128)(2,1)}, bf16[1024,1024]{1,0:T(8,128)(2,1)}, bf16[1024...) custom-call(f32[2]{0:T(128)} %pad_maximum_fusion.4.scal_ref, ...), custom_call_target="tpu_custom_call" | custom-call | flops 25769803776000 | bytes 37748736000 | tf_op jit(solution)/shard_map/feed_forward/pallas_call | solution.py:430
  192.9 8.1 %collective-permute-done.12 = bf16[1024,1024]{1,0:T(8,128)(2,1)} collective-permute-done((bf16[1024,1024]{1,0:T(8,128)(2,1)}, bf16[1024,1024]{1,0:T(8,128)(2,1)}, u32[]{:S(2)}, u32[]{:S(2)}) %collective-permute-start.12) | collective-permute-done | bytes 2097184 | tf_op jit(solution)/shard_map/ppermute | solution.py:676
  203.8 9.4 %second_back.1 = (f32[1024,1024]{1,0:T(8,128)}, bf16[1024,1024]{1,0:T(8,128)(2,1)}, f32[8,1024]{1,0:T(8,128)}) custom-call(f32[2]{0:T(128)} %pad_maximum_fusion.4.scal_ref, f32[1024,1024]{1,0:T(8,128)} %get-tuple-element.116.mid_ref, f32[1024,1024]{1,0:T(8,128)} %get-tuple-element.123.go_ref, bf16[1024,1024]{1,0:T(8,128)(2,1)} %copy-done.5, ...), custom_call_target="tpu_custom_call" | custom-call | flops 31 | bytes 18 | tf_op jit(solution)/shard_map/second_back/pallas_call | solution.py:467
  213.2 6.9 %output_back.2 = (bf16[1024,256]{1,0:T(8,128)(2,1)}, bf16[1024,256]{1,0:T(8,128)(2,1)}, f32[256,1024]{1,0:T(8,128)}, f32[256,1024]{1,0:T(8,128)}) custom-call(f32[2]{0:T(128)} %pad_maximum_fusion.4.scal_ref, bf16[1024,1024]{1,0:T(8,128)(2,1)} %get-tuple-element.127.low_ref, bf16[2048,256]{1,0:T(8,128)(2,1)} %get-tuple-element.101.refs_0_.a_ref, ...), custom_call_target="tpu_custom_call" | custom-call | flops 2147483648000 | bytes 4194304000 | tf_op jit(solution)/shard_map/output_back/pallas_call | solution.py:511
  220.2 7.3 %output_back.3 = (bf16[1024,256]{1,0:T(8,128)(2,1)}, bf16[1024,256]{1,0:T(8,128)(2,1)}, bf16[256,1024]{1,0:T(8,128)(2,1)}, bf16[256,1024]{1,0:T(8,128)(2,1)}) custom-call(f32[2]{0:T(128)} %pad_maximum_fusion.4.scal_ref, bf16[1024,1024]{1,0:T(8,128)(2,1)} %collective-permute-done.13.low_ref, bf16[2048,256]{1,0:T(8,128)(2,1)} %get-tuple-element.101.refs_0_.a_ref, ...), custom_call_target="tpu_custom_call" | custom-call | flops 2147 | bytes 4 | tf_op jit(solution)/shard_map/output_back/pallas_call | solution.py:511
  227.5 24.2 %attend_backward.3 = (bf16[2048,128]{1,0:T(8,128)(2,1)}, bf16[2048,128]{1,0:T(8,128)(2,1)}, bf16[2048,128]{1,0:T(8,128)(2,1)}, f32[8,128]{1,0:T(8,128)}) custom-call(bf16[2048,256]{1,0:T(8,128)(2,1)} %get-tuple-element.109.q_ref, bf16[2048,256]{1,0:T(8,128)(2,1)} %get-tuple-element.110.k_ref, bf16[2048,256]{1,0:T(8,128)(2,1)} %get-tuple-element.111.v_ref, ...), custom_call_target="tpu_custom_call" | custom-call | flops 21474836480000 | bytes 5242880000 | tf_op jit(solution)/shard_map/attend_backward/pallas_call | solution.py:295
  251.7 4.0 add_convert_fusion
  255.8 4.0 add_convert_fusion.1
  259.7 24.4 %attend_backward.4 = (bf16[2048,128]{1,0:T(8,128)(2,1)}, bf16[2048,128]{1,0:T(8,128)(2,1)}, bf16[2048,128]{1,0:T(8,128)(2,1)}, f32[8,128]{1,0:T(8,128)}) custom-call(bf16[2048,256]{1,0:T(8,128)(2,1)} %get-tuple-element.109.q_ref, bf16[2048,256]{1,0:T(8,128)(2,1)} %get-tuple-element.110.k_ref, bf16[2048,256]{1,0:T(8,128)(2,1)} %get-tuple-element.111.v_ref, ...), custom_call_target="tpu_custom_call" | custom-call | flops 21474836480000 | bytes 5242880000 | tf_op jit(solution)/shard_map/attend_backward/pallas_call | solution.py:295
  284.7 8.2 %input_term.2 = bf16[3072,256]{1,0:T(8,128)(2,1)} custom-call(f32[2]{0:T(128)} %pad_maximum_fusion.4.scal_ref, bf16[1024,1024]{1,0:T(8,128)(2,1)} %get-tuple-element.105.x_ref.no_ref, bf16[1024,1024]{1,0:T(8,128)(2,1)} %collective-permute-done.x_ref.nt_ref, bf16[2048,128]{1,0:T(8,128)(2,1)} %get-tuple-element.134.refs_0_.refs_3_, ...), custom_call_target="tpu_custom_call" | custom-call | flops 3221 | bytes 10 | tf_op jit(solution)/shard_map/input_term/pallas_call | solution.py:548
  294.4 45.0 %attend_backward.5 = (bf16[2048,256]{1,0:T(8,128)(2,1)}, bf16[2048,256]{1,0:T(8,128)(2,1)}, bf16[2048,256]{1,0:T(8,128)(2,1)}, f32[8,256]{1,0:T(8,128)}) custom-call(bf16[2048,256]{1,0:T(8,128)(2,1)} %get-tuple-element.98.q_ref, bf16[2048,256]{1,0:T(8,128)(2,1)} %get-tuple-element.99.k_ref, bf16[2048,256]{1,0:T(8,128)(2,1)} %get-tuple-element.100.v_ref, ...), custom_call_target="tpu_custom_call" | custom-call | flops 42949672960000 | bytes 10485760000 | tf_op jit(solution)/shard_map/attend_backward/pallas_call | solution.py:295
  339.5 8.5 %input_term.3 = bf16[3072,256]{1,0:T(8,128)(2,1)} custom-call(f32[2]{0:T(128)} %pad_maximum_fusion.4.scal_ref, bf16[1024,1024]{1,0:T(8,128)(2,1)} %get-tuple-element.105.x_ref.no_ref, bf16[1024,1024]{1,0:T(8,128)(2,1)} %collective-permute-done.x_ref.nt_ref, bf16[2048,256]{1,0:T(8,128)(2,1)} %get-tuple-element.153.refs_0_, ...), custom_call_target="tpu_custom_call" | custom-call | flops 3221 | bytes 10 | tf_op jit(solution)/shard_map/input_term/pallas_call | solution.py:548
  348.0 7.7 %first_other.1 = bf16[1024,1024]{1,0:T(8,128)(2,1)} custom-call(bf16[2048,256]{1,0:T(8,128)(2,1)} %get-tuple-element.153.refs_0_, bf16[2048,256]{1,0:T(8,128)(2,1)} %get-tuple-element.154.refs_1_, bf16[2048,256]{1,0:T(8,128)(2,1)} %get-tuple-element.155.refs_2_, bf16[2048,128]{1,0:T(8,128)(2,1)} %get-tuple-element.134.refs_0_.refs_3_, ...), custom_call_target="tpu_custom_call" | custom-call | flops 3221 | bytes 8 | tf_op jit(solution)/shard_map/first_other/pallas_call | solution.py:593
  361.1 11.2 %first_own.1 = (bf16[1024,1024]{1,0:T(8,128)(2,1)}, f32[8,1024]{1,0:T(8,128)}) custom-call(f32[2]{0:T(128)} %pad_maximum_fusion.4.scal_ref, bf16[2048,256]{1,0:T(8,128)(2,1)} %get-tuple-element.153.refs_0_, bf16[2048,256]{1,0:T(8,128)(2,1)} %get-tuple-element.154.refs_1_, bf16[2048,256]{1,0:T(8,128)(2,1)} %get-tuple-element.155.refs_2_, ...), custom_call_target="tpu_custom_call" | custom-call | flops 3221 | bytes 16 | tf_op jit(solution)/shard_map/first_own/pallas_call | solution.py:631
  373.2 6.7 %multiply_convert_fusion = bf16[1024,1024]{1,0:T(8,128)(2,1)} fusion(bf16[1024,1024]{1,0:T(8,128)(2,1)} %collective-permute-done.14, f32[1024,1024]{1,0:T(8,128)} %get-tuple-element.116.mid_ref, f32[1024,1024]{1,0:T(8,128)} %get-tuple-element.121, f32[1024]{0:T(1024)S(1)} %copy-done.14, f32[]{:T(128)} %convert_element_type.109), kind=kLoop, calls=%fused_computation.4 | loop fusion | flops 6291456 | bytes 12587012 | tf_op jit(solution)/shard_map/convert_element_type | solution.py:779
  379.8 6.3 %collective-permute-done.30 = bf16[1024,256]{1,0:T(8,128)(2,1)S(1)} collective-permute-done((bf16[1024,256]{1,0:T(8,128)(2,1)S(1)}, bf16[1024,256]{1,0:T(8,128)(2,1)S(1)}, u32[]{:S(2)}, u32[]{:S(2)}) %collective-permute-start.30) | collective-permute-done | bytes 524320 | tf_op jit(solution)/shard_map/ppermute | solution.py:682
  386.4 3.7 collective-permute-done.20
  390.4 3.8 collective-permute-done.21
  394.2 2.2 collective-permute-start.31
  396.5 3.5 collective-permute-done.22
  400.0 2.2 collective-permute-start.25
  402.2 20.7 %collective-permute-done.23 = f32[8,1024]{1,0:T(8,128)S(1)} collective-permute-done((f32[8,1024]{1,0:T(8,128)S(1)}, f32[8,1024]{1,0:T(8,128)S(1)}, u32[]{:S(2)}, u32[]{:S(2)}) %collective-permute-start.23) | collective-permute-done | bytes 32800 | tf_op jit(solution)/shard_map/ppermute | solution.py:682
  426.2 4.7 collective-permute-done.32
  431.9 7.6 %collective-permute-done.26 = bf16[256,256]{1,0:T(8,128)(2,1)S(1)} collective-permute-done((bf16[256,256]{1,0:T(8,128)(2,1)S(1)}, bf16[256,256]{1,0:T(8,128)(2,1)S(1)}, u32[]{:S(2)}, u32[]{:S(2)}) %collective-permute-start.26) | collective-permute-done | bytes 131104 | tf_op jit(solution)/shard_map/ppermute | solution.py:682
  439.7 3.0 collective-permute-start.34
  442.7 3.9 collective-permute-done.27
  446.7 4.2 convert_multiply_fusion
  453.1 4.3 collective-permute-done.28
  457.5 1.8 collective-permute-start.29
  459.4 2.6 convert_multiply_fusion.1
  463.9 7.4 %collective-permute-done.29 = bf16[1024,256]{1,0:T(8,128)(2,1)S(1)} collective-permute-done((bf16[1024,256]{1,0:T(8,128)(2,1)S(1)}, bf16[1024,256]{1,0:T(8,128)(2,1)S(1)}, u32[]{:S(2)}, u32[]{:S(2)}) %collective-permute-start.29) | collective-permute-done | bytes 524320 | tf_op jit(solution)/shard_map/ppermute | solution.py:682
  471.6 1.9 convert_multiply_fusion.2
  (171 shorter events, 36.0 us)
Async XLA Ops:
  7.3 97.8 %all-gather.2.cloned.1.call-start = ((), (), s32[]{:S(2)}) async-start(), calls=%async_computation | async-start | bytes 4718592 | tf_op jit(solution)/shard_map/all_gather | solution.py:692
  8.4 14.9 %collective-permute-start.1 = (bf16[1,2,128,1024]{3,2,1,0:T(8,128)(2,1)S(1)}, bf16[1,2,128,1024]{3,2,1,0:T(8,128)(2,1)S(1)}, u32[]{:S(2)}, u32[]{:S(2)}) collective-permute-start(bf16[1,2,128,1024]{3,2,1,0:T(8,128)(2,1)S(1)} %maximum_bitcast_fusion), channel_id=1, source_target_pairs={{0,2},{1,3},{2,0},{3,1},{4,6},{5,7},{6,4},{7,5},{8,10},{9,11},{10,... | collective-permute-start | bytes 1572872 | tf_op jit(solution)/shard_map/ppermute | solution.py:676
  20.8 12.4 %collective-permute-start = (bf16[1024,1024]{1,0:T(8,128)(2,1)}, bf16[1024,1024]{1,0:T(8,128)(2,1)}, u32[]{:S(2)}, u32[]{:S(2)}) collective-permute-start(bf16[1024,1024]{1,0:T(8,128)(2,1)} %get-tuple-element.105.x_ref.no_ref), channel_id=1, source_target_pairs={{0,1},{1,0},{2,3},{3,2},{4,5},{5,4},{6,7},{7,6},{8,9},{9,8},{10,11... | collective-permute-start | bytes 6291464 | tf_op jit(solution)/shard_map/ppermute | solution.py:673
  20.8 84.2 %collective-permute-start.7 = (bf16[256,1024]{1,0:T(8,128)(2,1)}, bf16[256,1024]{1,0:T(8,128)(2,1)}, u32[]{:S(2)}, u32[]{:S(2)}) collective-permute-start(bf16[256,1024]{1,0:T(8,128)(2,1)} %wa_ref.3), channel_id=1, source_target_pairs={{0,1},{1,0},{2,3},{3,2},{4,5},{5,4},{6,7},{7,6},{8,9},{9,8},{10,11... | collective-permute-start | bytes 1572872 | tf_op jit(solution)/shard_map/ppermute | solution.py:673
  23.4 6.8 %collective-permute-start.3 = (f32[12,128]{1,0:T(8,128)}, f32[12,128]{1,0:T(8,128)}, u32[]{:S(2)}, u32[]{:S(2)}) collective-permute-start(f32[12,128]{1,0:T(8,128)} %maximum_bitcast_fusion.1), channel_id=1, source_target_pairs={{0,2},{1,3},{2,0},{3,1},{4,6},{5,7},{6,4},{7,5},{8,10},{9,11},{10,... | collective-permute-start | bytes 18440 | tf_op jit(solution)/shard_map/ppermute | solution.py:676
  29.6 37.6 %collective-permute-start.2 = (bf16[3,1024,256]{2,1,0:T(8,128)(2,1)}, bf16[3,1024,256]{2,1,0:T(8,128)(2,1)}, u32[]{:S(2)}, u32[]{:S(2)}) collective-permute-start(bf16[3,1024,256]{2,1,0:T(8,128)(2,1)} %refs_9_.3), channel_id=1, source_target_pairs={{0,2},{1,3},{2,0},{3,1},{4,6},{5,7},{6,4},{7,5},{8,10},{9,11},{10,... | collective-permute-start | bytes 4718600 | tf_op jit(solution)/shard_map/ppermute | solution.py:676
  29.9 416.7 %all-reduce.5.cloned.1.call-start = ((), (), s32[]{:S(2)}) async-start(), calls=%async_computation.1 | async-start | bytes 8388608 | tf_op jit(solution)/shard_map/psum | solution.py:762
  31.5 69.3 %collective-permute-start.6 = (bf16[256,1024]{1,0:T(8,128)(2,1)}, bf16[256,1024]{1,0:T(8,128)(2,1)}, u32[]{:S(2)}, u32[]{:S(2)}) collective-permute-start(bf16[256,1024]{1,0:T(8,128)(2,1)} %wa_ref.3), channel_id=1, source_target_pairs={{0,2},{1,3},{2,0},{3,1},{4,6},{5,7},{6,4},{7,5},{8,10},{9,11},{10,... | collective-permute-start | bytes 1572872 | tf_op jit(solution)/shard_map/ppermute | solution.py:676
  62.2 9.6 %collective-permute-start.4 = (bf16[1024,256]{1,0:T(8,128)(2,1)}, bf16[1024,256]{1,0:T(8,128)(2,1)}, u32[]{:S(2)}, u32[]{:S(2)}) collective-permute-start(bf16[1024,256]{1,0:T(8,128)(2,1)} %slice.96), channel_id=1, source_target_pairs={{0,1},{1,0},{2,3},{3,2},{4,5},{5,4},{6,7},{7,6},{8,9},{9,8},{10,11... | collective-permute-start | bytes 1572872 | tf_op jit(solution)/shard_map/ppermute | solution.py:673
  76.4 24.8 %copy-start = (bf16[1024,1024]{1,0:T(8,128)(2,1)S(1)}, bf16[1024,1024]{1,0:T(8,128)(2,1)}, u32[]{:S(2)}) copy-start(bf16[1024,1024]{1,0:T(8,128)(2,1)} %get-tuple-element.118.co_ref.cot_ref) | copy-start | bytes 6291460
  100.7 2.0 collective-permute-start.5
  100.7 4.3 collective-permute-start.8
  101.2 13.4 %collective-permute-start.10 = (bf16[1024,1024]{1,0:T(8,128)(2,1)S(1)}, bf16[1024,1024]{1,0:T(8,128)(2,1)}, u32[]{:S(2)}, u32[]{:S(2)}) collective-permute-start(bf16[1024,1024]{1,0:T(8,128)(2,1)S(1)} %copy-done), channel_id=1, source_target_pairs={{0,1},{1,0},{2,3},{3,2},{4,5},{5,4},{6,7},{7,6},{8,9},{9,8},{10,11... | collective-permute-start | bytes 6291464 | tf_op jit(solution)/shard_map/ppermute | solution.py:673
  113.3 4.5 collective-permute-start.9
  152.9 48.0 %collective-permute-start.12 = (bf16[1024,1024]{1,0:T(8,128)(2,1)}, bf16[1024,1024]{1,0:T(8,128)(2,1)}, u32[]{:S(2)}, u32[]{:S(2)}) collective-permute-start(bf16[1024,1024]{1,0:T(8,128)(2,1)} %get-tuple-element.125), channel_id=1, source_target_pairs={{0,2},{1,3},{2,0},{3,1},{4,6},{5,7},{6,4},{7,5},{8,10},{9,11},{10,... | collective-permute-start | bytes 6291464 | tf_op jit(solution)/shard_map/ppermute | solution.py:676
  192.1 10.4 %collective-permute-start.11 = (bf16[1024,1024]{1,0:T(8,128)(2,1)}, bf16[1024,1024]{1,0:T(8,128)(2,1)S(1)}, u32[]{:S(2)}, u32[]{:S(2)}) collective-permute-start(bf16[1024,1024]{1,0:T(8,128)(2,1)} %get-tuple-element.124), channel_id=1, source_target_pairs={{0,1},{1,0},{2,3},{3,2},{4,5},{5,4},{6,7},{7,6},{8,9},{9,8},{10,11... | collective-permute-start | bytes 6291464 | tf_op jit(solution)/shard_map/ppermute | solution.py:673
  201.0 50.8 %collective-permute-start.15 = (bf16[1024,1024]{1,0:T(8,128)(2,1)}, bf16[1024,1024]{1,0:T(8,128)(2,1)}, u32[]{:S(2)}, u32[]{:S(2)}) collective-permute-start(bf16[1024,1024]{1,0:T(8,128)(2,1)} %get-tuple-element.141), channel_id=1, source_target_pairs={{0,2},{1,3},{2,0},{3,1},{4,6},{5,7},{6,4},{7,5},{8,10},{9,11},{10,... | collective-permute-start | bytes 6291464 | tf_op jit(solution)/shard_map/ppermute | solution.py:676
  213.1 7.0 %collective-permute-start.13 = (bf16[1024,1024]{1,0:T(8,128)(2,1)}, bf16[1024,1024]{1,0:T(8,128)(2,1)}, u32[]{:S(2)}, u32[]{:S(2)}) collective-permute-start(bf16[1024,1024]{1,0:T(8,128)(2,1)} %get-tuple-element.127.low_ref), channel_id=1, source_target_pairs={{0,1},{1,0},{2,3},{3,2},{4,5},{5,4},{6,7},{7,6},{8,9},{9,8},{10,11... | collective-permute-start | bytes 6291464 | tf_op jit(solution)/shard_map/ppermute | solution.py:673
  227.5 24.3 %copy-start.4 = (bf16[1024,1024]{1,0:T(8,128)(2,1)S(1)}, bf16[1024,1024]{1,0:T(8,128)(2,1)}, u32[]{:S(2)}) copy-start(bf16[1024,1024]{1,0:T(8,128)(2,1)} %get-tuple-element.139) | copy-start | bytes 6291460
  284.1 55.4 %collective-permute-start.17 = (bf16[256,1024]{1,0:T(8,128)(2,1)}, bf16[256,1024]{1,0:T(8,128)(2,1)}, u32[]{:S(2)}, u32[]{:S(2)}) collective-permute-start(bf16[256,1024]{1,0:T(8,128)(2,1)} %get-tuple-element.157), channel_id=1, source_target_pairs={{0,2},{1,3},{2,0},{3,1},{4,6},{5,7},{6,4},{7,5},{8,10},{9,11},{10,... | collective-permute-start | bytes 1572872 | tf_op jit(solution)/shard_map/ppermute | solution.py:676
  292.9 46.6 %collective-permute-start.16 = (bf16[3072,256]{1,0:T(8,128)(2,1)}, bf16[3072,256]{1,0:T(8,128)(2,1)}, u32[]{:S(2)}, u32[]{:S(2)}) collective-permute-start(bf16[3072,256]{1,0:T(8,128)(2,1)} %input_term.2), channel_id=1, source_target_pairs={{0,2},{1,3},{2,0},{3,1},{4,6},{5,7},{6,4},{7,5},{8,10},{9,11},{10,... | collective-permute-start | bytes 4718600 | tf_op jit(solution)/shard_map/ppermute | solution.py:676
  294.4 78.7 %collective-permute-start.14 = (bf16[1024,1024]{1,0:T(8,128)(2,1)}, bf16[1024,1024]{1,0:T(8,128)(2,1)}, u32[]{:S(2)}, u32[]{:S(2)}) collective-permute-start(bf16[1024,1024]{1,0:T(8,128)(2,1)} %get-tuple-element.135), channel_id=1, source_target_pairs={{0,1},{1,0},{2,3},{3,2},{4,5},{5,4},{6,7},{7,6},{8,9},{9,8},{10,11... | collective-permute-start | bytes 6291464 | tf_op jit(solution)/shard_map/ppermute | solution.py:673
  294.4 45.0 %copy-start.23 = (f32[8,128]{1,0:T(8,128)S(1)}, f32[8,128]{1,0:T(8,128)}, u32[]{:S(2)}) copy-start(f32[8,128]{1,0:T(8,128)} %get-tuple-element.167) | copy-start | bytes 12292
  294.4 45.0 %copy-start.24 = (f32[8,128]{1,0:T(8,128)S(1)}, f32[8,128]{1,0:T(8,128)}, u32[]{:S(2)}) copy-start(f32[8,128]{1,0:T(8,128)} %get-tuple-element.168) | copy-start | bytes 12292
  348.0 9.2 %copy-start.15 = (f32[1024]{0:T(1024)S(1)}, f32[1024]{0:T(1024)}, u32[]{:S(2)}) copy-start(f32[1024]{0:T(1024)} %pad.29.clone) | copy-start | bytes 12292
  348.0 9.2 %copy-start.8 = (bf16[256,1024]{1,0:T(8,128)(2,1)S(1)}, bf16[256,1024]{1,0:T(8,128)(2,1)}, u32[]{:S(2)}) copy-start(bf16[256,1024]{1,0:T(8,128)(2,1)} %get-tuple-element.170) | copy-start | bytes 1572868
  355.7 5.3 %collective-permute-start.18 = (bf16[1024,1024]{1,0:T(8,128)(2,1)}, bf16[1024,1024]{1,0:T(8,128)(2,1)}, u32[]{:S(2)}, u32[]{:S(2)}) collective-permute-start(bf16[1024,1024]{1,0:T(8,128)(2,1)} %first_other.1), channel_id=1, source_target_pairs={{0,1},{1,0},{2,3},{3,2},{4,5},{5,4},{6,7},{7,6},{8,9},{9,8},{10,11... | collective-permute-start | bytes 6291464 | tf_op jit(solution)/shard_map/ppermute | solution.py:673
  358.8 27.4 %collective-permute-start.30 = (bf16[1024,256]{1,0:T(8,128)(2,1)S(1)}, bf16[1024,256]{1,0:T(8,128)(2,1)S(1)}, u32[]{:S(2)}, u32[]{:S(2)}) collective-permute-start(bf16[1024,256]{1,0:T(8,128)(2,1)S(1)} %constant_dynamic-slice_fusion.2), channel_id=1, source_target_pairs={{0,8},{4,12},{8,0},{12,4},{16,24},{20,28},{24,16},{28,20},{1,9},{5... | collective-permute-start | bytes 1572872 | tf_op jit(solution)/shard_map/ppermute | solution.py:682
  360.4 11.9 %copy-start.10 = (f32[8,1024]{1,0:T(8,128)S(1)}, f32[8,1024]{1,0:T(8,128)}, u32[]{:S(2)}) copy-start(f32[8,1024]{1,0:T(8,128)} %get-tuple-element.163) | copy-start | bytes 98308
  360.4 12.7 %copy-start.14 = (f32[1024]{0:T(1024)S(1)}, f32[1024]{0:T(1024)}, u32[]{:S(2)}) copy-start(f32[1024]{0:T(1024)} %param.33) | copy-start | bytes 12292
  360.4 26.0 %collective-permute-start.24 = (bf16[1024,256]{1,0:T(8,128)(2,1)}, bf16[1024,256]{1,0:T(8,128)(2,1)S(1)}, u32[]{:S(2)}, u32[]{:S(2)}) collective-permute-start(bf16[1024,256]{1,0:T(8,128)(2,1)} %constant_dynamic-slice_fusion.5), channel_id=1, source_target_pairs={{0,4},{4,0},{8,12},{12,8},{16,20},{20,16},{24,28},{28,24},{1,5},{5... | collective-permute-start | bytes 1572872 | tf_op jit(solution)/shard_map/ppermute | solution.py:682
  373.1 13.1 %copy-start.12 = (f32[8,1024]{1,0:T(8,128)S(1)}, f32[8,1024]{1,0:T(8,128)}, u32[]{:S(2)}) copy-start(f32[8,1024]{1,0:T(8,128)} %get-tuple-element.166) | copy-start | bytes 98308
  373.1 17.1 %copy-start.11 = (f32[8,1024]{1,0:T(8,128)S(1)}, f32[8,1024]{1,0:T(8,128)}, u32[]{:S(2)}) copy-start(f32[8,1024]{1,0:T(8,128)} %get-tuple-element.164) | copy-start | bytes 98308
  373.1 13.1 %collective-permute-start.19 = (f32[8,1024]{1,0:T(8,128)S(1)}, f32[8,1024]{1,0:T(8,128)S(1)}, u32[]{:S(2)}, u32[]{:S(2)}) collective-permute-start(f32[8,1024]{1,0:T(8,128)S(1)} %add.155), channel_id=1, source_target_pairs={{0,1},{1,0},{2,3},{3,2},{4,5},{5,4},{6,7},{7,6},{8,9},{9,8},{10,11... | collective-permute-start | bytes 98312 | tf_op jit(solution)/shard_map/ppermute | solution.py:673
  386.2 4.0 collective-permute-start.20
  390.2 4.0 collective-permute-start.21
  394.2 5.8 %collective-permute-start.22 = (f32[8,1024]{1,0:T(8,128)S(1)}, f32[8,1024]{1,0:T(8,128)S(1)}, u32[]{:S(2)}, u32[]{:S(2)}) collective-permute-start(f32[8,1024]{1,0:T(8,128)S(1)} %add.162), channel_id=1, source_target_pairs={{0,8},{4,12},{8,0},{12,4},{16,24},{20,28},{24,16},{28,20},{1,9},{5... | collective-permute-start | bytes 98312 | tf_op jit(solution)/shard_map/ppermute | solution.py:682
  394.2 31.2 %collective-permute-start.31 = (bf16[512,256]{1,0:T(8,128)(2,1)S(1)}, bf16[512,256]{1,0:T(8,128)(2,1)S(1)}, u32[]{:S(2)}, u32[]{:S(2)}) collective-permute-start(bf16[512,256]{1,0:T(8,128)(2,1)S(1)} %constant_dynamic-slice_fusion.1), channel_id=1, source_target_pairs={{0,16},{4,20},{8,24},{12,28},{16,0},{20,4},{24,8},{28,12},{1,17},{... | collective-permute-start | bytes 786440 | tf_op jit(solution)/shard_map/ppermute | solution.py:682
  400.0 22.9 %collective-permute-start.23 = (f32[8,1024]{1,0:T(8,128)S(1)}, f32[8,1024]{1,0:T(8,128)S(1)}, u32[]{:S(2)}, u32[]{:S(2)}) collective-permute-start(f32[8,1024]{1,0:T(8,128)S(1)} %add.163), channel_id=1, source_target_pairs={{0,16},{4,20},{8,24},{12,28},{16,0},{20,4},{24,8},{28,12},{1,17},{... | collective-permute-start | bytes 98312 | tf_op jit(solution)/shard_map/ppermute | solution.py:682
  400.0 25.9 %collective-permute-start.25 = (bf16[512,256]{1,0:T(8,128)(2,1)S(1)}, bf16[512,256]{1,0:T(8,128)(2,1)S(1)}, u32[]{:S(2)}, u32[]{:S(2)}) collective-permute-start(bf16[512,256]{1,0:T(8,128)(2,1)S(1)} %constant_dynamic-slice_fusion.4), channel_id=1, source_target_pairs={{0,8},{4,12},{8,0},{12,4},{16,24},{20,28},{24,16},{28,20},{1,9},{5... | collective-permute-start | bytes 786440 | tf_op jit(solution)/shard_map/ppermute | solution.py:682
  425.5 5.4 %collective-permute-start.32 = (bf16[256,256]{1,0:T(8,128)(2,1)S(1)}, bf16[256,256]{1,0:T(8,128)(2,1)S(1)}, u32[]{:S(2)}, u32[]{:S(2)}) collective-permute-start(bf16[256,256]{1,0:T(8,128)(2,1)S(1)} %constant_dynamic-slice_fusion), channel_id=1, source_target_pairs={{0,4},{4,0},{8,12},{12,8},{16,20},{20,16},{24,28},{28,24},{1,5},{5... | collective-permute-start | bytes 393224 | tf_op jit(solution)/shard_map/ppermute | solution.py:682
  426.0 13.5 %collective-permute-start.26 = (bf16[256,256]{1,0:T(8,128)(2,1)S(1)}, bf16[256,256]{1,0:T(8,128)(2,1)S(1)}, u32[]{:S(2)}, u32[]{:S(2)}) collective-permute-start(bf16[256,256]{1,0:T(8,128)(2,1)S(1)} %constant_dynamic-slice_fusion.3), channel_id=1, source_target_pairs={{0,16},{4,20},{8,24},{12,28},{16,0},{20,4},{24,8},{28,12},{1,17},{... | collective-permute-start | bytes 393224 | tf_op jit(solution)/shard_map/ppermute | solution.py:682
  430.9 8.7 %collective-permute-start.33 = (bf16[256,256]{1,0:T(8,128)(2,1)S(1)}, bf16[256,256]{1,0:T(8,128)(2,1)S(1)}, u32[]{:S(2)}, u32[]{:S(2)}) collective-permute-start(bf16[256,256]{1,0:T(8,128)(2,1)S(1)} %add_convert_fusion.7), channel_id=1, source_target_pairs={{0,4},{4,0},{8,12},{12,8},{16,20},{20,16},{24,28},{28,24},{1,5},{5... | collective-permute-start | bytes 393224 | tf_op jit(solution)/shard_map/ppermute | solution.py:682
  439.5 7.0 %collective-permute-start.27 = (bf16[256,256]{1,0:T(8,128)(2,1)S(1)}, bf16[256,256]{1,0:T(8,128)(2,1)S(1)}, u32[]{:S(2)}, u32[]{:S(2)}) collective-permute-start(bf16[256,256]{1,0:T(8,128)(2,1)S(1)} %add_convert_fusion.8), channel_id=1, source_target_pairs={{0,16},{4,20},{8,24},{12,28},{16,0},{20,4},{24,8},{28,12},{1,17},{... | collective-permute-start | bytes 393224 | tf_op jit(solution)/shard_map/ppermute | solution.py:682
  439.7 12.3 %collective-permute-start.34 = (bf16[512,256]{1,0:T(8,128)(2,1)S(1)}, bf16[512,256]{1,0:T(8,128)(2,1)S(1)}, u32[]{:S(2)}, u32[]{:S(2)}) collective-permute-start(bf16[512,256]{1,0:T(8,128)(2,1)S(1)} %pad_maximum_fusion.3), channel_id=1, source_target_pairs={{0,16},{4,20},{8,24},{12,28},{16,0},{20,4},{24,8},{28,12},{1,17},{... | collective-permute-start | bytes 786440 | tf_op jit(solution)/shard_map/ppermute | solution.py:682
  446.6 10.8 %collective-permute-start.28 = (bf16[512,256]{1,0:T(8,128)(2,1)S(1)}, bf16[512,256]{1,0:T(8,128)(2,1)S(1)}, u32[]{:S(2)}, u32[]{:S(2)}) collective-permute-start(bf16[512,256]{1,0:T(8,128)(2,1)S(1)} %pad_maximum_fusion.2), channel_id=1, source_target_pairs={{0,8},{4,12},{8,0},{12,4},{16,24},{20,28},{24,16},{28,20},{1,9},{5... | collective-permute-start | bytes 786440 | tf_op jit(solution)/shard_map/ppermute | solution.py:682
  452.1 11.5 %collective-permute-start.35 = (bf16[1024,256]{1,0:T(8,128)(2,1)S(1)}, bf16[1024,256]{1,0:T(8,128)(2,1)S(1)}, u32[]{:S(2)}, u32[]{:S(2)}) collective-permute-start(bf16[1024,256]{1,0:T(8,128)(2,1)S(1)} %pad_maximum_fusion.1), channel_id=1, source_target_pairs={{0,8},{4,12},{8,0},{12,4},{16,24},{20,28},{24,16},{28,20},{1,9},{5... | collective-permute-start | bytes 1572872 | tf_op jit(solution)/shard_map/ppermute | solution.py:682
  457.5 13.8 %collective-permute-start.29 = (bf16[1024,256]{1,0:T(8,128)(2,1)S(1)}, bf16[1024,256]{1,0:T(8,128)(2,1)S(1)}, u32[]{:S(2)}, u32[]{:S(2)}) collective-permute-start(bf16[1024,256]{1,0:T(8,128)(2,1)S(1)} %pad_maximum_fusion), channel_id=1, source_target_pairs={{0,4},{4,0},{8,12},{12,8},{16,20},{20,16},{24,28},{28,24},{1,5},{5... | collective-permute-start | bytes 1572872 | tf_op jit(solution)/shard_map/ppermute | solution.py:682
  (16 other events, 85.2 us)
Sparse Core Ops, SparseCore 0:
  30.1 74.8 all-gather.1
  259.9 172.6 all-reduce.4
